TPU v7x, 32 devices: a whole 2x2x4 slice. The times are simulated.
32 devices in a mesh: batch: 8 (over y, x, core), frames: 4 (over z).
Axes of the slice: x: 2, y: 2, z: 4, core: 2. Of those that a mesh axis runs over, the one named last changes fastest.
Arguments:
- frames_in: bfloat16 [16, 1280, 1024], P('batch', 'frames'), may hold values from -6 to 6
- positions: int32 [16, 640], P('batch'), may hold values from -1 to 1279, as said below
- mask_vector: bfloat16 [1024], P(('batch', 'frames')), may hold values from -6 to 6
- norm_gains: bfloat16 [5, 1024], P(None, ('batch', 'frames')), may hold values from 0.5 to 1.5
- norm_biases: bfloat16 [5, 1024], P(None, ('batch', 'frames')), may hold values from -1.75 to 1.75
- depth_gain: bfloat16 [2048], P(('batch', 'frames')), may hold values from 0.5 to 1.5
- depth_bias: bfloat16 [2048], P(('batch', 'frames')), may hold values from -1.75 to 1.75
- early_in: bfloat16 [1024, 4096], P(('batch', 'frames')), may hold values from -0.1875 to 0.1875
- early_out: bfloat16 [4096, 1024], P(('batch', 'frames')), may hold values from -0.1875 to 0.1875
- qkv_weight: bfloat16 [1024, 3072], P(('batch', 'frames')), may hold values from -0.1875 to 0.1875
- mixer_out: bfloat16 [1024, 1024], P(('batch', 'frames')), may hold values from -1.5 to 1.5
- pointwise_in: bfloat16 [1024, 4096], P(('batch', 'frames')), may hold values from -0.1875 to 0.1875
- pointwise_out: bfloat16 [2048, 1024], P(('batch', 'frames')), may hold values from -0.1875 to 0.1875
- depth_kernel: bfloat16 [31, 2048], P(None, ('batch', 'frames')), may hold values from -1 to 1
- late_in: bfloat16 [1024, 4096], P(('batch', 'frames')), may hold values from -0.1875 to 0.1875
- late_out: bfloat16 [4096, 1024], P(('batch', 'frames')), may hold values from -0.1875 to 0.1875
- position_bias: bfloat16 [512], P(('batch', 'frames')), may hold values from -6 to 6
- cotangent: bfloat16 [16, 1280, 1024], P('batch', 'frames'), may hold values from -6 to 6
Outputs:
- activations: bfloat16 [16, 1280, 1024], P('batch', 'frames')
- grad_frames: float32 [16, 1280, 1024], P('batch', 'frames')
- grad_mask_vector: float32 [1024], P(('batch', 'frames'))
- grad_norm_gains: float32 [5, 1024], P(None, ('batch', 'frames'))
- grad_norm_biases: float32 [5, 1024], P(None, ('batch', 'frames'))
- grad_depth_gain: float32 [2048], P(('batch', 'frames'))
- grad_depth_bias: float32 [2048], P(('batch', 'frames'))
- grad_early_in: float32 [1024, 4096], P(('batch', 'frames'))
- grad_early_out: float32 [4096, 1024], P(('batch', 'frames'))
- grad_qkv_weight: float32 [1024, 3072], P(('batch', 'frames'))
- grad_mixer_out: float32 [1024, 1024], P(('batch', 'frames'))
- grad_pointwise_in: float32 [1024, 4096], P(('batch', 'frames'))
- grad_pointwise_out: float32 [2048, 1024], P(('batch', 'frames'))
- grad_depth_kernel: float32 [31, 2048], P(None, ('batch', 'frames'))
- grad_late_in: float32 [1024, 4096], P(('batch', 'frames'))
- grad_late_out: float32 [4096, 1024], P(('batch', 'frames'))
- grad_position_bias: float32 [512], P(('batch', 'frames'))
Inputs may be any that keep to these rules, and one draw needn't show every extreme that they name: `positions`: each row lists distinct frame numbers of its utterance, followed by -1 entries in the remaining slots; at least one row has no -1.
All inputs are finite; a program needn't handle non-finite values.
Results may differ from a plain program's by a relative error of at most 0.03.
Values may be sent and summed in bfloat16 or wider, within the bound.
A program may use at most 512 MiB of HBM per device.

v0:
```python
import math

import jax
import jax.numpy as jnp
from jax import lax
from jax.sharding import PartitionSpec as P

D = 1024
H = 16
DH = 64
C = 2048
KERNEL = 31
HALF = 15
NB = 32


EPS = 1e-05
LIMITS = (8, 12, 16, 24, 32, 48, 64, 96)


def padded_2(cells, sides, width):
    for axis, dim in sides:
        count = lax.axis_size(axis)
        ends = count - 1
        head = lax.slice_in_dim(cells, 0, width, axis=dim)
        tail = lax.slice_in_dim(cells, cells.shape[dim] - width, cells.shape[dim], axis=dim)
        cells = jnp.concatenate(
            [
                lax.ppermute(tail, axis, [(i, (i + 1) % count) for i in range(ends)]),
                cells,
                lax.ppermute(head, axis, [((i + 1) % count, i) for i in range(ends)]),
            ],
            axis=dim,
        )
    return cells


def layer_norm(values, norm_gain, norm_shift):
    centred = values - jnp.mean(values, axis=-1, keepdims=True)
    spread = jnp.mean(centred * centred, axis=-1, keepdims=True)
    return centred * lax.rsqrt(spread + EPS) * norm_gain + norm_shift


def bucket_of(relative):
    magnitude = jnp.abs(relative)
    above = jnp.zeros_like(relative)
    for threshold in LIMITS:
        above = above + (magnitude >= threshold).astype(jnp.int32)
    inner_bucket = jnp.where(magnitude < 8, magnitude, 7 + above)
    return inner_bucket + NB // 2 * (relative > 0).astype(jnp.int32)


def product(operand_a, operand_b):
    return jnp.dot(operand_a, operand_b, preferred_element_type=jnp.float32)


def weight_grad(operand_a, operand_b):
    return lax.dot_general(
        operand_a, operand_b, (((0,), (0,)), ((), ())), preferred_element_type=jnp.float32
    )


def back_product(operand_a, operand_b):
    return lax.dot_general(
        operand_a, operand_b, (((1,), (1,)), ((), ())), preferred_element_type=jnp.float32
    )


def gated_unit(paired):
    return paired[:, :C] * jax.nn.sigmoid(paired[:, C:])


def depth_post(depth_values, norm_gain, norm_shift):
    return jax.nn.silu(layer_norm(depth_values, norm_gain, norm_shift))


def norm_back(hidden, norm_gain, norm_shift, upstream):
    normed_unused, pull_back = jax.vjp(layer_norm, hidden, norm_gain, norm_shift)
    return pull_back(upstream)


def shards(
    frames_in,
    positions,
    mask_vector,
    norm_gains,
    norm_biases,
    depth_gain,
    depth_bias,
    early_in,
    early_out,
    qkv_weight,
    mixer_out,
    pointwise_in,
    pointwise_out,
    depth_kernel,
    late_in,
    late_out,
    position_bias,
    cotangent,
):
    groups, local_len, model_width = frames_in.shape
    length = local_len * lax.axis_size("frames")
    first_frame = lax.axis_index("frames") * local_len
    row_count = groups * local_len
    score_scale = 1.0 / math.sqrt(DH)

    def fetch_early():
        return (
            lax.all_gather(early_in, ("batch", "frames"), axis=0, tiled=True),
            lax.all_gather(early_out, ("batch", "frames"), axis=0, tiled=True),
            lax.all_gather(norm_gains, ("batch", "frames"), axis=1, tiled=True),
            lax.all_gather(norm_biases, ("batch", "frames"), axis=1, tiled=True),
            lax.all_gather(mask_vector, ("batch", "frames"), axis=0, tiled=True),
            lax.all_gather(position_bias, ("batch", "frames"), axis=0, tiled=True),
            lax.all_gather(depth_gain, ("batch", "frames"), axis=0, tiled=True),
            lax.all_gather(depth_bias, ("batch", "frames"), axis=0, tiled=True),
            lax.all_gather(depth_kernel, ("batch", "frames"), axis=1, tiled=True),
        )

    def fetch_mixer():
        return (
            lax.all_gather(qkv_weight, ("batch", "frames"), axis=0, tiled=True),
            lax.all_gather(mixer_out, ("batch", "frames"), axis=0, tiled=True),
        )

    def fetch_depth():
        return (
            lax.all_gather(pointwise_in, ("batch", "frames"), axis=0, tiled=True),
            lax.all_gather(pointwise_out, ("batch", "frames"), axis=0, tiled=True),
        )

    def fetch_late():
        return (
            lax.all_gather(late_in, ("batch", "frames"), axis=0, tiled=True),
            lax.all_gather(late_out, ("batch", "frames"), axis=0, tiled=True),
        )

    early_kept = fetch_early()
    gains = early_kept[2].astype(jnp.float32)
    biases = early_kept[3].astype(jnp.float32)
    mask_full = early_kept[4].astype(jnp.float32)
    table = early_kept[5].astype(jnp.float32).reshape(H, NB)
    channel_gain = early_kept[6].astype(jnp.float32)
    channel_bias = early_kept[7].astype(jnp.float32)
    kernel_full = early_kept[8].astype(jnp.float32)
    frame_ids = first_frame + jnp.arange(local_len, dtype=jnp.int32)
    masked = jnp.any(positions[:, :, None] == frame_ids[None, None, :], axis=1).reshape(
        row_count, 1
    )
    span = length + local_len
    relative = jnp.arange(span, dtype=jnp.int32) - (local_len - 1) - first_frame
    onehot = (bucket_of(relative)[:, None] == jnp.arange(NB, dtype=jnp.int32)[None, :]).astype(
        jnp.float32
    )
    along = jnp.dot(table, onehot.T, precision=lax.Precision.HIGHEST)
    tiled_rows = jnp.tile(along, (1, local_len + 1))[
        :, local_len - 1 : local_len - 1 + local_len * (span - 1)
    ]
    bias_grid = tiled_rows.reshape(H, local_len, span - 1)[:, :, :length]

    def ffn_inner(hidden, which_norm, weight_in):
        normed = layer_norm(hidden, gains[which_norm], biases[which_norm]).astype(jnp.bfloat16)
        inner_rows = product(normed, weight_in)
        return (normed, inner_rows, jax.nn.silu(inner_rows).astype(jnp.bfloat16))

    def ffn_back(hidden, which_norm, weight_in, weight_out, grad_hidden):
        normed, inner_rows, activated = ffn_inner(hidden, which_norm, weight_in)
        grad_out = (0.5 * grad_hidden).astype(jnp.bfloat16)
        grad_weight_out = weight_grad(activated, grad_out)
        grad_act = back_product(grad_out, weight_out)
        silu_unused, silu_pull = jax.vjp(jax.nn.silu, inner_rows)
        grad_inner = silu_pull(grad_act)[0].astype(jnp.bfloat16)
        grad_weight_in = weight_grad(normed, grad_inner)
        grad_normed = back_product(grad_inner, weight_in)
        grad_input, gain_grad, bias_grad = norm_back(
            hidden, gains[which_norm], biases[which_norm], grad_normed
        )
        return (grad_hidden + grad_input, grad_weight_in, grad_weight_out, gain_grad, bias_grad)

    def project(hidden, weight_qkv):
        normed = layer_norm(hidden, gains[1], biases[1]).astype(jnp.bfloat16)
        packed = product(normed, weight_qkv).astype(jnp.bfloat16).reshape(groups, local_len, 3 * D)
        return (normed, packed)

    def share_keys(packed):
        return lax.all_gather(packed[:, :, D:], "frames", axis=1, tiled=True)

    def split_group(local_pack, remote):
        queries = local_pack[:, :D].reshape(local_len, H, DH)
        key_rows = remote[:, :D].reshape(length, H, DH)
        value_rows = remote[:, D:].reshape(length, H, DH)
        scores = (
            jnp.einsum("qhd,khd->hqk", queries, key_rows, preferred_element_type=jnp.float32)
            * score_scale
            + bias_grid
        )
        return (queries, key_rows, value_rows, scores)

    def attend_group(group_inputs):
        local_pack, remote = group_inputs
        queries, key_rows, value_rows, scores = split_group(local_pack, remote)
        row_max = jnp.max(scores, axis=-1, keepdims=True)
        weights = jnp.exp(scores - row_max)
        totals = jnp.sum(weights, axis=-1, keepdims=True)
        probabilities = (weights / totals).astype(jnp.bfloat16)
        mixed_group = jnp.einsum(
            "hqk,khd->qhd", probabilities, value_rows, preferred_element_type=jnp.float32
        )
        return (
            mixed_group.reshape(local_len, D).astype(jnp.bfloat16),
            (row_max + jnp.log(totals))[:, :, 0],
        )

    def row_grads(local_pack, remote, log_total, grad_group):
        queries, key_rows, value_rows, scores = split_group(local_pack, remote)
        probabilities = jnp.exp(scores - log_total[:, :, None])
        grad_heads = grad_group.reshape(local_len, H, DH)
        grad_probs = jnp.einsum(
            "qhd,khd->hqk", grad_heads, value_rows, preferred_element_type=jnp.float32
        )
        centre = jnp.sum(probabilities * grad_probs, axis=-1, keepdims=True)
        grad_scores = (probabilities * (grad_probs - centre)).astype(jnp.bfloat16)
        grad_queries = (
            jnp.einsum("hqk,khd->qhd", grad_scores, key_rows, preferred_element_type=jnp.float32)
            * score_scale
        )
        return (queries, grad_heads, probabilities, centre, grad_scores, grad_queries)

    def attend_back(grid_sum, group_inputs):
        local_pack, remote, log_total, grad_group = group_inputs
        queries, grad_heads, probabilities, centre, grad_scores, grad_queries = row_grads(
            local_pack, remote, log_total, grad_group
        )
        grad_keys = (
            jnp.einsum("hqk,qhd->khd", grad_scores, queries, preferred_element_type=jnp.float32)
            * score_scale
        )
        grad_values = jnp.einsum(
            "hqk,qhd->khd",
            probabilities.astype(jnp.bfloat16),
            grad_heads,
            preferred_element_type=jnp.float32,
        )
        merged = jnp.concatenate(
            [grad_keys.reshape(length, D), grad_values.reshape(length, D)], axis=-1
        )
        return (
            grid_sum + grad_scores.astype(jnp.float32),
            (grad_queries.reshape(local_len, D), merged),
        )

    def depth_front(hidden, weight_in):
        normed = layer_norm(hidden, gains[2], biases[2]).astype(jnp.bfloat16)
        paired = product(normed, weight_in)
        gated = gated_unit(paired).astype(jnp.bfloat16).reshape(groups, local_len, C)
        padded = padded_2(gated, (("frames", 1),), HALF)
        depth_values = jnp.zeros((groups, local_len, C), jnp.float32)
        for offset in range(KERNEL):
            depth_values = (
                depth_values
                + padded[:, offset : offset + local_len].astype(jnp.float32) * kernel_full[offset]
            )
        return (normed, paired, padded, depth_values)

    hidden0 = jnp.where(
        masked, mask_full[None, :], frames_in.reshape(row_count, D).astype(jnp.float32)
    )
    normed1, inner1, act1 = ffn_inner(hidden0, 0, early_kept[0])
    hidden1 = hidden0 + 0.5 * product(act1, early_kept[1])
    mixer_kept = fetch_mixer()
    normed2, packed = project(hidden1, mixer_kept[0])
    gathered = share_keys(packed)
    mixed_rows, log_totals = lax.map(attend_group, (packed, gathered))
    mixed_rows = mixed_rows.reshape(row_count, D)
    hidden2 = hidden1 + product(mixed_rows, mixer_kept[1])
    depth_kept = fetch_depth()
    normed3, paired, padded, depth_values = depth_front(hidden2, depth_kept[0])
    post = (
        depth_post(depth_values, channel_gain, channel_bias)
        .astype(jnp.bfloat16)
        .reshape(row_count, C)
    )
    hidden3 = hidden2 + product(post, depth_kept[1])
    late_kept = fetch_late()
    normed5, inner5, act5 = ffn_inner(hidden3, 3, late_kept[0])
    hidden4 = hidden3 + 0.5 * product(act5, late_kept[1])
    activations = (
        layer_norm(hidden4, gains[4], biases[4]).astype(jnp.bfloat16).reshape(groups, local_len, D)
    )
    upstream = cotangent.reshape(row_count, D).astype(jnp.float32)
    grad4, gain_grad4, bias_grad4 = norm_back(hidden4, gains[4], biases[4], upstream)
    late_used = fetch_late()
    grad3, late_in_grad, late_out_grad, gain_grad3, bias_grad3 = ffn_back(
        hidden3, 3, late_used[0], late_used[1], grad4
    )
    late_sums = (
        lax.psum_scatter(late_in_grad, ("batch", "frames"), scatter_dimension=0, tiled=True),
        lax.psum_scatter(late_out_grad, ("batch", "frames"), scatter_dimension=0, tiled=True),
    )
    depth_used = fetch_depth()
    normed3, paired, padded, depth_values = depth_front(hidden2, depth_used[0])
    post_values, post_pull = jax.vjp(depth_post, depth_values, channel_gain, channel_bias)
    post = post_values.astype(jnp.bfloat16).reshape(row_count, C)
    grad_out3 = grad3.astype(jnp.bfloat16)
    pointwise_out_grad = weight_grad(post, grad_out3)
    grad_post = back_product(grad_out3, depth_used[1]).reshape(groups, local_len, C)
    grad_depth, channel_gain_grad, channel_bias_grad = post_pull(grad_post)
    grad_depth_low = grad_depth.astype(jnp.bfloat16)
    grad_depth_wide = grad_depth_low.astype(jnp.float32)
    kernel_grad = jnp.stack(
        [
            jnp.sum(
                padded[:, offset : offset + local_len].astype(jnp.float32) * grad_depth_wide,
                axis=(0, 1),
            )
            for offset in range(KERNEL)
        ]
    )
    extended = padded_2(grad_depth_low, (("frames", 1),), HALF)
    grad_gated = jnp.zeros((groups, local_len, C), jnp.float32)
    for offset in range(KERNEL):
        start_at = 2 * HALF - offset
        grad_gated = (
            grad_gated
            + extended[:, start_at : start_at + local_len].astype(jnp.float32) * kernel_full[offset]
        )
    pair_unused, pair_pull = jax.vjp(gated_unit, paired)
    grad_paired = pair_pull(grad_gated.reshape(row_count, C))[0].astype(jnp.bfloat16)
    pointwise_in_grad = weight_grad(normed3, grad_paired)
    grad_normed3 = back_product(grad_paired, depth_used[0])
    grad_in3, gain_grad2, bias_grad2 = norm_back(hidden2, gains[2], biases[2], grad_normed3)
    grad2 = grad3 + grad_in3
    depth_sums = (
        lax.psum_scatter(pointwise_in_grad, ("batch", "frames"), scatter_dimension=0, tiled=True),
        lax.psum_scatter(pointwise_out_grad, ("batch", "frames"), scatter_dimension=0, tiled=True),
    )
    mixer_used = fetch_mixer()
    normed2, packed = project(hidden1, mixer_used[0])
    gathered = share_keys(packed)
    grad_out2 = grad2.astype(jnp.bfloat16)
    mixer_out_grad = weight_grad(mixed_rows, grad_out2)
    grad_mixed = (
        back_product(grad_out2, mixer_used[1]).astype(jnp.bfloat16).reshape(groups, local_len, D)
    )
    grid_start = jnp.zeros((H, local_len, length), jnp.float32)
    grid_sum, (grad_queries, grad_kv_full) = lax.scan(
        attend_back, grid_start, (packed, gathered, log_totals, grad_mixed)
    )
    grad_kv = lax.psum_scatter(
        grad_kv_full.astype(jnp.bfloat16), "frames", scatter_dimension=1, tiled=True
    )
    grad_packed = jnp.concatenate([grad_queries.astype(jnp.bfloat16), grad_kv], axis=-1)
    grad_packed = grad_packed.reshape(row_count, 3 * D)
    qkv_grad = weight_grad(normed2, grad_packed)
    grad_normed2 = back_product(grad_packed, mixer_used[0])
    grad_in2, gain_grad1, bias_grad1 = norm_back(hidden1, gains[1], biases[1], grad_normed2)
    grad1 = grad2 + grad_in2
    mixer_sums = (
        lax.psum_scatter(qkv_grad, ("batch", "frames"), scatter_dimension=0, tiled=True),
        lax.psum_scatter(mixer_out_grad, ("batch", "frames"), scatter_dimension=0, tiled=True),
    )
    early_used = fetch_early()
    grad0, early_in_grad, early_out_grad, gain_grad0, bias_grad0 = ffn_back(
        hidden0, 0, early_used[0], early_used[1], grad1
    )
    grad_frames = jnp.where(masked, 0.0, grad0).reshape(groups, local_len, D)
    mask_grad = jnp.sum(jnp.where(masked, grad0, 0.0), axis=0)
    gain_stack = jnp.stack([gain_grad0, gain_grad1, gain_grad2, gain_grad3, gain_grad4])
    bias_stack = jnp.stack([bias_grad0, bias_grad1, bias_grad2, bias_grad3, bias_grad4])
    widened = jnp.pad(grid_sum, ((0, 0), (0, 0), (0, span - 1 - length)))
    flat_rows = widened.reshape(H, local_len * (span - 1))
    flat_rows = jnp.pad(flat_rows, ((0, 0), (local_len - 1, span + 1)))
    along_grad = jnp.sum(flat_rows.reshape(H, local_len + 1, span), axis=1)
    table_grad = jnp.dot(along_grad, onehot, precision=lax.Precision.HIGHEST).reshape(H * NB)
    early_sums = (
        lax.psum_scatter(early_in_grad, ("batch", "frames"), scatter_dimension=0, tiled=True),
        lax.psum_scatter(early_out_grad, ("batch", "frames"), scatter_dimension=0, tiled=True),
        lax.psum_scatter(gain_stack, ("batch", "frames"), scatter_dimension=1, tiled=True),
        lax.psum_scatter(bias_stack, ("batch", "frames"), scatter_dimension=1, tiled=True),
        lax.psum_scatter(mask_grad, ("batch", "frames"), scatter_dimension=0, tiled=True),
        lax.psum_scatter(table_grad, ("batch", "frames"), scatter_dimension=0, tiled=True),
        lax.psum_scatter(channel_gain_grad, ("batch", "frames"), scatter_dimension=0, tiled=True),
        lax.psum_scatter(channel_bias_grad, ("batch", "frames"), scatter_dimension=0, tiled=True),
        lax.psum_scatter(kernel_grad, ("batch", "frames"), scatter_dimension=1, tiled=True),
    )
    return (
        activations,
        grad_frames,
        early_sums[4],
        early_sums[2],
        early_sums[3],
        early_sums[6],
        early_sums[7],
        early_sums[0],
        early_sums[1],
        mixer_sums[0],
        mixer_sums[1],
        depth_sums[0],
        depth_sums[1],
        early_sums[8],
        late_sums[0],
        late_sums[1],
        early_sums[5],
    )


def solution(mesh):
    in_specs = (
        P("batch", "frames", None),
        P("batch", None),
        P(("batch", "frames")),
        P(None, ("batch", "frames")),
        P(None, ("batch", "frames")),
        P(("batch", "frames")),
        P(("batch", "frames")),
        P(("batch", "frames"), None),
        P(("batch", "frames"), None),
        P(("batch", "frames"), None),
        P(("batch", "frames"), None),
        P(("batch", "frames"), None),
        P(("batch", "frames"), None),
        P(None, ("batch", "frames")),
        P(("batch", "frames"), None),
        P(("batch", "frames"), None),
        P(("batch", "frames")),
        P("batch", "frames", None),
    )
    out_specs = (
        P("batch", "frames", None),
        P("batch", "frames", None),
        P(("batch", "frames")),
        P(None, ("batch", "frames")),
        P(None, ("batch", "frames")),
        P(("batch", "frames")),
        P(("batch", "frames")),
        P(("batch", "frames"), None),
        P(("batch", "frames"), None),
        P(("batch", "frames"), None),
        P(("batch", "frames"), None),
        P(("batch", "frames"), None),
        P(("batch", "frames"), None),
        P(None, ("batch", "frames")),
        P(("batch", "frames"), None),
        P(("batch", "frames"), None),
        P(("batch", "frames")),
    )
    return jax.shard_map(shards, mesh=mesh, in_specs=in_specs, out_specs=out_specs, check_vma=False)
```

profile of v0, /device:TPU:0, one launch (start us, length us, event | category | flops | bytes accessed | tf_op | source)
XLA Modules:
  0.0 4131.2 jit_solution(4812908029451595109)
XLA Ops:
  12.9 42.6 %all-reduce.13 = (bf16[1024]{0:T(1024)(128)(2,1)S(1)}, bf16[512]{0:T(512)(128)(2,1)S(1)}, bf16[2048]{0:T(1024)(128)(2,1)}, bf16[2048]{0:T(1024)(128)(2,1)}) all-reduce(bf16[1024]{0:T(1024)(128)(2,1)S(1)} %dynamic-update-slice, bf16[512]{0:T(512)(128)(2,1)S(1)} %dynamic-update-slice.1, ...), channel_id=1, replica_groups=mesh['batch'=8,'frames'=4] {'batch','frames'}, use_global_device_ids=true, to_apply=%add.4 | all-reduce | flops 5632 | bytes 22528
  61.0 68.1 %all-gather = bf16[32,32,5]{1,2,0:T(8,128)(2,1)S(1)} all-gather(bf16[1,32,5]{1,2,0:T(8,128)(2,1)} %bitcast.459), channel_id=1, replica_groups=mesh['batch'=8,'frames'=4] {'batch','frames'}, dimensions={0}, use_global_device_ids=true | all-gather | bytes 10560 | tf_op jit(solution)/shard_map/all_gather | solution.py:112
  129.2 65.1 %all-gather.1 = bf16[32,32,5]{1,2,0:T(8,128)(2,1)S(1)} all-gather(bf16[1,32,5]{1,2,0:T(8,128)(2,1)} %bitcast.460), channel_id=1, replica_groups=mesh['batch'=8,'frames'=4] {'batch','frames'}, dimensions={0}, use_global_device_ids=true | all-gather | bytes 10560 | tf_op jit(solution)/shard_map/all_gather | solution.py:113
  260.3 27.3 tile.4
  287.6 34.0 tile.10
  346.9 58.0 %reshape.475 = f32[16,320,1599]{2,1,0:T(8,128)} reshape(f32[16,511680]{1,0:T(8,128)} %slice.674) | data formatting | bytes 65495040 | tf_op jit(solution)/shard_map/reshape | solution.py:160
  423.7 71.2 %all-gather.2 = bf16[32,64,31]{1,2,0:T(8,128)(2,1)S(1)} all-gather(bf16[1,64,31]{1,2,0:T(8,128)(2,1)S(1)} %bitcast.448), channel_id=1, replica_groups=mesh['batch'=8,'frames'=4] {'batch','frames'}, dimensions={0}, use_global_device_ids=true | all-gather | bytes 130944 | tf_op jit(solution)/shard_map/all_gather | solution.py:118
  502.4 26.1 copy.76
  528.5 90.0 %while.27 = (s32[]{:T(128)}, bf16[2,320,1024]{2,1,0:T(8,128)(2,1)}, f32[2,16,320]{2,1,0:T(8,128)S(1)}, bf16[2,1280,2048]{1,2,0:T(8,128)(2,1)}, bf16[2,320,3072]{...) while((s32[]{:T(128)}, bf16[2,320,1024]{2,1,0:T(8,128)(2,1)}, f32[2,16,320]{2,1,0:T(8,128)S(1)}, ...), condition=%wide.region_8.9_spmd, body=%wide.region_5.8_spmd.sunk | while | flops 1730472960 | bytes 175550704 | solution.py:274
  645.0 26.5 fusion.206
  687.6 33.2 all-gather.27.cloned.1.call-done
  732.3 67.4 %all-gather.29.cloned.1.call-done = bf16[4096,1024]{1,0:T(8,128)(2,1)} async-done(((bf16[128,1024]{1,0:T(8,128)(2,1)}), bf16[4096,1024]{1,0:T(8,128)(2,1)}) %all-gather.29.cloned.1.call-update) | async-done | bytes 8388624 | tf_op jit(solution)/shard_map/all_gather | solution.py:136
  885.0 50.6 %fusion.59 = f32[2,320,2048]{2,1,0:T(8,128)} fusion(bf16[2,320,2048]{2,1,0:T(8,128)(2,1)} %copy-done.6, bf16[2,15,2048]{2,1,0:T(8,128)(2,1)S(1)} %collective-permute-done.3, bf16[2,15,2048]{2,1,0:T(8,128)(2,1)S(1)} %collective-permute-done.2, f32[2048]{0:T(1024)S(1)} %bitcast.342, f32[2048]{0:T(1024)S(1)} %bitcast.344, f32[2048]{0:T(1024)S(1)} %bitcast.346, ...), kind=kLoop, calls=%fused_computation.208 | loop fusion | flops 238551040 | bytes 8364032 | tf_op jit(solution)/shard_map/add | solution.py:325
  966.6 252.0 %while.28 = (s32[]{:T(128)}, f32[16,320,1280]{2,1,0:T(8,128)}, bf16[2,320,1024]{2,1,0:T(8,128)(2,1)}, bf16[2,1280,2048]{2,1,0:T(8,128)(2,1)}, bf16[2,320,3072]{1...) while((s32[]{:T(128)}, f32[16,320,1280]{2,1,0:T(8,128)}, ...), condition=%wide.region_27.28_spmd.clone, body=%wide.region_25.27_spmd.clone.sunk | while | flops 4286704640 | bytes 417568000 | solution.py:347
  990.0 27.7 multiply_reduce_fusion.18
  1017.7 26.0 select_add_fusion.2
  1111.7 27.6 multiply_reduce_fusion.18
  1139.3 34.2 select_add_fusion.2
  1242.9 154.5 %reduce-scatter.19.cloned.1.call-done = bf16[2,320,2048]{2,1,0:T(8,128)(2,1)} async-done(((bf16[2,1280,2048]{2,1,0:T(8,128)(2,1)}), bf16[2,320,2048]{2,1,0:T(8,128)(2,1)}) %reduce-scatter.19.cloned.1.call-update) | async-done | bytes 2621456 | tf_op jit(solution)/shard_map/reduce_scatter | solution.py:350
  1564.6 42.1 %reshape.495 = f32[16,511680]{1,0:T(8,128)} reshape(f32[16,320,1599]{2,1,0:T(8,128)} %pad.16) | data formatting | bytes 65495040 | tf_op jit(solution)/shard_map/reshape | solution.py:372
  1606.8 25.4 pad.17
  1632.1 35.9 reshape.496
  1687.5 41.7 %all-reduce.12 = (f32[1024]{0:T(1024)S(1)}, f32[2048]{0:T(1024)S(1)}, f32[2048]{0:T(1024)S(1)}, f32[512]{0:T(512)S(1)}) all-reduce(f32[1024]{0:T(1024)S(1)} %get-tuple-element.322, f32[2048]{0:T(1024)S(1)} %copy-done.113, f32[2048]{0:T(1024)S(1)} %copy-done.112, ...), channel_id=3, replica_groups=mesh['batch'=8,'frames'=4] {'batch','frames'}, use_global_device_ids=true, to_apply=%region_34.35.clone | all-reduce | flops 5632 | bytes 45056
  1732.9 69.3 %reduce-scatter.37.cloned.1.call-done = f32[32,5]{1,0:T(8,128)} async-done(((f32[1024,5]{1,0:T(8,128)}), f32[32,5]{1,0:T(8,128)}) %reduce-scatter.37.cloned.1.call-update) | async-done | bytes 656
  1803.6 145.8 %reduce-scatter.27.cloned.1.call-done = f32[32,1024]{1,0:T(8,128)} async-done(((f32[1024,1024]{1,0:T(8,128)}), f32[32,1024]{1,0:T(8,128)}) %reduce-scatter.27.cloned.1.call-update) | async-done | bytes 131088 | tf_op jit(solution)/shard_map/reduce_scatter | solution.py:361
  1949.4 187.6 %reduce-scatter.31.cloned.1.call-done = f32[64,1024]{1,0:T(8,128)} async-done(((f32[2048,1024]{1,0:T(8,128)}), f32[64,1024]{1,0:T(8,128)}) %reduce-scatter.31.cloned.1.call-update) | async-done | bytes 262160 | tf_op jit(solution)/shard_map/reduce_scatter | solution.py:336
  2137.0 364.7 %reduce-scatter.35.cloned.1.call-done = f32[128,1024]{1,0:T(8,128)} async-done(((f32[4096,1024]{1,0:T(8,128)}), f32[128,1024]{1,0:T(8,128)}) %reduce-scatter.35.cloned.1.call-update) | async-done | bytes 524304 | tf_op jit(solution)/shard_map/reduce_scatter | solution.py:299
  2501.7 365.0 %reduce-scatter.33.cloned.1.call-done = f32[32,4096]{1,0:T(8,128)} async-done(((f32[1024,4096]{1,0:T(8,128)}), f32[32,4096]{1,0:T(8,128)}) %reduce-scatter.33.cloned.1.call-update) | async-done | bytes 524304 | tf_op jit(solution)/shard_map/reduce_scatter | solution.py:298
  2866.8 365.0 %reduce-scatter.29.cloned.1.call-done = f32[32,4096]{1,0:T(8,128)} async-done(((f32[1024,4096]{1,0:T(8,128)}), f32[32,4096]{1,0:T(8,128)}) %reduce-scatter.29.cloned.1.call-update) | async-done | bytes 524304 | tf_op jit(solution)/shard_map/reduce_scatter | solution.py:335
  3231.8 161.0 %reduce-scatter.25.cloned.1.call-done = f32[32,3072]{1,0:T(8,128)} async-done(((f32[1024,3072]{1,0:T(8,128)}), f32[32,3072]{1,0:T(8,128)}) %reduce-scatter.25.cloned.1.call-update) | async-done | bytes 393232 | tf_op jit(solution)/shard_map/reduce_scatter | solution.py:360
  3392.7 366.1 %reduce-scatter.23.cloned.1.call-done = f32[128,1024]{1,0:T(8,128)} async-done(((f32[4096,1024]{1,0:T(8,128)}), f32[128,1024]{1,0:T(8,128)}) %reduce-scatter.23.cloned.1.call-update) | async-done | bytes 524304 | tf_op jit(solution)/shard_map/reduce_scatter | solution.py:378
  3758.8 365.1 %reduce-scatter.21.cloned.1.call-done = f32[32,4096]{1,0:T(8,128)} async-done(((f32[1024,4096]{1,0:T(8,128)}), f32[32,4096]{1,0:T(8,128)}) %reduce-scatter.21.cloned.1.call-update) | async-done | bytes 524304 | tf_op jit(solution)/shard_map/reduce_scatter | solution.py:377
  (558 shorter events, 738.8 us)
Async XLA Ops:
  7.2 190.5 %all-gather.13.cloned.1.call-start = ((), (), s32[]{:S(2)}) async-start(), calls=%async_computation.12 | async-start | bytes 8650752 | tf_op jit(solution)/shard_map/all_gather | solution.py:110
  7.9 202.0 %all-gather.15.cloned.1.call-start = ((), (), s32[]{:S(2)}) async-start(), calls=%async_computation.13 | async-start | bytes 8650752 | tf_op jit(solution)/shard_map/all_gather | solution.py:111
  8.7 233.4 %all-gather.17.cloned.1.call-start = ((), (), s32[]{:S(2)}) async-start(), calls=%async_computation.14 | async-start | bytes 6488064 | tf_op jit(solution)/shard_map/all_gather | solution.py:123
  9.4 493.0 %all-gather.19.cloned.1.call-start = ((), (), s32[]{:S(2)}) async-start(), calls=%async_computation.15 | async-start | bytes 13107200 | tf_op jit(solution)/shard_map/all_gather | solution.py:187
  256.3 362.2 %all-gather.21.cloned.1.call-start = ((), (), s32[]{:S(2)}) async-start(), calls=%async_computation.16 | async-start | bytes 2162688 | tf_op jit(solution)/shard_map/all_gather | solution.py:124
  256.9 366.5 %all-gather.23.cloned.1.call-start = ((), (), s32[]{:S(2)}) async-start(), calls=%async_computation.17 | async-start | bytes 8650752 | tf_op jit(solution)/shard_map/all_gather | solution.py:129
  257.5 421.4 %all-gather.25.cloned.1.call-start = ((), (), s32[]{:S(2)}) async-start(), calls=%async_computation.18 | async-start | bytes 4325376 | tf_op jit(solution)/shard_map/all_gather | solution.py:130
  258.2 462.5 %all-gather.27.cloned.1.call-start = ((), (), s32[]{:S(2)}) async-start(), calls=%async_computation.19 | async-start | bytes 8650752 | tf_op jit(solution)/shard_map/all_gather | solution.py:135
  259.0 540.7 %all-gather.29.cloned.1.call-start = ((), (), s32[]{:S(2)}) async-start(), calls=%async_computation.20 | async-start | bytes 8650752 | tf_op jit(solution)/shard_map/all_gather | solution.py:136
  259.7 1137.6 %reduce-scatter.19.cloned.1.call-start = ((), (), s32[]{:S(2)}) async-start(), calls=%async_computation.21 | async-start | bytes 13107200 | tf_op jit(solution)/shard_map/reduce_scatter | solution.py:350
  623.0 336.7 %copy-start.45 = (f32[640]{0:T(1024)}, f32[640]{0:T(1024)S(1)}, u32[]{:S(2)}) copy-start(f32[640]{0:T(1024)S(1)} %broadcast_multiply_fusion.2) | copy-start | bytes 7684
  623.4 336.3 %copy-start.53 = (f32[640]{0:T(1024)}, f32[640]{0:T(1024)S(1)}, u32[]{:S(2)}) copy-start(f32[640]{0:T(1024)S(1)} %fusion.185) | copy-start | bytes 7684
  636.6 218.4 %copy-start.4 = (bf16[640,2048]{1,0:T(8,128)(2,1)}, bf16[640,2048]{1,0:T(8,128)(2,1)S(1)}, u32[]{:S(2)}) copy-start(bf16[640,2048]{1,0:T(8,128)(2,1)S(1)} %multiply_convert_fusion.4) | copy-start | bytes 7864324
  636.7 4.1 collective-permute-start
  638.0 6.9 collective-permute-start.1
  644.8 210.2 %copy-start.40 = (bf16[2,15,2048]{2,1,0:T(8,128)(2,1)}, bf16[2,15,2048]{2,1,0:T(8,128)(2,1)S(1)}, u32[]{:S(2)}) copy-start(bf16[2,15,2048]{2,1,0:T(8,128)(2,1)S(1)} %collective-permute-done.1) | copy-start | bytes 368644
  876.3 7.6 collective-permute-start.2
  877.6 7.4 collective-permute-start.3
  1218.7 462.3 %reduce-scatter.41.cloned.1.call-start = ((), (), s32[]{:S(2)}) async-start(), calls=%async_computation.32 | async-start | bytes 1081344
  1241.4 158.3 %copy-start.27 = (f32[640,1024]{1,0:T(8,128)S(1)}, f32[640,1024]{1,0:T(8,128)}, u32[]{:S(2)}) copy-start(f32[640,1024]{1,0:T(8,128)} %copy-done.26) | copy-start | bytes 7864324
  1241.4 158.3 %copy-start.86 = (f32[640]{0:T(1024)S(1)}, f32[640]{0:T(1024)}, u32[]{:S(2)}) copy-start(f32[640]{0:T(1024)} %copy-done.85) | copy-start | bytes 7684
  1241.4 158.3 %copy-start.115 = (f32[1,1024]{1,0:T(1,128)S(1)}, f32[1,1024]{1,0:T(1,128)}, u32[]{:S(2)}) copy-start(f32[1,1024]{1,0:T(1,128)} %copy-done.114) | copy-start | bytes 12292
  1242.9 488.7 %reduce-scatter.39.cloned.1.call-start = ((), (), s32[]{:S(2)}) async-start(), calls=%async_computation.31 | async-start | bytes 540672
  1437.5 364.7 %reduce-scatter.37.cloned.1.call-start = ((), (), s32[]{:S(2)}) async-start(), calls=%async_computation.30 | async-start | bytes 540672
  1438.7 510.7 %reduce-scatter.27.cloned.1.call-start = ((), (), s32[]{:S(2)}) async-start(), calls=%async_computation.25 | async-start | bytes 4325376 | tf_op jit(solution)/shard_map/reduce_scatter | solution.py:361
  1443.8 693.2 %reduce-scatter.31.cloned.1.call-start = ((), (), s32[]{:S(2)}) async-start(), calls=%async_computation.27 | async-start | bytes 8650752 | tf_op jit(solution)/shard_map/reduce_scatter | solution.py:336
  1453.6 1048.2 %reduce-scatter.35.cloned.1.call-start = ((), (), s32[]{:S(2)}) async-start(), calls=%async_computation.29 | async-start | bytes 17301504 | tf_op jit(solution)/shard_map/reduce_scatter | solution.py:299
  1470.7 1396.0 %reduce-scatter.33.cloned.1.call-start = ((), (), s32[]{:S(2)}) async-start(), calls=%async_computation.28 | async-start | bytes 17301504 | tf_op jit(solution)/shard_map/reduce_scatter | solution.py:298
  1485.5 1746.3 %reduce-scatter.29.cloned.1.call-start = ((), (), s32[]{:S(2)}) async-start(), calls=%async_computation.26 | async-start | bytes 17301504 | tf_op jit(solution)/shard_map/reduce_scatter | solution.py:335
  1501.8 1891.0 %reduce-scatter.25.cloned.1.call-start = ((), (), s32[]{:S(2)}) async-start(), calls=%async_computation.24 | async-start | bytes 12976128 | tf_op jit(solution)/shard_map/reduce_scatter | solution.py:360
  1513.8 2245.0 %reduce-scatter.23.cloned.1.call-start = ((), (), s32[]{:S(2)}) async-start(), calls=%async_computation.23 | async-start | bytes 17301504 | tf_op jit(solution)/shard_map/reduce_scatter | solution.py:378
  1530.3 2593.6 %reduce-scatter.21.cloned.1.call-start = ((), (), s32[]{:S(2)}) async-start(), calls=%async_computation.22 | async-start | bytes 17301504 | tf_op jit(solution)/shard_map/reduce_scatter | solution.py:377
  (147 other events, 2616.5 us)
Sparse Core Ops, SparseCore 0:
  11.0 80.4 all-gather.12
  94.4 76.3 all-gather.14
  173.7 68.2 all-gather.16
  256.4 183.6 all-gather.18
  442.9 54.7 all-gather.20
  500.4 76.2 all-gather.22
  579.7 61.4 all-gather.24
  644.1 76.6 all-gather.26
  723.7 75.9 all-gather.28
  1218.8 178.5 reduce-scatter.18
  1399.6 136.3 reduce-scatter.40
  1538.1 130.9 reduce-scatter.38
  1671.4 130.8 reduce-scatter.36
  1805.0 144.3 reduce-scatter.26
  1952.2 184.7 reduce-scatter.30
  2139.8 361.8 reduce-scatter.34
  2504.5 362.1 reduce-scatter.32
  2869.6 362.1 reduce-scatter.28
  3239.4 153.2 reduce-scatter.24
  3395.5 363.3 reduce-scatter.22
  3761.7 362.1 reduce-scatter.20
where the time goes:
time: 4140 us; the launch traced here: 4130 us
  waiting for transfers between devices  2670 us (64%)
  matrix products  440 us (11%)
  local copies, waits for them, and re-layouts  432 us (10%)
  blocking collectives  289 us (7%)
  other arithmetic  269 us (6%)
    reduce_scatter x1, waiting for transfers between devices, shards(): lax.psum_scatter(early_out_grad, ('batch', 'frames'), scatter_dimension=0...  366 us
    reduce_scatter x1, waiting for transfers between devices, shards(): lax.psum_scatter(early_in_grad, ('batch', 'frames'), scatter_dimension=0,...  365 us
    reduce_scatter x1, waiting for transfers between devices, shards(): lax.psum_scatter(late_in_grad, ('batch', 'frames'), scatter_dimension=0,...  365 us
    reduce_scatter x1, waiting for transfers between devices, shards(): lax.psum_scatter(pointwise_in_grad, ('batch', 'frames'), scatter_dimensio...  365 us
    reduce_scatter x1, waiting for transfers between devices, shards(): lax.psum_scatter(late_out_grad, ('batch', 'frames'), scatter_dimension=0,...  365 us
    reduce_scatter x1, waiting for transfers between devices, shards(): lax.psum_scatter(pointwise_out_grad, ('batch', 'frames'), scatter_dimensi...  188 us
    reduce_scatter x1, waiting for transfers between devices, shards(): lax.psum_scatter(qkv_grad, ('batch', 'frames'), scatter_dimension=0, tile...  161 us
    reduce_scatter x1, waiting for transfers between devices, shards(): lax.psum_scatter(grad_kv_full.astype(jnp.bfloat16), 'frames', scatter_dim...  154 us
  transfers between devices with their start and end apart: 25, of which 16 were waited for; matrix products, arithmetic and copies ran while one was open for 17% of the time, Pallas kernels for 0%

commit v1 on v0

v1 whole, which is shorter than its diff:
```python
import functools
import math

import jax
import jax.numpy as jnp
from jax import lax
from jax.experimental import pallas as pl
from jax.experimental.pallas import tpu as pltpu
from jax.sharding import PartitionSpec as P

MESH = pl.DeviceIdType.MESH


def ring_spot(index, count):
    half = count // 2
    return index + (index // half) * (3 * half - 1 - 2 * index)


def places(chips, frames):
    batch, depth = lax.axis_index("batch"), lax.axis_index("frames")
    chip, core = batch // 2, lax.rem(batch, 2)
    spot = ring_spot(chip, chips)

    def chip_at(offset):
        return ring_spot(lax.rem(spot + offset + chips, chips), chips)

    return chip, core, depth, chip_at


def shares(columns):
    first = columns * 3 // 4 if columns % 1024 == 0 else columns
    return ((0, first), (first, columns - first))


def greet(chips, frames, partners):
    chip, core, depth, chip_at = places(chips, frames)
    barrier = pltpu.get_barrier_semaphore()
    for offset in (1, -1):
        pl.semaphore_signal(
            barrier, inc=1, device_id=(chip_at(offset) * 2 + core, depth), device_id_type=MESH
        )
    pl.semaphore_signal(
        barrier, inc=1, device_id=(chip * 2 + 1 - core, depth), device_id_type=MESH
    )

    @pl.when(depth > 0)
    def _():
        pl.semaphore_signal(barrier, inc=1, device_id=(chip * 2 + core, depth - 1), device_id_type=MESH)

    @pl.when(depth < frames - 1)
    def _():
        pl.semaphore_signal(barrier, inc=1, device_id=(chip * 2 + core, depth + 1), device_id_type=MESH)

    count = 3 + jnp.minimum(depth, 1) + jnp.minimum(frames - 1 - depth, 1)
    if partners:
        groups = frames // 2
        for place in range(groups):
            there, side = core * groups + place, depth // groups

            @pl.when(jnp.logical_or(there != depth, side != core))
            def _():
                pl.semaphore_signal(
                    barrier, inc=1, device_id=(chip * 2 + side, there), device_id_type=MESH
                )

        count = count + groups - (1 - jnp.abs(depth // groups - core))
    pl.semaphore_wait(barrier, count)


def swap_frames(chips, frames, sources, targets, send_sems, recv_sems, local_sem):
    chip, core, depth, chip_at = places(chips, frames)
    groups = frames // 2
    later = []
    for at, (source, target) in enumerate(zip(sources, targets)):
        for place in range(groups):
            there, side = core * groups + place, depth // groups
            mine = jnp.logical_and(there == depth, side == core)
            slot = lax.rem(depth, groups)
            remote = pltpu.make_async_remote_copy(
                src_ref=source.at[place],
                dst_ref=target.at[slot],
                send_sem=send_sems.at[at * groups + place],
                recv_sem=recv_sems.at[at * groups + slot],
                device_id=(chip * 2 + side, there),
                device_id_type=MESH,
            )
            here = pltpu.make_async_copy(source.at[place], target.at[slot], local_sem.at[at])
            pl.when(jnp.logical_not(mine))(remote.start)
            pl.when(mine)(here.start)
            arrival = pltpu.make_async_remote_copy(
                src_ref=source.at[place],
                dst_ref=target.at[place],
                send_sem=send_sems.at[at * groups + place],
                recv_sem=recv_sems.at[at * groups + place],
                device_id=(chip * 2 + side, there),
                device_id_type=MESH,
            )
            later.append((mine, remote, arrival, here))

    def finish():
        for mine, remote, arrival, here in later:
            pl.when(jnp.logical_not(mine))(remote.wait_send)
            pl.when(jnp.logical_not(mine))(arrival.wait_recv)
            pl.when(mine)(here.wait)

    return finish


class Gather:
    def __init__(self, spots, chips, frames, shard, whole, send_sems, recv_sems, local_sem):
        self.chips, self.frames = chips, frames
        self.chip, self.core, self.depth, self.chip_at = spots
        self.shard, self.whole = shard, whole
        self.send_sems, self.recv_sems, self.local_sem = send_sems, recv_sems, local_sem
        self.sent = []
        self.local = None
        self.phases = (frames - 1) + chips // 2
        self.waiting = []
        self.used = 0
        self.pair = None

    def copy(self, source, target, device, condition=None):
        at = self.used
        self.used += 1
        made = pltpu.make_async_remote_copy(
            src_ref=source,
            dst_ref=target,
            send_sem=self.send_sems.at[at],
            recv_sem=self.recv_sems.at[at],
            device_id=device,
            device_id_type=MESH,
        )
        return made

    def line_step(self, step, start, width, wide):
        columns = pl.ds(start, width)
        for way in (1, -1):
            origin = self.depth - way * (step - 1)
            to = self.depth + way
            valid = jnp.logical_and(
                jnp.logical_and(origin >= 0, origin < self.frames),
                jnp.logical_and(to >= 0, to < self.frames),
            )
            held = jnp.clip(origin, 0, self.frames - 1)
            into = jnp.clip(to, 0, self.frames - 1)
            if wide:
                source = self.whole.at[:, self.core, held, :, columns]
                target = source
            else:
                target = self.whole.at[self.chip, self.core, held, :, columns]
                source = self.shard.at[:, columns] if step == 1 else target
            made = self.copy(source, target, (self.chip * 2 + self.core, into))
            pl.when(valid)(made.start)
            self.sent.append((valid, made))
            before = self.depth - way * step
            comes = jnp.logical_and(before >= 0, before < self.frames)
            self.waiting.append((comes, made))

    def ring_step(self, step, start, width, wide):
        last = step == self.chips // 2
        for side, way in enumerate((1, -1)):
            origin = self.chip_at(-way * (step - 1))
            columns = pl.ds(start + (side * width // 2 if last else 0), width // 2 if last else width)
            if wide:
                source = self.whole.at[origin, self.core, :, :, columns]
                target = source
            else:
                target = self.whole.at[origin, self.core, self.depth, :, columns]
                source = self.shard.at[:, columns] if step == 1 else target
            made = self.copy(source, target, (self.chip_at(way) * 2 + self.core, self.depth))
            made.start()
            self.sent.append((None, made))
            self.waiting.append((None, made))

    def arrive(self):
        for condition, made in self.waiting:
            if condition is None:
                made.wait_recv()
            else:
                pl.when(condition)(made.wait_recv)
        self.waiting = []

    def phase(self, at):
        line, ring = self.frames - 1, self.chips // 2
        if at == 0:
            self.local = pltpu.make_async_copy(
                self.shard, self.whole.at[self.chip, self.core, self.depth], self.local_sem
            )
            self.local.start()
        self.arrive()
        if at == min(line, ring):
            self.local.wait()
        (first_start, first_width), (last_start, last_width) = shares(self.shard.shape[1])
        if at < self.phases:
            if at < line:
                self.line_step(at + 1, first_start, first_width, False)
            else:
                self.ring_step(at - line + 1, first_start, first_width, True)
            if last_width:
                if at < ring:
                    self.ring_step(at + 1, last_start, last_width, False)
                else:
                    self.line_step(at - ring + 1, last_start, last_width, True)
        elif at == self.phases:
            half = self.whole.at[:, self.core]
            self.pair = self.copy(half, half, (self.chip * 2 + 1 - self.core, self.depth))
            self.pair.start()
        else:
            self.pair.wait()

    def drain(self):
        for condition, made in self.sent:
            if condition is None:
                made.wait_send()
            else:
                pl.when(condition)(made.wait_send)


def gather_kernel(chips, frames, count, swaps, *refs):
    shards, refs = refs[:count], refs[count:]
    sources, refs = refs[:swaps], refs[swaps:]
    wholes, refs = refs[:count], refs[count:]
    targets, refs = refs[:swaps], refs[swaps:]
    send_sems, recv_sems, local_sems, swap_send, swap_recv, swap_local = refs
    greet(chips, frames, swaps > 0)
    finish = (
        swap_frames(chips, frames, sources, targets, swap_send, swap_recv, swap_local)
        if swaps
        else None
    )
    spots = places(chips, frames)
    parts = [
        Gather(
            spots, chips, frames, shard, whole, send_sems.at[at], recv_sems.at[at], local_sems.at[at]
        )
        for at, (shard, whole) in enumerate(zip(shards, wholes))
    ]
    phases = parts[0].phases + 2
    for time in range(phases + count - 1):
        for at, part in enumerate(parts):
            if 0 <= time - at < phases:
                part.phase(time - at)
    for part in parts:
        part.drain()
    if finish is not None:
        finish()


def gather_all(mesh_sizes, shards, swapped, identity):
    chips, frames = mesh_sizes
    count, swaps = len(shards), len(swapped)
    copies = 2 * 2 * (frames - 1 + chips // 2) + 1
    out_shape = [
        jax.ShapeDtypeStruct((chips, 2, frames) + shard.shape, shard.dtype) for shard in shards
    ] + [jax.ShapeDtypeStruct(array.shape, array.dtype) for array in swapped]
    groups = frames // 2
    return pl.pallas_call(
        functools.partial(gather_kernel, chips, frames, count, swaps),
        out_shape=out_shape,
        in_specs=[pl.BlockSpec(memory_space=pl.ANY)] * (count + swaps),
        out_specs=[pl.BlockSpec(memory_space=pl.ANY)] * (count + swaps),
        scratch_shapes=[
            pltpu.SemaphoreType.DMA((count, copies)),
            pltpu.SemaphoreType.DMA((count, copies)),
            pltpu.SemaphoreType.DMA((count,)),
            pltpu.SemaphoreType.DMA((max(swaps, 1) * groups,)),
            pltpu.SemaphoreType.DMA((max(swaps, 1) * groups,)),
            pltpu.SemaphoreType.DMA((max(swaps, 1),)),
        ],
        compiler_params=pltpu.CompilerParams(collective_id=identity, has_side_effects=True),
    )(*shards, *swapped)


class Scatter:
    def __init__(self, spots, chips, frames, grads, out, total, stage, bounds, send_sems, recv_sems, local_sems):
        self.chips, self.frames = chips, frames
        self.chip, self.core, self.depth, self.chip_at = spots
        self.grads, self.out, self.total, self.stage = grads, out, total, stage
        self.bounds = list(bounds)
        self.send_sems, self.recv_sems, self.local_sems = send_sems, recv_sems, local_sems
        self.sent = []
        self.waiting = []
        self.phases = (frames - 1) + chips // 2
        self.used = 0
        self.pair = None

    def copy(self, source, target, device):
        at = self.used
        self.used += 1
        return pltpu.make_async_remote_copy(
            src_ref=source,
            dst_ref=target,
            send_sem=self.send_sems.at[at],
            recv_sem=self.recv_sems.at[at],
            device_id=device,
            device_id_type=MESH,
        )

    def begin(self):
        self.pair = self.copy(
            self.grads.at[:, 1 - self.core], self.total, (self.chip * 2 + 1 - self.core, self.depth)
        )
        self.pair.start()

    def load(self, chip):
        slot = chip % 2
        made = pltpu.make_async_copy(
            self.grads.at[chip, self.core], self.stage.at[slot], self.local_sems.at[slot]
        )
        made.start()
        return made

    def merge(self):
        loads = [self.load(0)]
        self.pair.wait()
        total, stage = self.total, self.stage
        for chip in range(self.chips):
            if chip + 1 < self.chips:
                loads.append(self.load(chip + 1))
            loads[chip].wait()

            @pl.loop(0, self.frames)
            def _(depth):
                total[chip, depth] = (
                    total[chip, depth].astype(jnp.float32)
                    + stage[chip % 2, depth].astype(jnp.float32)
                ).astype(total.dtype)

    def line_step(self, step, start, width, wide):
        frames = self.frames
        for way in (1, -1):
            reach = frames - step
            goal = self.depth + way * reach
            valid = jnp.logical_and(goal >= 0, goal < frames)
            held = jnp.clip(goal, 0, frames - 1)
            into = jnp.clip(self.depth + way, 0, frames - 1)
            columns = pl.ds(start, width)
            if wide:
                source = self.total.at[:, held, :, columns]
            else:
                source = self.total.at[self.chip, held, :, columns]
            landed = self.bounds.pop(0)
            made = self.copy(source, landed, (self.chip * 2 + self.core, into))
            pl.when(valid)(made.start)
            self.sent.append((valid, made))
            before = self.depth - way
            origin_goal = before + way * reach
            comes = jnp.logical_and(
                jnp.logical_and(before >= 0, before < frames),
                jnp.logical_and(origin_goal >= 0, origin_goal < frames),
            )
            goes = jnp.clip(origin_goal, 0, frames - 1)
            self.waiting.append((comes, made, landed, ("line", goes, wide, start, width)))

    def ring_step(self, step, start, width, wide):
        half = self.chips // 2
        for side, way in enumerate((1, -1)):
            reach = half - step + 1
            first = start + (side * width // 2 if step == 1 else 0)
            extent = width // 2 if step == 1 else width
            columns = pl.ds(first, extent)
            goal = self.chip_at(way * reach)
            if wide:
                source = self.total.at[goal, :, :, columns]
            else:
                source = self.total.at[goal, self.depth, :, columns]
            landed = self.bounds.pop(0)
            made = self.copy(source, landed, (self.chip_at(way) * 2 + self.core, self.depth))
            made.start()
            self.sent.append((None, made))
            goes = self.chip_at(way * (reach - 1))
            self.waiting.append((None, made, landed, ("ring", goes, wide, first, extent)))

    def arrive(self):
        for condition, made, landed, place in self.waiting:
            kind, goes, wide, start, width = place

            def settle(made=made, landed=landed, kind=kind, goes=goes, wide=wide, start=start, width=width):
                made.wait_recv()
                columns = pl.ds(start, width)
                total = self.total

                def merged(at, piece):
                    total[at] = (total[at].astype(jnp.float32) + piece.astype(jnp.float32)).astype(
                        total.dtype
                    )

                if not wide:
                    where = (self.chip, goes) if kind == "line" else (goes, self.depth)
                    merged(where + (slice(None), columns), landed[...])
                else:
                    count = self.chips if kind == "line" else self.frames

                    @pl.loop(0, count)
                    def _(at):
                        where = (at, goes) if kind == "line" else (goes, at)
                        merged(where + (slice(None), columns), landed[at])

            if condition is None:
                settle()
            else:
                pl.when(condition)(settle)
        self.waiting = []

    def phase(self, at):
        line, ring = self.frames - 1, self.chips // 2
        self.arrive()
        (first_start, first_width), (last_start, last_width) = shares(self.total.shape[-1])
        if at < self.phases:
            if at < ring:
                self.ring_step(at + 1, first_start, first_width, True)
            else:
                self.line_step(at - ring + 1, first_start, first_width, False)
            if last_width:
                if at < line:
                    self.line_step(at + 1, last_start, last_width, True)
                else:
                    self.ring_step(at - line + 1, last_start, last_width, False)
        else:
            self.out[...] = self.total[self.chip, self.depth].astype(self.out.dtype)

    def drain(self):
        for condition, made in self.sent:
            if condition is None:
                made.wait_send()
            else:
                pl.when(condition)(made.wait_send)


def landing_shapes(chips, frames, rows, columns):
    (_, first), (_, last) = shares(columns)
    line, ring = frames - 1, chips // 2
    shapes = []
    for at in range(line + ring):
        if at < ring:
            shapes += [(frames, rows, first // 2 if at == 0 else first)] * 2
        else:
            shapes += [(rows, first)] * 2
        if last:
            if at < line:
                shapes += [(chips, rows, last)] * 2
            else:
                shapes += [(rows, last // 2 if at == line else last)] * 2
    return shapes


def scatter_kernel(chips, frames, count, swaps, landings, *refs):
    grads, refs = refs[:count], refs[count:]
    sources, refs = refs[:swaps], refs[swaps:]
    outs, refs = refs[:count], refs[count:]
    targets, refs = refs[:swaps], refs[swaps:]
    totals, refs = refs[:count], refs[count:]
    stages, refs = refs[:count], refs[count:]
    bounds = []
    for many in landings:
        bounds.append(refs[:many])
        refs = refs[many:]
    send_sems, recv_sems, local_sems, swap_send, swap_recv, swap_local = refs
    greet(chips, frames, swaps > 0)
    finish = (
        swap_frames(chips, frames, sources, targets, swap_send, swap_recv, swap_local)
        if swaps
        else None
    )
    spots = places(chips, frames)
    parts = [
        Scatter(
            spots,
            chips,
            frames,
            grads[at],
            outs[at],
            totals[at],
            stages[at],
            bounds[at],
            send_sems.at[at],
            recv_sems.at[at],
            local_sems.at[at],
        )
        for at in range(count)
    ]
    for part in parts:
        part.begin()
    phases = parts[0].phases + 1
    for time in range(phases + count - 1):
        for at, part in enumerate(parts):
            if 0 <= time - at < phases:
                if time == at:
                    part.merge()
                part.phase(time - at)
    for part in parts:
        part.drain()
    if finish is not None:
        finish()


def scatter_all(mesh_sizes, grads, swapped, identity):
    chips, frames = mesh_sizes
    count, swaps = len(grads), len(swapped)
    copies = 2 * 2 * (frames - 1 + chips // 2) + 1
    groups = frames // 2
    shards = [grad.shape[3:] for grad in grads]
    landings = [landing_shapes(chips, frames, *shard) for shard in shards]
    any_spec = pl.BlockSpec(memory_space=pl.ANY)
    scratch = [pltpu.VMEM((chips, frames) + shard, jnp.bfloat16) for shard in shards]
    scratch += [pltpu.VMEM((2, frames) + shard, jnp.bfloat16) for shard in shards]
    scratch += [pltpu.VMEM(shape, jnp.bfloat16) for shapes in landings for shape in shapes]
    return pl.pallas_call(
        functools.partial(
            scatter_kernel, chips, frames, count, swaps, [len(shapes) for shapes in landings]
        ),
        out_shape=[jax.ShapeDtypeStruct(shard, jnp.float32) for shard in shards]
        + [jax.ShapeDtypeStruct(array.shape, array.dtype) for array in swapped],
        in_specs=[any_spec] * (count + swaps),
        out_specs=[pl.BlockSpec(memory_space=pltpu.VMEM)] * count + [any_spec] * swaps,
        scratch_shapes=scratch
        + [
            pltpu.SemaphoreType.DMA((count, copies)),
            pltpu.SemaphoreType.DMA((count, copies)),
            pltpu.SemaphoreType.DMA((count, 2)),
            pltpu.SemaphoreType.DMA((max(swaps, 1) * groups,)),
            pltpu.SemaphoreType.DMA((max(swaps, 1) * groups,)),
            pltpu.SemaphoreType.DMA((max(swaps, 1),)),
        ],
        compiler_params=pltpu.CompilerParams(
            collective_id=identity, has_side_effects=True, vmem_limit_bytes=58 * 1024 * 1024
        ),
    )(*grads, *swapped)


D = 1024
H = 16
DH = 64
C = 2048
KERNEL = 31
HALF = 15
NB = 32
EPS = 1e-05
LIMITS = (8, 12, 16, 24, 32, 48, 64, 96)
BOTH = ("batch", "frames")
SMALL = (16, 512)


def layer_norm(values, norm_gain, norm_shift):
    centred = values - jnp.mean(values, axis=-1, keepdims=True)
    spread = jnp.mean(centred * centred, axis=-1, keepdims=True)
    return centred * lax.rsqrt(spread + EPS) * norm_gain + norm_shift


def bucket_of(relative):
    magnitude = jnp.abs(relative)
    above = jnp.zeros_like(relative)
    for threshold in LIMITS:
        above = above + (magnitude >= threshold).astype(jnp.int32)
    inner_bucket = jnp.where(magnitude < 8, magnitude, 7 + above)
    return inner_bucket + NB // 2 * (relative > 0).astype(jnp.int32)


def product(operand_a, operand_b):
    return jnp.dot(operand_a, operand_b, preferred_element_type=jnp.float32)


def weight_grad(operand_a, operand_b):
    return lax.dot_general(
        operand_a, operand_b, (((0,), (0,)), ((), ())), preferred_element_type=jnp.float32
    ).astype(jnp.bfloat16)


def back_product(operand_a, operand_b):
    return lax.dot_general(
        operand_a, operand_b, (((1,), (1,)), ((), ())), preferred_element_type=jnp.float32
    )


def gated_unit(paired):
    return paired[:, :C] * jax.nn.sigmoid(paired[:, C:])


def depth_post(depth_values, norm_gain, norm_shift):
    return jax.nn.silu(layer_norm(depth_values, norm_gain, norm_shift))


def norm_back(hidden, norm_gain, norm_shift, upstream):
    normed_unused, pull_back = jax.vjp(layer_norm, hidden, norm_gain, norm_shift)
    return pull_back(upstream)


def as_shard(array):
    rows = array.shape[0]
    return array if rows % 16 == 0 else array.reshape(16, rows * array.shape[1] // 16)


def as_weight(whole, like):
    devices = math.prod(whole.shape[:3])
    return whole.reshape(devices * like.shape[0], like.shape[1])


def as_parts(grad, sizes, like):
    chips, frames = sizes
    shard = as_shard(jnp.zeros(like.shape, jnp.bfloat16)).shape
    return grad.reshape((chips, 2, frames) + shard)


def pack_small(values, small_shapes):
    flat = jnp.concatenate([value.reshape(-1) for value in values])
    return jnp.pad(flat, (0, SMALL[0] * SMALL[1] - flat.shape[0])).reshape(SMALL)


def unpack_small(packed, shapes):
    devices = packed.shape[0]
    at, out = 0, []
    for shape in shapes:
        size = math.prod(shape)
        piece = packed[:, at : at + size].reshape((devices,) + shape)
        at += size
        piece = jnp.moveaxis(piece, 0, -2)
        out.append(piece.reshape(shape[:-1] + (devices * shape[-1],)))
    return out


def repack_small(values, shapes, devices):
    pieces = []
    for value, shape in zip(values, shapes):
        piece = value.reshape(shape[:-1] + (devices, shape[-1]))
        pieces.append(jnp.moveaxis(piece, -2, 0).reshape(devices, -1))
    flat = jnp.concatenate(pieces, axis=1)
    return jnp.pad(flat, ((0, 0), (0, SMALL[0] * SMALL[1] - flat.shape[1])))


def shards(
    frames_in,
    positions,
    mask_vector,
    norm_gains,
    norm_biases,
    depth_gain,
    depth_bias,
    early_in,
    early_out,
    qkv_weight,
    mixer_out,
    pointwise_in,
    pointwise_out,
    depth_kernel,
    late_in,
    late_out,
    position_bias,
    cotangent,
):
    groups, run, model_width = frames_in.shape
    line = lax.axis_size("frames")
    chips = lax.axis_size("batch") // 2
    sizes = (chips, line)
    devices = 2 * chips * line
    length = run * line
    rows = groups * run
    score_scale = 1.0 / math.sqrt(DH)
    batch, depth = lax.axis_index("batch"), lax.axis_index("frames")
    core = lax.rem(batch, 2)
    first_frame = core * rows
    partner = [(at, at + 1 - 2 * (at % 2)) for at in range(2 * chips)]

    def from_other(array):
        return lax.ppermute(array, "batch", partner)

    big = [early_in, early_out, qkv_weight, mixer_out, pointwise_in, pointwise_out, late_in, late_out]
    small = [mask_vector, norm_gains, norm_biases, depth_gain, depth_bias, depth_kernel, position_bias]
    small_shapes = [value.shape for value in small]
    small_size = sum(math.prod(shape) for shape in small_shapes)
    gathered = gather_all(
        sizes,
        [as_shard(value) for value in big] + [pack_small(small, small_shapes)],
        [frames_in, cotangent],
        0,
    )
    wholes = [as_weight(whole, like) for whole, like in zip(gathered, big)]
    w_early_in, w_early_out, w_qkv, w_mixer, w_point_in, w_point_out, w_late_in, w_late_out = wholes
    small_whole = gathered[len(big)].reshape(devices, SMALL[0] * SMALL[1])
    mask_full, gains, biases, channel_gain, channel_bias, kernel_full, table = [
        value.astype(jnp.float32) for value in unpack_small(small_whole, small_shapes)
    ]
    table = table.reshape(H, NB)
    frames_here = gathered[len(big) + 1].reshape(rows, D)
    upstream = gathered[len(big) + 2].reshape(rows, D).astype(jnp.float32)

    both = jnp.where(core == 0, 0, 1)
    other_positions = from_other(positions)
    owner = depth // groups
    listed = jnp.where(owner == both, positions, other_positions)
    listed = lax.dynamic_index_in_dim(listed, lax.rem(depth, groups), 0, keepdims=False)
    frame_ids = first_frame + jnp.arange(rows, dtype=jnp.int32)
    masked = jnp.any(listed[:, None] == frame_ids[None, :], axis=0).reshape(rows, 1)

    relative = jnp.arange(length, dtype=jnp.int32)[None, :] - frame_ids[:, None]
    bucket_index = bucket_of(relative)
    bias_grid = jnp.zeros((H, rows, length), jnp.float32)
    for at in range(NB):
        bias_grid = jnp.where(bucket_index[None] == at, table[:, at][:, None, None], bias_grid)

    def ffn_inner(hidden, which_norm, weight_in):
        normed = layer_norm(hidden, gains[which_norm], biases[which_norm]).astype(jnp.bfloat16)
        inner_rows = product(normed, weight_in)
        return (normed, inner_rows, jax.nn.silu(inner_rows).astype(jnp.bfloat16))

    def ffn_back(hidden, which_norm, kept, weight_in, weight_out, grad_hidden):
        normed, inner_rows, activated = kept
        grad_out = (0.5 * grad_hidden).astype(jnp.bfloat16)
        grad_weight_out = weight_grad(activated, grad_out)
        grad_act = back_product(grad_out, weight_out)
        silu_unused, silu_pull = jax.vjp(jax.nn.silu, inner_rows)
        grad_inner = silu_pull(grad_act)[0].astype(jnp.bfloat16)
        grad_weight_in = weight_grad(normed, grad_inner)
        grad_normed = back_product(grad_inner, weight_in)
        grad_input, gain_grad, bias_grad = norm_back(
            hidden, gains[which_norm], biases[which_norm], grad_normed
        )
        return (grad_hidden + grad_input, grad_weight_in, grad_weight_out, gain_grad, bias_grad)

    def in_order(mine, other):
        return jnp.where(
            core == 0,
            jnp.concatenate([mine, other], axis=0),
            jnp.concatenate([other, mine], axis=0),
        )

    def halves(whole):
        first, second = whole[:rows], whole[rows:]
        return jnp.where(core == 0, first, second), jnp.where(core == 0, second, first)

    hidden0 = jnp.where(masked, mask_full[None, :], frames_here.astype(jnp.float32))
    kept1 = ffn_inner(hidden0, 0, w_early_in)
    hidden1 = hidden0 + 0.5 * product(kept1[2], w_early_out)
    normed2 = layer_norm(hidden1, gains[1], biases[1]).astype(jnp.bfloat16)
    packed = product(normed2, w_qkv).astype(jnp.bfloat16)
    key_values = in_order(packed[:, D:], from_other(packed[:, D:]))
    queries = packed[:, :D].reshape(rows, H, DH)
    key_rows = key_values[:, :D].reshape(length, H, DH)
    value_rows = key_values[:, D:].reshape(length, H, DH)
    scores = (
        jnp.einsum("qhd,khd->hqk", queries, key_rows, preferred_element_type=jnp.float32)
        * score_scale
        + bias_grid
    )
    probabilities = jax.nn.softmax(scores, axis=-1)
    mixed_rows = (
        jnp.einsum(
            "hqk,khd->qhd",
            probabilities.astype(jnp.bfloat16),
            value_rows,
            preferred_element_type=jnp.float32,
        )
        .reshape(rows, D)
        .astype(jnp.bfloat16)
    )
    hidden2 = hidden1 + product(mixed_rows, w_mixer)

    normed3 = layer_norm(hidden2, gains[2], biases[2]).astype(jnp.bfloat16)
    paired = product(normed3, w_point_in)
    gated = gated_unit(paired).astype(jnp.bfloat16)

    def with_edges(array):
        sent = jnp.where(core == 0, array[rows - HALF :], array[:HALF])
        edge = from_other(sent)
        nothing = jnp.zeros_like(edge)
        return jnp.concatenate(
            [jnp.where(core == 0, nothing, edge), array, jnp.where(core == 0, edge, nothing)], axis=0
        )

    padded = with_edges(gated)
    depth_values = jnp.zeros((rows, C), jnp.float32)
    for offset in range(KERNEL):
        depth_values = (
            depth_values + padded[offset : offset + rows].astype(jnp.float32) * kernel_full[offset]
        )
    post_values, post_pull = jax.vjp(depth_post, depth_values, channel_gain, channel_bias)
    post = post_values.astype(jnp.bfloat16)
    hidden3 = hidden2 + product(post, w_point_out)
    kept5 = ffn_inner(hidden3, 3, w_late_in)
    hidden4 = hidden3 + 0.5 * product(kept5[2], w_late_out)
    activations = layer_norm(hidden4, gains[4], biases[4]).astype(jnp.bfloat16)

    grad4, gain_grad4, bias_grad4 = norm_back(hidden4, gains[4], biases[4], upstream)
    grad3, late_in_grad, late_out_grad, gain_grad3, bias_grad3 = ffn_back(
        hidden3, 3, kept5, w_late_in, w_late_out, grad4
    )
    grad_out3 = grad3.astype(jnp.bfloat16)
    pointwise_out_grad = weight_grad(post, grad_out3)
    grad_post = back_product(grad_out3, w_point_out)
    grad_depth, channel_gain_grad, channel_bias_grad = post_pull(grad_post)
    grad_depth_low = grad_depth.astype(jnp.bfloat16)
    grad_depth_wide = grad_depth_low.astype(jnp.float32)
    kernel_grad = jnp.stack(
        [
            jnp.sum(padded[offset : offset + rows].astype(jnp.float32) * grad_depth_wide, axis=0)
            for offset in range(KERNEL)
        ]
    )
    extended = with_edges(grad_depth_low)
    grad_gated = jnp.zeros((rows, C), jnp.float32)
    for offset in range(KERNEL):
        start_at = 2 * HALF - offset
        grad_gated = (
            grad_gated
            + extended[start_at : start_at + rows].astype(jnp.float32) * kernel_full[offset]
        )
    pair_unused, pair_pull = jax.vjp(gated_unit, paired)
    grad_paired = pair_pull(grad_gated)[0].astype(jnp.bfloat16)
    pointwise_in_grad = weight_grad(normed3, grad_paired)
    grad_normed3 = back_product(grad_paired, w_point_in)
    grad_in3, gain_grad2, bias_grad2 = norm_back(hidden2, gains[2], biases[2], grad_normed3)
    grad2 = grad3 + grad_in3

    grad_out2 = grad2.astype(jnp.bfloat16)
    mixer_out_grad = weight_grad(mixed_rows, grad_out2)
    grad_heads = back_product(grad_out2, w_mixer).astype(jnp.bfloat16).reshape(rows, H, DH)
    grad_probs = jnp.einsum(
        "qhd,khd->hqk", grad_heads, value_rows, preferred_element_type=jnp.float32
    )
    centre = jnp.sum(probabilities * grad_probs, axis=-1, keepdims=True)
    grad_scores = probabilities * (grad_probs - centre)
    table_grad = jnp.stack(
        [
            jnp.sum(jnp.where(bucket_index[None] == at, grad_scores, 0.0), axis=(1, 2))
            for at in range(NB)
        ],
        axis=-1,
    ).reshape(H * NB)
    grad_scores = grad_scores.astype(jnp.bfloat16)
    grad_queries = (
        jnp.einsum("hqk,khd->qhd", grad_scores, key_rows, preferred_element_type=jnp.float32)
        * score_scale
    )
    grad_keys = (
        jnp.einsum("hqk,qhd->khd", grad_scores, queries, preferred_element_type=jnp.float32)
        * score_scale
    )
    grad_values = jnp.einsum(
        "hqk,qhd->khd",
        probabilities.astype(jnp.bfloat16),
        grad_heads,
        preferred_element_type=jnp.float32,
    )
    merged = jnp.concatenate([grad_keys.reshape(length, D), grad_values.reshape(length, D)], axis=-1)
    merged_own, merged_other = halves(merged)
    grad_kv = merged_own + from_other(merged_other.astype(jnp.bfloat16)).astype(jnp.float32)
    grad_packed = jnp.concatenate(
        [grad_queries.reshape(rows, D).astype(jnp.bfloat16), grad_kv.astype(jnp.bfloat16)], axis=-1
    )
    qkv_grad = weight_grad(normed2, grad_packed)
    grad_normed2 = back_product(grad_packed, w_qkv)
    grad_in2, gain_grad1, bias_grad1 = norm_back(hidden1, gains[1], biases[1], grad_normed2)
    grad1 = grad2 + grad_in2
    grad0, early_in_grad, early_out_grad, gain_grad0, bias_grad0 = ffn_back(
        hidden0, 0, kept1, w_early_in, w_early_out, grad1
    )
    grad_frames = jnp.where(masked, 0.0, grad0).astype(jnp.bfloat16)
    mask_grad = jnp.sum(jnp.where(masked, grad0, 0.0), axis=0)
    gain_stack = jnp.stack([gain_grad0, gain_grad1, gain_grad2, gain_grad3, gain_grad4])
    bias_stack = jnp.stack([bias_grad0, bias_grad1, bias_grad2, bias_grad3, bias_grad4])
    small_grads = repack_small(
        [mask_grad, gain_stack, bias_stack, channel_gain_grad, channel_bias_grad, kernel_grad, table_grad],
        small_shapes,
        devices,
    ).astype(jnp.bfloat16)

    def parts(grad, like):
        return as_parts(grad, sizes, like)

    sums_late = scatter_all(
        sizes,
        [
            parts(late_out_grad, late_out),
            parts(late_in_grad, late_in),
            parts(pointwise_out_grad, pointwise_out),
            parts(pointwise_in_grad, pointwise_in),
        ],
        [],
        1,
    )
    sums_early = scatter_all(
        sizes,
        [
            parts(mixer_out_grad, mixer_out),
            parts(qkv_grad, qkv_weight),
            parts(early_out_grad, early_out),
            parts(early_in_grad, early_in),
            small_grads.reshape((chips, 2, line) + SMALL),
        ],
        [activations.reshape(groups, run, D), grad_frames.reshape(groups, run, D)],
        2,
    )
    small_sums = sums_early[4].reshape(-1)[:small_size]
    small_out, at = [], 0
    for shape in small_shapes:
        size = math.prod(shape)
        small_out.append(small_sums[at : at + size].reshape(shape))
        at += size
    return (
        sums_early[5],
        sums_early[6].astype(jnp.float32),
        small_out[0],
        small_out[1],
        small_out[2],
        small_out[3],
        small_out[4],
        sums_early[3].reshape(early_in.shape),
        sums_early[2].reshape(early_out.shape),
        sums_early[1].reshape(qkv_weight.shape),
        sums_early[0].reshape(mixer_out.shape),
        sums_late[3].reshape(pointwise_in.shape),
        sums_late[2].reshape(pointwise_out.shape),
        small_out[5],
        sums_late[1].reshape(late_in.shape),
        sums_late[0].reshape(late_out.shape),
        small_out[6],
    )


def solution(mesh):
    in_specs = (
        P("batch", "frames", None),
        P("batch", None),
        P(("batch", "frames")),
        P(None, ("batch", "frames")),
        P(None, ("batch", "frames")),
        P(("batch", "frames")),
        P(("batch", "frames")),
        P(("batch", "frames"), None),
        P(("batch", "frames"), None),
        P(("batch", "frames"), None),
        P(("batch", "frames"), None),
        P(("batch", "frames"), None),
        P(("batch", "frames"), None),
        P(None, ("batch", "frames")),
        P(("batch", "frames"), None),
        P(("batch", "frames"), None),
        P(("batch", "frames")),
        P("batch", "frames", None),
    )
    out_specs = (
        P("batch", "frames", None),
        P("batch", "frames", None),
        P(("batch", "frames")),
        P(None, ("batch", "frames")),
        P(None, ("batch", "frames")),
        P(("batch", "frames")),
        P(("batch", "frames")),
        P(("batch", "frames"), None),
        P(("batch", "frames"), None),
        P(("batch", "frames"), None),
        P(("batch", "frames"), None),
        P(("batch", "frames"), None),
        P(("batch", "frames"), None),
        P(None, ("batch", "frames")),
        P(("batch", "frames"), None),
        P(("batch", "frames"), None),
        P(("batch", "frames")),
    )
    return jax.shard_map(shards, mesh=mesh, in_specs=in_specs, out_specs=out_specs, check_vma=False)
```

time: 4140 us -> 1580 us (0.38)
  waiting for transfers between devices: 2670 us -> 0.01 us
  Pallas kernels: 0 us -> 576 us
  local copies, waits for them, and re-layouts: 432 us -> 75.8 us
  blocking collectives: 289 us -> 0 us
  other arithmetic: 269 us -> 451 us
    reduce_scatter x9 -> x0, waiting for transfers between devices: 2470 us -> none  [the longest x1 366 us: shards(): lax.psum_scatter(early_out_grad, ('batch', 'frames'), scatter_dimension=0...]
    pallas_call x0 -> x3, Pallas kernels: none -> 576 us  [the longest x2 294 us: scatter_all(): pl.pallas_call(functools.partial(scatter_kernel, chips, frames, count, sw...]
    all_gather x3 -> x0, blocking collectives: 204 us -> none  [the longest x1 71.2 us: fetch_early(): lax.all_gather(depth_kernel, ('batch', 'frames'), axis=1, tiled=True)]
    reduce_sum x8 -> x6, other arithmetic: 73.2 us -> 266 us  [the longest x2 229 us: shards(): jnp.sum(jnp.where(bucket_index[None] == at, grad_scores, 0.0), axis=(1, 2))]
    reshape x5 -> x11, local copies, waits for them, and re-layouts: 136 us -> 6.1 us  [the longest x3 2.31 us: pack_small(): flat = jnp.concatenate([value.reshape(-1) for value in values])]
    all_gather x9 -> x0, waiting for transfers between devices: 118 us -> none  [the longest x1 67.4 us: fetch_late(): lax.all_gather(late_out, ('batch', 'frames'), axis=0, tiled=True)]
    add x5 -> x1, other arithmetic: 111 us -> 0.01 us  [shards(): frame_ids = first_frame + jnp.arange(rows, dtype=jnp.int32)]
    unnamed x2 -> x0, blocking collectives: 84.3 us -> none
  transfers between devices with their start and end apart: 25 -> 5, of which waited for: 16 -> 0; matrix products, arithmetic and copies ran while one was open for 17% -> 5% of each run, Pallas kernels for 0% -> 18%
where the time goes in v1:
time: 1580 us; the launch traced here: 1570 us
  Pallas kernels  576 us (36%)
  matrix products  463 us (29%)
  other arithmetic  451 us (29%)
  local copies, waits for them, and re-layouts  75.8 us (5%)
    pallas_call x2, Pallas kernels, scatter_all(): pl.pallas_call(functools.partial(scatter_kernel, chips, frames, count, sw...  294 us
    pallas_call x1, Pallas kernels, gather_all(): pl.pallas_call(functools.partial(gather_kernel, chips, frames, count, swa...  282 us
    reduce_sum x2, other arithmetic, shards(): jnp.sum(jnp.where(bucket_index[None] == at, grad_scores, 0.0), axis=(1, 2))  229 us
    dot_general x1, matrix products, shards(): jnp.einsum('qhd,khd->hqk', queries, key_rows, preferred_element_type=jnp....  131 us
    dot_general x8, matrix products, weight_grad(): lax.dot_general(operand_a, operand_b, (((0,), (0,)), ((), ())), preferred...  81.4 us
    dot_general x8, matrix products, back_product(): lax.dot_general(operand_a, operand_b, (((1,), (1,)), ((), ())), preferred...  75 us
    dot_general x8, matrix products, product(): return jnp.dot(operand_a, operand_b, preferred_element_type=jnp.float32)  58.6 us
    sub x1, other arithmetic, shards(): probabilities = jax.nn.softmax(scores, axis=-1)  53.5 us
  transfers between devices with their start and end apart: 5, of which 0 were waited for; matrix products, arithmetic and copies ran while one was open for 5% of the time, Pallas kernels for 18%

profile of v1, /device:TPU:0, one launch (start us, length us, event | category | flops | bytes accessed | tf_op | source)
XLA Modules:
  0.0 1571.6 jit_solution(3549319803064754088)
XLA Ops:
  6.9 282.0 %shard_map.305 = (bf16[4,2,4,32,4096]{4,3,2,1,0:T(8,128)(2,1)}, bf16[4,2,4,128,1024]{4,3,2,1,0:T(8,128)(2,1)}, bf16[4,2,4,32,3072]{4,3,2,1,0:T(8,128)(2,1)}, bf1...) custom-call(bf16[32,4096]{1,0:T(8,128)(2,1)} %refs_0_.1, ...), custom_call_target="tpu_custom_call" | custom-call | tf_op jit(solution)/shard_map/pallas_call | solution.py:257
  298.8 12.0 fusion.229
  310.9 9.9 fusion.224
  326.5 23.8 %broadcast_compare_fusion.25 = (pred[640,1280]{1,0:T(8,128)(4,1)S(1)}, pred[640,1280]{1,0:T(8,128)(4,1)}, pred[640,1280]{1,0:T(8,128)(4,1)}, pred[640,1280]{1,0:...) fusion(s32[640]{0:T(1024)S(1)} %iota_add_fusion), kind=kLoop, calls=%fused_computation.453 | loop fusion | flops 51609600 | bytes 26216960 | tf_op jit(solution)/shard_map/eq | solution.py:698
  383.2 131.4 %select_add_fusion = f32[16,640,1280]{2,1,0:T(8,128)} fusion(bf16[640,16,64]{0,2,1:T(8,128)(2,1)} %bitcast.222, bf16[1280,16,64]{0,2,1:T(8,128)(2,1)S(1)} %bitcast.216, f32[16]{0:T(128)S(1)} %get-tuple-element.173, f32[16]{0:T(128)S(1)} %get-tuple-element.174, f32[16]{0:T(128)S(1)} %get-tuple-element.175, f32[16]{0:T(128)S(1)} %get-tuple-element.176, ...), kind=kOutput, calls=%fused_computation.36 | convolution fusion | flops 2123366400 | bytes 82577408 | tf_op jit(solution)/shard_map/qhd,khd->hqk/dot_general | solution.py:740
  514.7 53.5 %fusion.225 = (f32[16,640]{1,0:T(8,128)S(1)}, f32[16,640,1280]{2,1,0:T(8,128)}) fusion(f32[16,640,1280]{2,1,0:T(8,128)} %select_add_fusion), kind=kOutput, calls=%fused_computation.678 | output fusion | flops 26215680 | bytes 104898560 | tf_op jit(solution)/shard_map/sub | solution.py:744
  568.2 18.9 %fusion.178 = bf16[16,64,640]{2,1,0:T(8,128)(2,1)S(1)} fusion(bf16[1280,16,64]{0,2,1:T(8,128)(2,1)S(1)} %bitcast.229, f32[16,640,1280]{2,1,0:T(8,128)} %get-tuple-element.287, f32[16,640]{1,0:T(8,128)S(1)} %get-tuple-element.286), kind=kOutput, calls=%fused_computation.463 | convolution fusion | flops 1704591360 | bytes 56401920 | tf_op jit(solution)/shard_map/hqk,khd->qhd/dot_general | solution.py:746
  609.7 24.9 %fusion.216 = (f32[640]{0:T(1024)S(1)}, f32[640,2048]{1,0:T(8,128)S(1)}) fusion(f32[2048]{0:T(1024)S(1)} %mul.1187, bf16[15,2048]{1,0:T(8,128)(2,1)S(1)} %get-tuple-element.247, bf16[640,2048]{1,0:T(8,128)(2,1)S(1)} %multiply_convert_fusion.3, f32[2048]{0:T(1024)S(1)} %mul.1184, f32[2048]{0:T(1024)S(1)} %mul.1181, f32[2048]{0:T(1024)S(1)} %mul.1178, ...), kind=kLoop, calls=%fused_computation.670 | loop fusion | flops 239861120 | bytes 8243712 | tf_op jit(solution)/shard_map/jvp()/reduce_sum | solution.py:545
  639.7 8.7 fusion.207
  648.4 12.2 fusion.228
  664.3 14.5 fusion.11
  678.9 14.8 convolution_convert_fusion.3
  693.7 9.0 multiply_reduce_fusion.4
  702.6 9.6 convolution_convert_fusion.1
  728.7 18.9 %fusion.95 = (bf16[2048]{0:T(1024)(128)(2,1)S(1)}, bf16[2048]{0:T(1024)(128)(2,1)S(1)}, bf16[2048]{0:T(1024)(128)(2,1)S(1)}, bf16[2048]{0:T(1024)(128)(2,1)S(1)}...) fusion(bf16[15,2048]{1,0:T(8,128)(2,1)S(1)} %copy-done.36, ...), kind=kLoop, calls=%fused_computation.270 | loop fusion | flops 74692608 | bytes 10586624 | tf_op jit(solution)/shard_map/reduce_sum | solution.py:794
  759.0 6.6 fusion.79
  773.6 27.8 %fusion.47 = (f32[640,2048]{1,0:T(8,128)}, f32[640,2048]{1,0:T(8,128)S(1)}) fusion(f32[640,4096]{1,0:T(8,128)} %copy-done.2, f32[2048]{0:T(1024)S(1)} %copy-done.90, bf16[640,2048]{1,0:T(8,128)(2,1)S(1)} %get-tuple-element.205, bf16[15,2048]{1,0:T(8,128)(2,1)S(1)} %get-tuple-element.245, f32[2048]{0:T(1024)S(1)} %copy-done.92, f32[2048]{0:T(1024)S(1)} %copy-done.94, ...), kind=kLoop, calls=%fused_computation.222 | loop fusion | flops 247726080 | bytes 23969792 | tf_op jit(solution)/shard_map/transpose(jvp())/mul | solution.py:576
  807.9 14.5 multiply_reduce_fusion.5
  822.3 13.5 convolution_convert_fusion
  845.7 19.7 %fusion.5 = f32[16,64,1280]{2,1,0:T(8,128)} fusion(bf16[640,16,64]{0,2,1:T(8,128)(2,1)S(1)} %bitcast.237, f32[16,640,1280]{2,1,0:T(8,128)} %get-tuple-element.287, f32[16,640]{1,0:T(8,128)S(1)} %copy-done.57), kind=kOutput, calls=%fused_computation.132 | convolution fusion | flops 1703936000 | bytes 59023360 | tf_op jit(solution)/shard_map/hqk,qhd->khd/dot_general | solution.py:837
  865.5 39.7 %multiply_reduce_fusion = (f32[16,640]{1,0:T(8,128)S(1)}, f32[16,640,1280]{2,1,0:T(8,128)}) fusion(f32[16,640,1280]{2,1,0:T(8,128)} %get-tuple-element.287, f32[16,640]{1,0:T(8,128)S(1)} %copy-done.57, bf16[640,16,64]{0,2,1:T(8,128)(2,1)} %bitcast.238, bf16[1280,16,64]{0,2,1:T(8,128)(2,1)} %bitcast.228), kind=kOutput, calls=%fused_computation.34 | convolution fusion | flops 1717032960 | bytes 108871680 | tf_op jit(solution)/shard_map/qhd,khd->hqk/dot_general | solution.py:816
  905.2 136.8 %select_reduce_fusion = (bf16[16]{0:T(256)(128)(2,1)S(1)}, bf16[16]{0:T(256)(128)(2,1)S(1)}, bf16[16]{0:T(256)(128)(2,1)S(1)}, bf16[16]{0:T(256)(128)(2,1)S(1)},...) fusion(pred[640,1280]{1,0:T(8,128)(4,1)S(1)} %copy-done.21, ...), kind=kLoop, calls=%fused_computation.1 | loop fusion | flops 511180672 | bytes 172114496 | tf_op jit(solution)/shard_map/reduce_sum | solution.py:823
  1042.0 92.4 %select_reduce_fusion.18 = (bf16[16]{0:T(256)(128)(2,1)S(1)}, bf16[16]{0:T(256)(128)(2,1)S(1)}, bf16[16]{0:T(256)(128)(2,1)S(1)}, bf16[16]{0:T(256)(128)(2,1)S(1...) fusion(f32[16,640,1280]{2,1,0:T(8,128)} %get-tuple-element.204,, ...), kind=kLoop, calls=%fused_computation.19 | loop fusion | flops 367001408 | bytes 63898048 | tf_op jit(solution)/shard_map/reduce_sum | solution.py:823
  1134.4 19.8 %fusion.99 = f32[16,64,1280]{2,1,0:T(8,128)} fusion(bf16[640,16,64]{0,2,1:T(8,128)(2,1)S(1)} %bitcast.223, f32[16,640,1280]{2,1,0:T(8,128)} %get-tuple-element.204), kind=kOutput, calls=%fused_computation.288 | convolution fusion | flops 1692139520 | bytes 58982400 | tf_op jit(solution)/shard_map/hqk,qhd->khd/dot_general | solution.py:834
  1154.3 137.7 %shard_map.307 = (f32[128,1024]{1,0:T(8,128)}, f32[32,4096]{1,0:T(8,128)}, f32[64,1024]{1,0:T(8,128)}, f32[32,4096]{1,0:T(8,128)}) custom-call(bf16[4,2,4,128,1024]{4,3,2,1,0:T(8,128)(2,1)} %bitcast.218, bf16[4,2,4,32,4096]{4,3,2,1,0:T(8,128)(2,1)} %bitcast.219, bf16[4,2,4,64,1024]{4,3,2,1,0:T(8,128)(2,1)} %bitcast.227, bf16[4,2,4,32,4096]{4,3,2,1,0:T(8,128)(2,1)} %bitcast.213), custom_call_target="tpu_custom_call" | custom-call | tf_op jit(solution)/shard_map/pallas_call | solution.py:508
  1298.8 18.5 %multiply_convert_fusion.5 = bf16[16,64,640]{2,1,0:T(8,128)(2,1)S(1)} fusion(bf16[1280,16,64]{0,2,1:T(8,128)(2,1)S(1)} %bitcast.217, f32[16,640,1280]{2,1,0:T(8,128)} %get-tuple-element.204), kind=kOutput, calls=%fused_computation.404 | convolution fusion | flops 1692139520 | bytes 56360960 | tf_op jit(solution)/shard_map/hqk,khd->qhd/dot_general | solution.py:830
  1323.3 8.9 multiply_reduce_fusion.6
  1332.2 8.9 convolution_convert_fusion.5
  1343.2 14.5 fusion.14
  1357.7 14.0 convolution_convert_fusion.4
  1386.9 11.6 convolution_convert_fusion.2
  1398.5 156.2 %shard_map.306 = (f32[32,1024]{1,0:T(8,128)}, f32[32,3072]{1,0:T(8,128)}, f32[128,1024]{1,0:T(8,128)}, f32[32,4096]{1,0:T(8,128)}, f32[16,512]{1,0:T(8,128)}, /*...) custom-call(bf16[4,2,4,32,1024]{4,3,2,1,0:T(8,128)(2,1)} %bitcast.231, bf16[4,2,4,32,3072]{4,3,2,1,0:T(8,128)(2,1)} %bitcast.224, ...), custom_call_target="tpu_custom_call" | custom-call | tf_op jit(solution)/shard_map/pallas_call | solution.py:508
  (713 shorter events, 182.5 us)
Async XLA Ops:
  0.7 292.7 %copy-start.190 = (s32[2,640]{1,0:T(2,128)S(1)}, s32[2,640]{1,0:T(2,128)}, u32[]{:S(2)}) copy-start(s32[2,640]{1,0:T(2,128)} %param.19) | copy-start | bytes 15364
  0.7 292.7 %collective-permute-start = (s32[2,640]{1,0:T(2,128)}, s32[2,640]{1,0:T(2,128)S(1)}, u32[]{:S(2)}, u32[]{:S(2)}) collective-permute-start(s32[2,640]{1,0:T(2,128)} %param.19), channel_id=1, source_target_pairs={{0,4},{4,0},{8,12},{12,8},{16,20},{20,16},{24,28},{28,24},{1,5},{5... | collective-permute-start | bytes 15368 | tf_op jit(solution)/shard_map/ppermute | solution.py:664
  326.3 41.7 %collective-permute-start.1 = (bf16[640,2048]{1,0:T(8,128)(2,1)S(1)}, bf16[640,2048]{1,0:T(8,128)(2,1)}, u32[]{:S(2)}, u32[]{:S(2)}) collective-permute-start(bf16[640,2048]{1,0:T(8,128)(2,1)S(1)} %slice.826), channel_id=1, source_target_pairs={{0,4},{4,0},{8,12},{12,8},{16,20},{20,16},{24,28},{28,24},{1,5},{5... | collective-permute-start | bytes 7864328 | tf_op jit(solution)/shard_map/ppermute | solution.py:664
  350.3 32.9 %copy-start.20 = (pred[640,1280]{1,0:T(8,128)(4,1)}, pred[640,1280]{1,0:T(8,128)(4,1)S(1)}, u32[]{:S(2)}) copy-start(pred[640,1280]{1,0:T(8,128)(4,1)S(1)} %get-tuple-element.250) | copy-start | bytes 2457604
  378.3 136.4 %copy-start.8 = (bf16[1280,1024]{0,1:T(8,128)(2,1)}, bf16[1280,1024]{0,1:T(8,128)(2,1)S(1)}, u32[]{:S(2)}) copy-start(bf16[1280,1024]{0,1:T(8,128)(2,1)S(1)} %copy.85) | copy-start | bytes 7864324
  514.7 53.5 %copy-start.32 = (bf16[1280,1024]{0,1:T(8,128)(2,1)S(1)}, bf16[1280,1024]{0,1:T(8,128)(2,1)}, u32[]{:S(2)}) copy-start(bf16[1280,1024]{0,1:T(8,128)(2,1)} %copy.83) | copy-start | bytes 7864324
  514.7 75.5 %slice-start.6 = ((s8[8388608]{0:T(1024)(128)(4,1)}), s8[4194304]{0:T(1024)(128)(4,1)S(1)}, s32[]{:S(2)}) async-start(s8[8388608]{0:T(1024)(128)(4,1)} %bitcast.299), calls=%async_computation.6 | async-start | bytes 8388608
  599.9 34.7 %copy-start = (bf16[640,2048]{1,0:T(8,128)(2,1)}, bf16[640,2048]{1,0:T(8,128)(2,1)S(1)}, u32[]{:S(2)}) copy-start(bf16[640,2048]{1,0:T(8,128)(2,1)S(1)} %multiply_convert_fusion.3) | copy-start | bytes 7864324
  600.0 9.7 collective-permute-start.2
  771.5 1.8 collective-permute-start.3
  865.4 39.7 %copy-start.21 = (pred[640,1280]{1,0:T(8,128)(4,1)S(1)}, pred[640,1280]{1,0:T(8,128)(4,1)}, u32[]{:S(2)}) copy-start(pred[640,1280]{1,0:T(8,128)(4,1)} %copy-done.20) | copy-start | bytes 2457604
  865.4 39.7 %copy-start.22 = (pred[640,1280]{1,0:T(8,128)(4,1)S(1)}, pred[640,1280]{1,0:T(8,128)(4,1)}, u32[]{:S(2)}) copy-start(pred[640,1280]{1,0:T(8,128)(4,1)} %get-tuple-element.251) | copy-start | bytes 2457604
  865.4 39.7 %copy-start.23 = (pred[640,1280]{1,0:T(8,128)(4,1)S(1)}, pred[640,1280]{1,0:T(8,128)(4,1)}, u32[]{:S(2)}) copy-start(pred[640,1280]{1,0:T(8,128)(4,1)} %get-tuple-element.252) | copy-start | bytes 2457604
  865.4 39.7 %copy-start.24 = (pred[640,1280]{1,0:T(8,128)(4,1)S(1)}, pred[640,1280]{1,0:T(8,128)(4,1)}, u32[]{:S(2)}) copy-start(pred[640,1280]{1,0:T(8,128)(4,1)} %get-tuple-element.253) | copy-start | bytes 2457604
  865.4 39.8 %copy-start.25 = (pred[640,1280]{1,0:T(8,128)(4,1)S(1)}, pred[640,1280]{1,0:T(8,128)(4,1)}, u32[]{:S(2)}) copy-start(pred[640,1280]{1,0:T(8,128)(4,1)} %get-tuple-element.254) | copy-start | bytes 2457604
  865.4 39.8 %copy-start.26 = (pred[640,1280]{1,0:T(8,128)(4,1)S(1)}, pred[640,1280]{1,0:T(8,128)(4,1)}, u32[]{:S(2)}) copy-start(pred[640,1280]{1,0:T(8,128)(4,1)} %get-tuple-element.255) | copy-start | bytes 2457604
  865.4 39.8 %copy-start.27 = (pred[640,1280]{1,0:T(8,128)(4,1)S(1)}, pred[640,1280]{1,0:T(8,128)(4,1)}, u32[]{:S(2)}) copy-start(pred[640,1280]{1,0:T(8,128)(4,1)} %get-tuple-element.256) | copy-start | bytes 2457604
  865.4 39.8 %copy-start.28 = (pred[640,1280]{1,0:T(8,128)(4,1)S(1)}, pred[640,1280]{1,0:T(8,128)(4,1)}, u32[]{:S(2)}) copy-start(pred[640,1280]{1,0:T(8,128)(4,1)} %get-tuple-element.257) | copy-start | bytes 2457604
  865.4 39.8 %copy-start.29 = (pred[640,1280]{1,0:T(8,128)(4,1)S(1)}, pred[640,1280]{1,0:T(8,128)(4,1)}, u32[]{:S(2)}) copy-start(pred[640,1280]{1,0:T(8,128)(4,1)} %get-tuple-element.258) | copy-start | bytes 2457604
  865.5 39.8 %copy-start.30 = (pred[640,1280]{1,0:T(8,128)(4,1)S(1)}, pred[640,1280]{1,0:T(8,128)(4,1)}, u32[]{:S(2)}) copy-start(pred[640,1280]{1,0:T(8,128)(4,1)} %get-tuple-element.259) | copy-start | bytes 2457604
  1042.0 92.4 %copy-start.18 = (bf16[640,1024]{0,1:T(8,128)(2,1)S(1)}, bf16[640,1024]{0,1:T(8,128)(2,1)}, u32[]{:S(2)}) copy-start(bf16[640,1024]{0,1:T(8,128)(2,1)} %copy.84) | copy-start | bytes 3932164
  1154.3 137.8 %copy-start.181 = (bf16[1024]{0:T(1024)(128)(2,1)S(1)}, bf16[1024]{0:T(1024)(128)(2,1)}, u32[]{:S(2)}) copy-start(bf16[1024]{0:T(1024)(128)(2,1)} %get-tuple-element.127) | copy-start | bytes 6148
  1154.3 137.9 %copy-start.180 = (bf16[1024]{0:T(1024)(128)(2,1)S(1)}, bf16[1024]{0:T(1024)(128)(2,1)}, u32[]{:S(2)}) copy-start(bf16[1024]{0:T(1024)(128)(2,1)} %get-tuple-element.138) | copy-start | bytes 6148
  1154.3 137.9 %copy-start.182 = (bf16[16]{0:T(256)(128)(2,1)S(1)}, bf16[16]{0:T(256)(128)(2,1)}, u32[]{:S(2)}) copy-start(bf16[16]{0:T(256)(128)(2,1)} %get-tuple-element.71) | copy-start | bytes 100
  1154.3 137.9 %copy-start.183 = (bf16[16]{0:T(256)(128)(2,1)S(1)}, bf16[16]{0:T(256)(128)(2,1)}, u32[]{:S(2)}) copy-start(bf16[16]{0:T(256)(128)(2,1)} %get-tuple-element.72) | copy-start | bytes 100
  1154.3 137.9 %copy-start.184 = (bf16[16]{0:T(256)(128)(2,1)S(1)}, bf16[16]{0:T(256)(128)(2,1)}, u32[]{:S(2)}) copy-start(bf16[16]{0:T(256)(128)(2,1)} %get-tuple-element.73) | copy-start | bytes 100
  1154.3 137.9 %copy-start.185 = (bf16[16]{0:T(256)(128)(2,1)S(1)}, bf16[16]{0:T(256)(128)(2,1)}, u32[]{:S(2)}) copy-start(bf16[16]{0:T(256)(128)(2,1)} %get-tuple-element.74) | copy-start | bytes 100
  1154.3 137.9 %copy-start.186 = (bf16[16]{0:T(256)(128)(2,1)S(1)}, bf16[16]{0:T(256)(128)(2,1)}, u32[]{:S(2)}) copy-start(bf16[16]{0:T(256)(128)(2,1)} %get-tuple-element.75) | copy-start | bytes 100
  1154.3 137.9 %copy-start.187 = (bf16[16]{0:T(256)(128)(2,1)S(1)}, bf16[16]{0:T(256)(128)(2,1)}, u32[]{:S(2)}) copy-start(bf16[16]{0:T(256)(128)(2,1)} %get-tuple-element.76) | copy-start | bytes 100
  1154.3 137.9 %copy-start.188 = (bf16[16]{0:T(256)(128)(2,1)S(1)}, bf16[16]{0:T(256)(128)(2,1)}, u32[]{:S(2)}) copy-start(bf16[16]{0:T(256)(128)(2,1)} %get-tuple-element.77) | copy-start | bytes 100
  1154.3 137.9 %copy-start.189 = (bf16[16]{0:T(256)(128)(2,1)S(1)}, bf16[16]{0:T(256)(128)(2,1)}, u32[]{:S(2)}) copy-start(bf16[16]{0:T(256)(128)(2,1)} %get-tuple-element.78) | copy-start | bytes 100
  1298.8 18.5 %collective-permute-start.4 = (bf16[640,2048]{0,1:T(8,128)(2,1)}, bf16[640,2048]{0,1:T(8,128)(2,1)}, u32[]{:S(2)}, u32[]{:S(2)}) collective-permute-start(bf16[640,2048]{0,1:T(8,128)(2,1)} %select_convert_fusion), channel_id=1, source_target_pairs={{0,4},{4,0},{8,12},{12,8},{16,20},{20,16},{24,28},{28,24},{1,5},{5... | collective-permute-start | bytes 7864328 | tf_op jit(solution)/shard_map/ppermute | solution.py:664
  (186 other events, 2814.5 us)

commit v2 on v0

v2 whole, which is shorter than its diff:
```python
import functools
import math

import jax
import jax.numpy as jnp
from jax import lax
from jax.experimental import pallas as pl
from jax.experimental.pallas import tpu as pltpu
from jax.sharding import PartitionSpec as P

D = 1024
H = 16
DH = 64
C = 2048
KERNEL = 31
HALF = 15
NB = 32
EPS = 1e-05
LIMITS = (8, 12, 16, 24, 32, 48, 64, 96)
BOTH = ("batch", "frames")
SMALL = (16, 512)


MESH = pl.DeviceIdType.MESH
VMEM_BYTES = 58 * 1024 * 1024


def ring_spot(index, count):
    half = count // 2
    return index + (index // half) * (3 * half - 1 - 2 * index)


def places(chips, frames):
    batch, depth = lax.axis_index("batch"), lax.axis_index("frames")
    chip, core = batch // 2, lax.rem(batch, 2)
    spot = ring_spot(chip, chips)

    def chip_at(offset):
        return ring_spot(lax.rem(spot + offset + chips, chips), chips)

    return chip, core, depth, chip_at


def greet(chips, frames, partners):
    chip, core, depth, chip_at = places(chips, frames)
    barrier = pltpu.get_barrier_semaphore()
    for offset in (1, -1):
        pl.semaphore_signal(
            barrier, inc=1, device_id=(chip_at(offset) * 2 + core, depth), device_id_type=MESH
        )
    pl.semaphore_signal(
        barrier, inc=1, device_id=(chip * 2 + 1 - core, depth), device_id_type=MESH
    )

    @pl.when(depth > 0)
    def _():
        pl.semaphore_signal(barrier, inc=1, device_id=(chip * 2 + core, depth - 1), device_id_type=MESH)

    @pl.when(depth < frames - 1)
    def _():
        pl.semaphore_signal(barrier, inc=1, device_id=(chip * 2 + core, depth + 1), device_id_type=MESH)

    count = 3 + jnp.minimum(depth, 1) + jnp.minimum(frames - 1 - depth, 1)
    if partners:
        groups = frames // 2
        for place in range(groups):
            there, side = core * groups + place, depth // groups

            @pl.when(jnp.logical_or(there != depth, side != core))
            def _():
                pl.semaphore_signal(
                    barrier, inc=1, device_id=(chip * 2 + side, there), device_id_type=MESH
                )

        count = count + groups - (1 - jnp.abs(depth // groups - core))
    pl.semaphore_wait(barrier, count)


def swap_frames(chips, frames, sources, targets, send_sems, recv_sems, local_sem):
    chip, core, depth, chip_at = places(chips, frames)
    groups = frames // 2
    starts, ends = [], []
    for at, (source, target) in enumerate(zip(sources, targets)):
        for place in range(groups):
            there, side = core * groups + place, depth // groups
            mine = jnp.logical_and(there == depth, side == core)
            slot = lax.rem(depth, groups)
            remote = pltpu.make_async_remote_copy(
                src_ref=source.at[place],
                dst_ref=target.at[slot],
                send_sem=send_sems.at[at * groups + place],
                recv_sem=recv_sems.at[at * groups + slot],
                device_id=(chip * 2 + side, there),
                device_id_type=MESH,
            )
            arrival = pltpu.make_async_remote_copy(
                src_ref=source.at[place],
                dst_ref=target.at[place],
                send_sem=send_sems.at[at * groups + place],
                recv_sem=recv_sems.at[at * groups + place],
                device_id=(chip * 2 + side, there),
                device_id_type=MESH,
            )
            here = pltpu.make_async_copy(source.at[place], target.at[slot], local_sem.at[at])
            away = jnp.logical_not(mine)
            starts += [gated(away, remote.start), gated(mine, here.start)]
            ends += [
                gated(away, remote.wait_send),
                gated(away, arrival.wait_recv),
                gated(mine, here.wait),
            ]
    return starts, ends


def gated(condition, action):
    if condition is None:
        return action
    return lambda: pl.when(condition)(action)


class Mover:
    def __init__(self, spots, sizes, send_sems, recv_sems):
        self.chips, self.frames = sizes
        self.chip, self.core, self.depth, self.chip_at = spots
        self.send_sems, self.recv_sems = send_sems, recv_sems
        self.used = 0
        self.levels = [[] for _ in range(self.frames + self.chips // 2 + 1)]
        self.departures = []

    def copy(self, source, target, device, condition):
        at = self.used
        self.used += 1
        made = pltpu.make_async_remote_copy(
            src_ref=source,
            dst_ref=target,
            send_sem=self.send_sems.at[at],
            recv_sem=self.recv_sems.at[at],
            device_id=device,
            device_id_type=MESH,
        )
        self.departures.append(gated(condition, made.wait_send))
        return made

    def other_core(self):
        return (self.chip * 2 + 1 - self.core, self.depth)

    def group(self, offset):
        at = self.depth + offset
        if offset == 0:
            return at, None
        return jnp.clip(at, 0, self.frames - 1), jnp.logical_and(at >= 0, at < self.frames)

    def offsets(self, distance):
        return (0,) if distance == 0 else (-distance, distance)


class Gather(Mover):
    def __init__(self, spots, sizes, shard, whole, send_sems, recv_sems, local_sems):
        super().__init__(spots, sizes, send_sems, recv_sems)
        self.shard, self.whole = shard, whole
        self.local = pltpu.make_async_copy(
            shard, whole.at[self.chip, self.core, self.depth], local_sems.at[0]
        )
        self.levels[0].append(self.local.start)
        for distance in range(self.frames):
            self.spread(distance)
        self.levels[-1] += self.departures

    def spread(self, distance):
        chip, core, depth, half = self.chip, self.core, self.depth, self.chips // 2
        for offset in self.offsets(distance):
            held, valid = self.group(offset)
            block = self.whole.at[chip, core, held]
            source = block if distance else self.shard
            for way in (1, -1):
                if distance + 1 == self.frames or offset * way > 0:
                    continue
                into, there = self.group(way)
                condition = there if valid is None else jnp.logical_and(valid, there)
                made = self.copy(source, block, (chip * 2 + core, into), condition)
                self.levels[distance].append(gated(condition, made.start))
                comes = self.group(offset - way)[1]
                self.levels[distance + 1].insert(0, gated(comes, made.wait_recv))
            columns = self.shard.shape[1]
            for step in range(1, half + 1):
                level = distance + step - 1
                for side, way in enumerate((1, -1)):
                    part = slice(None)
                    if step == half:
                        part = pl.ds(side * columns // 2, columns // 2)
                    origin = self.chip_at(-way * (step - 1))
                    target = self.whole.at[origin, core, held, :, part]
                    start = self.shard.at[:, part] if distance == 0 and step == 1 else target
                    made = self.copy(start, target, (self.chip_at(way) * 2 + core, depth), valid)
                    self.levels[level].append(gated(valid, made.start))
                    self.levels[level + 1].append(gated(valid, made.wait_recv))
            if distance == 0:
                self.levels[half].append(self.local.wait)
            line = self.whole.at[:, core, held]
            pair = self.copy(line, line, self.other_core(), valid)
            self.levels[distance + half].append(gated(valid, pair.start))
            self.levels[-1].append(gated(valid, pair.wait_recv))


class Scatter(Mover):
    def __init__(
        self, spots, sizes, grads, out, total, stage, landings, send_sems, recv_sems, local_sems
    ):
        super().__init__(spots, sizes, send_sems, recv_sems)
        self.grads, self.out, self.total, self.stage = grads, out, total, stage
        self.landings = list(landings)
        self.local_sems = local_sems
        self.begins = []
        self.columns = out.shape[1]
        self.merges = 0
        for distance in reversed(range(self.frames)):
            self.collect(distance)
        self.levels[-1] += [self.finish] + self.departures

    def add(self, where, piece):
        total = self.total
        total[where] = (total[where].astype(jnp.float32) + piece.astype(jnp.float32)).astype(
            total.dtype
        )

    def merge(self, held, pair, load, stage):
        load.wait()
        pair.wait_recv()

        @pl.loop(0, self.chips)
        def _(chip):
            self.add((chip, held), stage[chip])

    def settle(self, made, where, landed):
        made.wait_recv()
        self.add(where, landed[...])

    def collect(self, distance):
        core, depth, half = self.core, self.depth, self.chips // 2
        first = self.frames - 1 - distance
        for offset in self.offsets(distance):
            held, valid = self.group(offset)
            pair = self.copy(
                self.grads.at[:, 1 - core, held], self.total.at[:, held], self.other_core(), valid
            )
            stage = self.stage.at[self.merges]
            load = pltpu.make_async_copy(
                self.grads.at[:, core, held], stage, self.local_sems.at[self.merges]
            )
            self.merges += 1
            self.begins += [gated(valid, pair.start), gated(valid, load.start)]
            self.levels[0].append(
                gated(valid, functools.partial(self.merge, held, pair, load, stage))
            )
            for step in range(1, half + 1):
                for side, way in enumerate((1, -1)):
                    part = slice(None)
                    if step == 1:
                        part = pl.ds(side * self.columns // 2, self.columns // 2)
                    reach = half - step + 1
                    goal = self.chip_at(way * reach)
                    landed = self.landings.pop(0)
                    made = self.copy(
                        self.total.at[goal, held, :, part],
                        landed,
                        (self.chip_at(way) * 2 + core, depth),
                        valid,
                    )
                    self.levels[step - 1 if step == 1 else first + step - 1].append(
                        gated(valid, made.start)
                    )
                    where = (self.chip_at(way * (reach - 1)), held, slice(None), part)
                    self.levels[first + step].append(
                        gated(valid, functools.partial(self.settle, made, where, landed))
                    )
            if distance == 0:
                continue
            way = 1 if offset > 0 else -1
            landed = self.landings.pop(0)
            made = self.copy(
                self.total.at[self.chip, held],
                landed,
                (self.chip * 2 + core, self.group(way)[0]),
                valid,
            )
            self.levels[first + half].append(gated(valid, made.start))
            before = self.group(-way)[1]
            goes, there = self.group(offset - way)
            comes = before if there is None else jnp.logical_and(before, there)
            where = (self.chip, goes, slice(None), slice(None))
            self.levels[first + half + 1].append(
                gated(comes, functools.partial(self.settle, made, where, landed))
            )

    def finish(self):
        self.out[...] = self.total[self.chip, self.depth].astype(self.out.dtype)


def landing_shapes(sizes, rows, columns):
    chips, frames = sizes
    shapes = []
    for distance in reversed(range(frames)):
        for _ in range(2 if distance else 1):
            shapes += [(rows, columns // 2)] * 2 + [(rows, columns)] * (2 * (chips // 2 - 1))
            if distance:
                shapes.append((rows, columns))
    return shapes


class Traffic:
    def __init__(self, sizes, identity, shards=(), grads=(), swapped=(), swap_at=0):
        self.sizes, self.identity = sizes, identity
        self.shards, self.grads, self.swapped = list(shards), list(grads), list(swapped)
        self.swap_at = swap_at
        self.active = bool(self.shards or self.grads or self.swapped)

    def operands(self):
        return self.shards + self.grads + self.swapped

    def in_specs(self):
        return [pl.BlockSpec(memory_space=pl.ANY)] * len(self.operands())

    def out_shapes(self):
        chips, frames = self.sizes
        return (
            [jax.ShapeDtypeStruct((chips, 2, frames) + s.shape, s.dtype) for s in self.shards]
            + [jax.ShapeDtypeStruct(g.shape[3:], jnp.float32) for g in self.grads]
            + [jax.ShapeDtypeStruct(s.shape, s.dtype) for s in self.swapped]
        )

    def out_specs(self):
        anywhere = pl.BlockSpec(memory_space=pl.ANY)
        return (
            [anywhere] * len(self.shards)
            + [pl.BlockSpec(memory_space=pltpu.VMEM)] * len(self.grads)
            + [anywhere] * len(self.swapped)
        )

    def scratch(self):
        if not self.active:
            return []
        chips, frames = self.sizes
        shapes = []
        for grad in self.grads:
            shard = grad.shape[3:]
            shapes += [
                pltpu.VMEM((chips, frames) + shard, grad.dtype),
                pltpu.VMEM((2 * frames - 1, chips) + shard, grad.dtype),
            ]
            shapes += [pltpu.VMEM(shape, grad.dtype) for shape in landing_shapes(self.sizes, *shard)]
        copies = (2 * frames - 1) * (3 + chips)
        arrays = max(len(self.shards) + len(self.grads), 1)
        swaps = max(len(self.swapped), 1)
        return shapes + [
            pltpu.SemaphoreType.DMA((arrays, copies)),
            pltpu.SemaphoreType.DMA((arrays, copies)),
            pltpu.SemaphoreType.DMA((arrays, 2 * frames - 1)),
            pltpu.SemaphoreType.DMA((swaps * (frames // 2),)),
            pltpu.SemaphoreType.DMA((swaps * (frames // 2),)),
            pltpu.SemaphoreType.DMA((swaps,)),
        ]

    def plan(self, ins, outs, scratch):
        if not self.active:
            return []
        chips, frames = self.sizes
        scratch = list(scratch)
        send_sems, recv_sems, local_sems, swap_send, swap_recv, swap_local = scratch[-6:]
        spots = places(chips, frames)
        gathers, scatters = len(self.shards), len(self.grads)
        parts, begins = [], []
        for at in range(gathers + scatters):
            sems = (send_sems.at[at], recv_sems.at[at], local_sems.at[at])
            if at < gathers:
                parts.append(Gather(spots, self.sizes, ins[at], outs[at], *sems))
                continue
            total, stage = scratch.pop(0), scratch.pop(0)
            many = len(landing_shapes(self.sizes, *outs[at].shape))
            landings = [scratch.pop(0) for _ in range(many)]
            parts.append(
                Scatter(spots, self.sizes, ins[at], outs[at], total, stage, landings, *sems)
            )
            begins += parts[-1].begins
        times = [[], []]
        if parts:
            times = [sum(level, []) for level in zip(*[part.levels for part in parts])]
        if self.swapped:
            starts, ends = swap_frames(
                chips, frames, ins[gathers + scatters :], outs[gathers + scatters :],
                swap_send, swap_recv, swap_local,
            )
            times[min(self.swap_at, len(times) - 1)] += starts
            times[-1] += ends
        times[0] = [functools.partial(greet, chips, frames, bool(self.swapped))] + begins + times[0]
        return times


def run_plan(times, step=None, steps=1):
    if step is None:
        for actions in times:
            for action in actions:
                action()
        return
    by_step = {}
    for at, actions in enumerate(times):
        by_step.setdefault(at * steps // len(times), []).extend(actions)
    for at, actions in by_step.items():

        def run(actions=actions):
            for action in actions:
                action()

        pl.when(step == at)(run)


def finish_plan(times):
    for action in times[-1]:
        action()


def traffic_kernel(traffic, *refs):
    count = len(traffic.operands())
    run_plan(traffic.plan(refs[:count], refs[count : 2 * count], refs[2 * count :]))


def move(traffic):
    return pl.pallas_call(
        functools.partial(traffic_kernel, traffic),
        out_shape=traffic.out_shapes(),
        in_specs=traffic.in_specs(),
        out_specs=traffic.out_specs(),
        scratch_shapes=traffic.scratch(),
        compiler_params=traffic_params(traffic),
    )(*traffic.operands())


def traffic_params(traffic):
    if not traffic.active:
        return pltpu.CompilerParams(vmem_limit_bytes=VMEM_BYTES)
    return pltpu.CompilerParams(
        collective_id=traffic.identity, has_side_effects=True, vmem_limit_bytes=VMEM_BYTES
    )


def layer_norm(values, norm_gain, norm_shift):
    centred = values - jnp.mean(values, axis=-1, keepdims=True)
    spread = jnp.mean(centred * centred, axis=-1, keepdims=True)
    return centred * lax.rsqrt(spread + EPS) * norm_gain + norm_shift


def bucket_of(relative):
    magnitude = jnp.abs(relative)
    above = jnp.zeros_like(relative)
    for threshold in LIMITS:
        above = above + (magnitude >= threshold).astype(jnp.int32)
    inner_bucket = jnp.where(magnitude < 8, magnitude, 7 + above)
    return inner_bucket + NB // 2 * (relative > 0).astype(jnp.int32)


def product(operand_a, operand_b):
    return jnp.dot(operand_a, operand_b, preferred_element_type=jnp.float32)


def weight_grad(operand_a, operand_b):
    return lax.dot_general(
        operand_a, operand_b, (((0,), (0,)), ((), ())), preferred_element_type=jnp.float32
    ).astype(jnp.bfloat16)


def back_product(operand_a, operand_b):
    return lax.dot_general(
        operand_a, operand_b, (((1,), (1,)), ((), ())), preferred_element_type=jnp.float32
    )


def gated_unit(paired):
    return paired[:, :C] * jax.nn.sigmoid(paired[:, C:])


def depth_post(depth_values, norm_gain, norm_shift):
    return jax.nn.silu(layer_norm(depth_values, norm_gain, norm_shift))


def norm_back(hidden, norm_gain, norm_shift, upstream):
    normed_unused, pull_back = jax.vjp(layer_norm, hidden, norm_gain, norm_shift)
    return pull_back(upstream)


TILE = 512
CHUNK = 64


def dot_nt(left, right):
    return lax.dot_general(left, right, (((1,), (1,)), ((), ())), preferred_element_type=jnp.float32)


def dot_nn(left, right):
    return lax.dot_general(left, right, (((1,), (0,)), ((), ())), preferred_element_type=jnp.float32)


def sigmoid(values):
    return 0.5 * jnp.tanh(0.5 * values) + 0.5


def norm_parts(values):
    centred = values - jnp.mean(values, axis=-1, keepdims=True)
    rstd = lax.rsqrt(jnp.mean(centred * centred, axis=-1, keepdims=True) + EPS)
    return centred * rstd, rstd


def norm_chunk(values, norms_ref, which):
    scaled, _ = norm_parts(values)
    return scaled * norms_ref[2 * which : 2 * which + 1, :] + norms_ref[2 * which + 1 : 2 * which + 2, :]


def chunks(rows):
    def each(body):
        @pl.loop(0, rows // CHUNK)
        def _(at):
            body(pl.ds(pl.multiple_of(at * CHUNK, CHUNK), CHUNK))

    return each


def ffn_kernel(traffic, hidden_ref, norms_ref, w_in_ref, w_out_ref, *refs):
    moved = len(traffic.operands())
    ins, refs = refs[:moved], refs[moved:]
    out_ref, inner_ref, normed_ref, next_ref = refs[:4]
    outs, refs = refs[4 : 4 + moved], refs[4 + moved :]
    total, refs = refs[0], refs[1:]
    step, steps = pl.program_id(0), pl.num_programs(0)
    run_plan(traffic.plan(ins, outs, refs), step, FFN_STEPS)
    each = chunks(hidden_ref.shape[0])

    @pl.when(step == 0)
    def _():
        def body(here):
            normed_ref[here, :] = norm_chunk(hidden_ref[here, :], norms_ref, 0).astype(jnp.bfloat16)
            total[here, :] = jnp.zeros((CHUNK, total.shape[1]), jnp.float32)

        each(body)

    inner = dot_nn(normed_ref[...], w_in_ref[...])
    inner_ref[...] = inner.astype(jnp.bfloat16)
    total[...] += dot_nn((inner * sigmoid(inner)).astype(jnp.bfloat16), w_out_ref[...])

    @pl.when(step == steps - 1)
    def _():
        def body(here):
            hidden = hidden_ref[here, :] + 0.5 * total[here, :]
            out_ref[here, :] = hidden
            next_ref[here, :] = norm_chunk(hidden, norms_ref, 1).astype(jnp.bfloat16)

        each(body)


FFN_STEPS = 8


def resident(shape):
    return pl.BlockSpec(shape, lambda step: (0,) * len(shape))


def ffn(hidden, norms, weight_in, weight_out, traffic):
    rows, width = hidden.shape
    tile = weight_in.shape[1] // FFN_STEPS
    return pl.pallas_call(
        functools.partial(ffn_kernel, traffic),
        grid=(FFN_STEPS,),
        out_shape=[
            jax.ShapeDtypeStruct((rows, width), jnp.float32),
            jax.ShapeDtypeStruct((rows, weight_in.shape[1]), jnp.bfloat16),
            jax.ShapeDtypeStruct((rows, width), jnp.bfloat16),
            jax.ShapeDtypeStruct((rows, width), jnp.bfloat16),
        ]
        + traffic.out_shapes(),
        in_specs=[
            resident((rows, width)),
            resident(norms.shape),
            pl.BlockSpec((width, tile), lambda step: (0, step)),
            pl.BlockSpec((tile, width), lambda step: (step, 0)),
        ]
        + traffic.in_specs(),
        out_specs=[
            resident((rows, width)),
            pl.BlockSpec((rows, tile), lambda step: (0, step)),
            resident((rows, width)),
            resident((rows, width)),
        ]
        + traffic.out_specs(),
        scratch_shapes=[pltpu.VMEM((rows, width), jnp.float32)] + traffic.scratch(),
        compiler_params=traffic_params(traffic),
    )(hidden, norms, weight_in, weight_out, *traffic.operands())


def ffn_back_kernel(
    traffic, hidden_ref, normed_ref, grad_ref, norms_ref, inner_ref, w_in_ref, w_out_ref, *refs
):
    moved = len(traffic.operands())
    ins, refs = refs[:moved], refs[moved:]
    out_ref, g_in_ref, g_out_ref, sums_ref = refs[:4]
    outs, refs = refs[4 : 4 + moved], refs[4 + moved :]
    (half_grad, turned, total), refs = refs[:3], refs[3:]
    step, steps = pl.program_id(0), pl.num_programs(0)
    run_plan(traffic.plan(ins, outs, refs), step, FFN_STEPS)
    each = chunks(hidden_ref.shape[0])

    @pl.when(step == 0)
    def _():
        def body(here):
            half_grad[here, :] = (0.5 * grad_ref[here, :]).astype(jnp.bfloat16)
            total[here, :] = jnp.zeros((CHUNK, total.shape[1]), jnp.float32)

        each(body)
        turned[...] = normed_ref[...].T
        sums_ref[...] = jnp.zeros_like(sums_ref)

    inner = inner_ref[...].astype(jnp.float32)
    gate = sigmoid(inner)
    active = (inner * gate).astype(jnp.bfloat16)
    g_out_ref[...] = dot_nn(active.T, half_grad[...]).astype(jnp.bfloat16)
    slope = gate * (1.0 + inner * (1.0 - gate))
    grad_inner = (dot_nt(half_grad[...], w_out_ref[...]) * slope).astype(jnp.bfloat16)
    g_in_ref[...] = dot_nn(turned[...], grad_inner).astype(jnp.bfloat16)
    total[...] += dot_nt(grad_inner, w_in_ref[...])

    @pl.when(step == steps - 1)
    def _():
        def body(here):
            scaled, rstd = norm_parts(hidden_ref[here, :])
            upstream = total[here, :]
            sums_ref[0:1, :] += jnp.sum(upstream * scaled, axis=0, keepdims=True)
            sums_ref[1:2, :] += jnp.sum(upstream, axis=0, keepdims=True)
            weighted = upstream * norms_ref[0:1, :]
            back = weighted - jnp.mean(weighted, axis=-1, keepdims=True)
            back = back - scaled * jnp.mean(weighted * scaled, axis=-1, keepdims=True)
            out_ref[here, :] = grad_ref[here, :] + rstd * back

        each(body)


def ffn_back(hidden, normed, grad, norms, inner, weight_in, weight_out, traffic):
    rows, width = hidden.shape
    tile = weight_in.shape[1] // FFN_STEPS
    return pl.pallas_call(
        functools.partial(ffn_back_kernel, traffic),
        grid=(FFN_STEPS,),
        out_shape=[
            jax.ShapeDtypeStruct((rows, width), jnp.float32),
            jax.ShapeDtypeStruct(weight_in.shape, jnp.bfloat16),
            jax.ShapeDtypeStruct(weight_out.shape, jnp.bfloat16),
            jax.ShapeDtypeStruct((8, width), jnp.float32),
        ]
        + traffic.out_shapes(),
        in_specs=[
            resident((rows, width)),
            resident((rows, width)),
            resident((rows, width)),
            resident(norms.shape),
            pl.BlockSpec((rows, tile), lambda step: (0, step)),
            pl.BlockSpec((width, tile), lambda step: (0, step)),
            pl.BlockSpec((tile, width), lambda step: (step, 0)),
        ]
        + traffic.in_specs(),
        out_specs=[
            resident((rows, width)),
            pl.BlockSpec((width, tile), lambda step: (0, step)),
            pl.BlockSpec((tile, width), lambda step: (step, 0)),
            resident((8, width)),
        ]
        + traffic.out_specs(),
        scratch_shapes=[
            pltpu.VMEM((rows, width), jnp.bfloat16),
            pltpu.VMEM((width, rows), jnp.bfloat16),
            pltpu.VMEM((rows, width), jnp.float32),
        ]
        + traffic.scratch(),
        compiler_params=traffic_params(traffic),
    )(hidden, normed, grad, norms, inner, weight_in, weight_out, *traffic.operands())


QB = 128
PAIRS = H // 2
BAND = 3 * QB


def stacked(block):
    lanes = lax.broadcasted_iota(jnp.int32, block.shape, 1)
    nothing = jnp.zeros_like(block)
    return jnp.concatenate(
        [jnp.where(lanes < DH, block, nothing), jnp.where(lanes >= DH, block, nothing)], axis=0
    )


def own_halves(both):
    channels = lax.broadcasted_iota(jnp.int32, (2 * DH, QB), 0)
    return jnp.where(channels < DH, both[:, :QB], both[:, QB:]).T


def offset_rows(table):
    offsets = (jnp.arange(4, dtype=jnp.int32)[:, None] - 1) * QB - jnp.arange(QB, dtype=jnp.int32)
    onehot = (jnp.arange(NB)[:, None, None] == bucket_of(offsets)[None]).astype(jnp.float32)
    rows = jnp.dot(table, onehot.reshape(NB, 4 * QB), precision=lax.Precision.HIGHEST)
    return rows.reshape(PAIRS, 8, QB)


def fill_strip(strip, rows_ref, length):
    far = length - 2 * QB
    rows_of = lax.broadcasted_iota(jnp.int32, (QB, QB), 0)
    lanes_of = lax.broadcasted_iota(jnp.int32, (QB, QB), 1)
    for head in range(2):
        columns = slice(head * QB, (head + 1) * QB)
        turned = []
        for at in range(4):
            row = jnp.broadcast_to(rows_ref[0, head * 4 + at : head * 4 + at + 1, :], (QB, QB))
            turned.append(pltpu.roll(row, 0, 1, stride=1, stride_axis=0))
        for tile in range(3):
            strip[far + tile * QB : far + (tile + 1) * QB, columns] = jnp.where(
                lanes_of >= rows_of, turned[tile], turned[tile + 1]
            )

        @pl.loop(0, far // QB)
        def _(at):
            before, after = pl.multiple_of(at * QB, QB), pl.multiple_of(far + BAND + at * QB, QB)
            strip[pl.ds(before, QB), columns] = turned[0]
            strip[pl.ds(after, QB), columns] = turned[3]


def strip_start(rows, length):
    first = lax.rem(lax.axis_index("batch"), 2) * rows + pl.program_id(1) * QB
    return pl.multiple_of(length - QB - first, QB), first


def attend_kernel(rows, length, traffic, rows_ref, q_ref, k_ref, v_ref, *refs):
    moved = len(traffic.operands())
    ins, refs = refs[:moved], refs[moved:]
    (out_ref, log_ref), refs = refs[:2], refs[2:]
    outs, refs = refs[:moved], refs[moved:]
    (strip, score, prob, vt), refs = refs[:4], refs[4:]
    blocks = rows // QB
    run_plan(
        traffic.plan(ins, outs, refs), pl.program_id(0) * blocks + pl.program_id(1), PAIRS * blocks
    )

    @pl.when(pl.program_id(1) == 0)
    def _():
        fill_strip(strip, rows_ref, length)
        vt[...] = v_ref[...].T

    start, _ = strip_start(rows, length)
    score[...] = dot_nt(k_ref[...], stacked(q_ref[...] * 0.125))

    def highest(at, most):
        here = pl.ds(pl.multiple_of(at * QB, QB), QB)
        values = score[here, :] + strip[pl.ds(pl.multiple_of(start + at * QB, QB), QB), :]
        score[here, :] = values
        return jnp.maximum(most, jnp.max(values.reshape(QB // 8, 8, 2 * QB), axis=0))

    most = lax.fori_loop(
        0, length // QB, highest, jnp.full((8, 2 * QB), -jnp.inf, jnp.float32), unroll=True
    )
    most = jnp.max(most, axis=0, keepdims=True)

    def weigh(at, total):
        here = pl.ds(pl.multiple_of(at * QB, QB), QB)
        values = jnp.exp(score[here, :] - most)
        prob[here, :] = values.astype(jnp.bfloat16)
        return total + jnp.sum(values.reshape(QB // 8, 8, 2 * QB), axis=0)

    total = lax.fori_loop(
        0, length // QB, weigh, jnp.zeros((8, 2 * QB), jnp.float32), unroll=True
    )
    total = jnp.sum(total, axis=0, keepdims=True)
    mixed = dot_nn(vt[...], prob[...]) / total
    out_ref[...] = own_halves(mixed).astype(out_ref.dtype)
    log_ref[0] = most + jnp.log(total)


def attend(queries, key_values, offsets, traffic):
    rows, length = queries.shape[0], key_values.shape[0]
    blocks = rows // QB
    return pl.pallas_call(
        functools.partial(attend_kernel, rows, length, traffic),
        grid=(PAIRS, blocks),
        out_shape=[
            jax.ShapeDtypeStruct((rows, D), jnp.bfloat16),
            jax.ShapeDtypeStruct((PAIRS * blocks, 1, 2 * QB), jnp.float32),
        ]
        + traffic.out_shapes(),
        in_specs=[
            pl.BlockSpec((1, 8, QB), lambda p, b: (p, 0, 0)),
            pl.BlockSpec((QB, 2 * DH), lambda p, b: (b, p)),
            pl.BlockSpec((length, 2 * DH), lambda p, b: (0, p)),
            pl.BlockSpec((length, 2 * DH), lambda p, b: (0, PAIRS + p)),
        ]
        + traffic.in_specs(),
        out_specs=[
            pl.BlockSpec((QB, 2 * DH), lambda p, b: (b, p)),
            pl.BlockSpec((1, 1, 2 * QB), lambda p, b: (p * blocks + b, 0, 0)),
        ]
        + traffic.out_specs(),
        scratch_shapes=[
            pltpu.VMEM((2 * length - QB, 2 * QB), jnp.float32),
            pltpu.VMEM((length, 2 * QB), jnp.float32),
            pltpu.VMEM((length, 2 * QB), jnp.bfloat16),
            pltpu.VMEM((2 * DH, length), jnp.bfloat16),
        ]
        + traffic.scratch(),
        compiler_params=traffic_params(traffic),
    )(offsets, queries, key_values, key_values, *traffic.operands())


def attend_back_kernel(
    rows, length, traffic, rows_ref, q_ref, k_ref, v_ref, g_ref, log_ref, *refs
):
    moved = len(traffic.operands())
    ins, refs = refs[:moved], refs[moved:]
    (dq_ref, dk_ref, dv_ref, near_ref, sums_ref), refs = refs[:5], refs[5:]
    outs, refs = refs[:moved], refs[moved:]
    (strip, score, slope, prob, change, kt, dk_sum, dv_sum, near), refs = refs[:9], refs[9:]
    block, blocks = pl.program_id(1), rows // QB
    run_plan(traffic.plan(ins, outs, refs), pl.program_id(0) * blocks + block, PAIRS * blocks)

    @pl.when(block == 0)
    def _():
        fill_strip(strip, rows_ref, length)
        kt[...] = k_ref[...].T
        dk_sum[...] = jnp.zeros_like(dk_sum)
        dv_sum[...] = jnp.zeros_like(dv_sum)
        near[...] = jnp.zeros_like(near)
        change[0:QB, :] = jnp.zeros((QB, 2 * QB), jnp.bfloat16)
        change[length + QB : length + 2 * QB, :] = jnp.zeros((QB, 2 * QB), jnp.bfloat16)

    start, first = strip_start(rows, length)
    q_both = stacked(q_ref[...] * 0.125)
    g_both = stacked(g_ref[...])
    score[...] = dot_nt(k_ref[...], q_both)
    slope[...] = dot_nt(v_ref[...], g_both)
    log_total = log_ref[0]

    def weigh(at, total):
        here = pl.ds(pl.multiple_of(at * QB, QB), QB)
        values = jnp.exp(
            score[here, :] + strip[pl.ds(pl.multiple_of(start + at * QB, QB), QB), :] - log_total
        )
        score[here, :] = values
        prob[here, :] = values.astype(jnp.bfloat16)
        return total + jnp.sum((values * slope[here, :]).reshape(QB // 8, 8, 2 * QB), axis=0)

    centre = lax.fori_loop(
        0, length // QB, weigh, jnp.zeros((8, 2 * QB), jnp.float32), unroll=True
    )
    centre = jnp.sum(centre, axis=0, keepdims=True)

    for at in range(length // QB):
        here = pl.ds(at * QB, QB)
        values = score[here, :] * (slope[here, :] - centre)
        change[pl.ds(at * QB + QB, QB), :] = values.astype(jnp.bfloat16)
        sums_ref[0, at : at + 1, :] = jnp.sum(values, axis=0, keepdims=True)

    dv_sum[...] += dot_nn(prob[...], g_both)
    moved = change[QB : QB + length, :]
    dk_sum[...] += dot_nn(moved, q_both)
    dq_ref[...] = (own_halves(dot_nn(kt[...], moved)) * 0.125).astype(dq_ref.dtype)
    near[...] += change[pl.ds(pl.multiple_of(first, QB), BAND), :].astype(jnp.float32)

    @pl.when(block == pl.num_programs(1) - 1)
    def _():
        dk_ref[...] = dk_sum[...].astype(dk_ref.dtype)
        dv_ref[...] = dv_sum[...].astype(dv_ref.dtype)
        rows_of = lax.broadcasted_iota(jnp.int32, (QB, QB), 0)
        lanes_of = lax.broadcasted_iota(jnp.int32, (QB, QB), 1)
        for head in range(2):
            for tile in range(3):
                turned = near[tile * QB : (tile + 1) * QB, head * QB : (head + 1) * QB]
                step = 1
                while step < QB:
                    turned = jnp.where(
                        lax.rem(rows_of // step, 2) == 1, pltpu.roll(turned, QB - step, 1), turned
                    )
                    step *= 2
                upper = jnp.where((lanes_of >= 1) & (lanes_of + rows_of < QB), turned, 0.0)
                for half, piece in enumerate((upper, turned - upper)):
                    at = head * 6 + tile * 2 + half
                    near_ref[0, at : at + 1, :] = jnp.sum(piece, axis=0, keepdims=True)


def attend_back(queries, key_values, offsets, log_total, grads, traffic):
    rows, length = queries.shape[0], key_values.shape[0]
    blocks = rows // QB
    big = (length, 2 * QB)
    return pl.pallas_call(
        functools.partial(attend_back_kernel, rows, length, traffic),
        grid=(PAIRS, blocks),
        out_shape=[
            jax.ShapeDtypeStruct((rows, D), jnp.bfloat16),
            jax.ShapeDtypeStruct((length, D), jnp.bfloat16),
            jax.ShapeDtypeStruct((length, D), jnp.bfloat16),
            jax.ShapeDtypeStruct((PAIRS, 12, QB), jnp.float32),
            jax.ShapeDtypeStruct((PAIRS * blocks, length // QB, 2 * QB), jnp.float32),
        ]
        + traffic.out_shapes(),
        in_specs=[
            pl.BlockSpec((1, 8, QB), lambda p, b: (p, 0, 0)),
            pl.BlockSpec((QB, 2 * DH), lambda p, b: (b, p)),
            pl.BlockSpec((length, 2 * DH), lambda p, b: (0, p)),
            pl.BlockSpec((length, 2 * DH), lambda p, b: (0, PAIRS + p)),
            pl.BlockSpec((QB, 2 * DH), lambda p, b: (b, p)),
            pl.BlockSpec((1, 1, 2 * QB), lambda p, b: (p * blocks + b, 0, 0)),
        ]
        + traffic.in_specs(),
        out_specs=[
            pl.BlockSpec((QB, 2 * DH), lambda p, b: (b, p)),
            pl.BlockSpec((length, 2 * DH), lambda p, b: (0, p)),
            pl.BlockSpec((length, 2 * DH), lambda p, b: (0, p)),
            pl.BlockSpec((1, 12, QB), lambda p, b: (p, 0, 0)),
            pl.BlockSpec((1, length // QB, 2 * QB), lambda p, b: (p * blocks + b, 0, 0)),
        ]
        + traffic.out_specs(),
        scratch_shapes=[
            pltpu.VMEM((2 * length - QB, 2 * QB), jnp.float32),
            pltpu.VMEM(big, jnp.float32),
            pltpu.VMEM(big, jnp.float32),
            pltpu.VMEM(big, jnp.bfloat16),
            pltpu.VMEM((length + 2 * QB, 2 * QB), jnp.bfloat16),
            pltpu.VMEM((2 * DH, length), jnp.bfloat16),
            pltpu.VMEM((length, 2 * DH), jnp.float32),
            pltpu.VMEM((length, 2 * DH), jnp.float32),
            pltpu.VMEM((BAND, 2 * QB), jnp.float32),
        ]
        + traffic.scratch(),
        compiler_params=traffic_params(traffic),
    )(offsets, queries, key_values, key_values, grads, log_total, *traffic.operands())


def table_back(near, sums, first_block):
    blocks = sums.shape[0] // PAIRS
    count = sums.shape[1]
    lane = jnp.arange(QB, dtype=jnp.int32)[None, None, :]
    tile = jnp.arange(3, dtype=jnp.int32)[:, None, None]
    half = jnp.arange(2, dtype=jnp.int32)[None, :, None]
    behind = jnp.where(half == 0, jnp.where(lane == 0, QB, lane), jnp.where(lane == 0, 0, lane - QB))
    offsets = (tile - 1) * QB - behind
    onehot = (bucket_of(offsets)[..., None] == jnp.arange(NB)).astype(jnp.float32)
    close = jnp.einsum(
        "zthl,thlb->zb",
        near.reshape(H, 3, 2, QB),
        onehot,
        precision=lax.Precision.HIGHEST,
    )
    by_block = sums.reshape(PAIRS, blocks, count, 2, QB).sum(axis=4)
    here = first_block + jnp.arange(blocks, dtype=jnp.int32)[:, None]
    there = jnp.arange(count, dtype=jnp.int32)[None, :]
    below = jnp.einsum(
        "pbch,bc->ph", by_block, (there < here - 1).astype(jnp.float32), precision=lax.Precision.HIGHEST
    ).reshape(H)
    above = jnp.einsum(
        "pbch,bc->ph", by_block, (there > here + 1).astype(jnp.float32), precision=lax.Precision.HIGHEST
    ).reshape(H)
    spread = jnp.arange(NB)[None, :]
    close = close + jnp.where(spread == NB // 2 - 1, below[:, None], 0.0)
    return close + jnp.where(spread == NB - 1, above[:, None], 0.0)


EDGE = 16
LANES = 128
BLOCK = 128


def shifted_rows(window):
    for low in range(8):
        turned = pltpu.roll(window, window.shape[0] - low, 0) if low else window
        for high in range(4):
            offset = 8 * high + low
            if 1 <= offset <= KERNEL:
                yield offset, turned[8 * high : 8 * high + BLOCK, :]


def conv_kernel(traffic, padded_ref, taps_ref, norms_ref, *refs):
    moved = len(traffic.operands())
    ins, refs = refs[:moved], refs[moved:]
    (depth_ref, post_ref), refs = refs[:2], refs[2:]
    outs, refs = refs[:moved], refs[moved:]
    step = pl.program_id(0)
    run_plan(traffic.plan(ins, outs, refs), step, CONV_BLOCKS)
    first = pl.multiple_of(step * BLOCK, BLOCK)

    @pl.loop(0, C // LANES)
    def _(at):
        lanes = pl.ds(pl.multiple_of(at * LANES, LANES), LANES)
        window = padded_ref[pl.ds(first, BLOCK + 2 * EDGE), lanes].astype(jnp.float32)
        total = jnp.zeros((BLOCK, LANES), jnp.float32)
        for offset, rows in shifted_rows(window):
            total = total + rows * taps_ref[offset - 1 : offset, lanes]
        depth_ref[:, lanes] = total

    @pl.loop(0, BLOCK // 16)
    def _(at):
        here = pl.ds(pl.multiple_of(at * 16, 16), 16)
        scaled, _ = norm_parts(depth_ref[here, :])
        normed = scaled * norms_ref[0:1, :] + norms_ref[1:2, :]
        post_ref[here, :] = (normed * sigmoid(normed)).astype(jnp.bfloat16)


CONV_BLOCKS = 5


def convolve(padded, taps, norms, traffic):
    rows = padded.shape[0] - 2 * EDGE
    return pl.pallas_call(
        functools.partial(conv_kernel, traffic),
        grid=(CONV_BLOCKS,),
        out_shape=[
            jax.ShapeDtypeStruct((rows, C), jnp.float32),
            jax.ShapeDtypeStruct((rows, C), jnp.bfloat16),
        ]
        + traffic.out_shapes(),
        in_specs=[resident(padded.shape), resident(taps.shape), resident(norms.shape)]
        + traffic.in_specs(),
        out_specs=[
            pl.BlockSpec((BLOCK, C), lambda step: (step, 0)),
            pl.BlockSpec((BLOCK, C), lambda step: (step, 0)),
        ]
        + traffic.out_specs(),
        scratch_shapes=traffic.scratch(),
        compiler_params=traffic_params(traffic),
    )(padded, taps, norms, *traffic.operands())


def conv_back_kernel(traffic, change_ref, gated_ref, first_ref, second_ref, taps_ref, *refs):
    moved = len(traffic.operands())
    ins, refs = refs[:moved], refs[moved:]
    (g_first_ref, g_second_ref, g_taps_ref), refs = refs[:3], refs[3:]
    outs, refs = refs[:moved], refs[moved:]
    sums, refs = refs[0], refs[1:]
    run_plan(traffic.plan(ins, outs, refs), pl.program_id(0), C // LANES)
    sums[...] = jnp.zeros_like(sums)

    @pl.loop(0, CONV_BLOCKS)
    def _(block):
        first = pl.multiple_of(block * BLOCK, BLOCK)
        here = pl.ds(first, BLOCK)
        around = pl.ds(first, BLOCK + 2 * EDGE)
        window = change_ref[around, :].astype(jnp.float32)
        total = jnp.zeros((BLOCK, LANES), jnp.float32)
        for offset, rows in shifted_rows(window):
            total = total + rows * taps_ref[KERNEL - offset : KERNEL - offset + 1, :]
        gate = sigmoid(second_ref[here, :].astype(jnp.float32))
        through = total * gate
        g_first_ref[here, :] = through.astype(jnp.bfloat16)
        g_second_ref[here, :] = (
            through * first_ref[here, :].astype(jnp.float32) * (1.0 - gate)
        ).astype(jnp.bfloat16)

        change = change_ref[pl.ds(pl.multiple_of(first + EDGE, EDGE), BLOCK), :].astype(jnp.float32)
        window = gated_ref[around, :].astype(jnp.float32)
        for offset, rows in shifted_rows(window):
            part = jnp.sum((rows * change).reshape(BLOCK // 8, 8, LANES), axis=0)
            sums[8 * (offset - 1) : 8 * offset, :] += part

    for tap in range(KERNEL):
        g_taps_ref[tap : tap + 1, :] = jnp.sum(sums[8 * tap : 8 * tap + 8, :], axis=0, keepdims=True)


def convolve_back(change, gated, paired, taps, traffic):
    rows = change.shape[0] - 2 * EDGE
    half = C // LANES
    column = pl.BlockSpec((rows, LANES), lambda step: (0, step))
    edged = pl.BlockSpec((rows + 2 * EDGE, LANES), lambda step: (0, step))
    return pl.pallas_call(
        functools.partial(conv_back_kernel, traffic),
        grid=(half,),
        out_shape=[
            jax.ShapeDtypeStruct((rows, C), jnp.bfloat16),
            jax.ShapeDtypeStruct((rows, C), jnp.bfloat16),
            jax.ShapeDtypeStruct((KERNEL + 1, C), jnp.float32),
        ]
        + traffic.out_shapes(),
        in_specs=[
            edged,
            edged,
            column,
            pl.BlockSpec((rows, LANES), lambda step: (0, half + step)),
            pl.BlockSpec((KERNEL + 1, LANES), lambda step: (0, step)),
        ]
        + traffic.in_specs(),
        out_specs=[column, column, pl.BlockSpec((KERNEL + 1, LANES), lambda step: (0, step))]
        + traffic.out_specs(),
        scratch_shapes=[pltpu.VMEM((8 * KERNEL, LANES), jnp.float32)] + traffic.scratch(),
        compiler_params=traffic_params(traffic),
    )(change, gated, paired, paired, taps, *traffic.operands())


def as_shard(array):
    rows = array.shape[0]
    return array if rows % 16 == 0 else array.reshape(16, rows * array.shape[1] // 16)


def as_weight(whole, like):
    devices = math.prod(whole.shape[:3])
    return whole.reshape(devices * like.shape[0], like.shape[1])


def as_parts(grad, sizes, like):
    chips, frames = sizes
    shard = as_shard(jnp.zeros(like.shape, jnp.bfloat16)).shape
    return grad.reshape((chips, 2, frames) + shard)


def pack_small(values, small_shapes):
    flat = jnp.concatenate([value.reshape(-1) for value in values])
    return jnp.pad(flat, (0, SMALL[0] * SMALL[1] - flat.shape[0])).reshape(SMALL)


def unpack_small(packed, shapes):
    devices = packed.shape[0]
    at, out = 0, []
    for shape in shapes:
        size = math.prod(shape)
        piece = packed[:, at : at + size].reshape((devices,) + shape)
        at += size
        piece = jnp.moveaxis(piece, 0, -2)
        out.append(piece.reshape(shape[:-1] + (devices * shape[-1],)))
    return out


def repack_small(values, shapes, devices):
    pieces = []
    for value, shape in zip(values, shapes):
        piece = value.reshape(shape[:-1] + (devices, shape[-1]))
        pieces.append(jnp.moveaxis(piece, -2, 0).reshape(devices, -1))
    flat = jnp.concatenate(pieces, axis=1)
    return jnp.pad(flat, ((0, 0), (0, SMALL[0] * SMALL[1] - flat.shape[1])))


def shards(
    frames_in,
    positions,
    mask_vector,
    norm_gains,
    norm_biases,
    depth_gain,
    depth_bias,
    early_in,
    early_out,
    qkv_weight,
    mixer_out,
    pointwise_in,
    pointwise_out,
    depth_kernel,
    late_in,
    late_out,
    position_bias,
    cotangent,
):
    groups, run, model_width = frames_in.shape
    line = lax.axis_size("frames")
    chips = lax.axis_size("batch") // 2
    sizes = (chips, line)
    devices = 2 * chips * line
    length = run * line
    rows = groups * run
    batch, depth = lax.axis_index("batch"), lax.axis_index("frames")
    core = lax.rem(batch, 2)
    first_frame = core * rows
    partner = [(at, at + 1 - 2 * (at % 2)) for at in range(2 * chips)]

    def from_other(array):
        return lax.ppermute(array, "batch", partner)

    big = [early_in, early_out, qkv_weight, mixer_out, pointwise_in, pointwise_out, late_in, late_out]
    small = [mask_vector, norm_gains, norm_biases, depth_gain, depth_bias, depth_kernel, position_bias]
    small_shapes = [value.shape for value in small]
    small_size = sum(math.prod(shape) for shape in small_shapes)
    shard_of = [as_shard(value) for value in big]
    gathered = move(
        Traffic(
            sizes,
            0,
            shards=shard_of[:2] + [pack_small(small, small_shapes)],
            swapped=[frames_in],
            swap_at=2,
        )
    )
    w_early_in, w_early_out = as_weight(gathered[0], early_in), as_weight(gathered[1], early_out)
    small_whole = gathered[2].reshape(devices, SMALL[0] * SMALL[1])
    mask_full, gains, biases, channel_gain, channel_bias, kernel_full, table = [
        value.astype(jnp.float32) for value in unpack_small(small_whole, small_shapes)
    ]
    table = table.reshape(H, NB)
    frames_here = gathered[3].reshape(rows, D)

    both = jnp.where(core == 0, 0, 1)
    other_positions = from_other(positions)
    owner = depth // groups
    listed = jnp.where(owner == both, positions, other_positions)
    listed = lax.dynamic_index_in_dim(listed, lax.rem(depth, groups), 0, keepdims=False)
    frame_ids = first_frame + jnp.arange(rows, dtype=jnp.int32)
    masked = jnp.any(listed[:, None] == frame_ids[None, :], axis=0).reshape(rows, 1)

    offsets = offset_rows(table)

    def norms_of(*which):
        rows_of = [row for at in which for row in (gains[at], biases[at])]
        return jnp.stack(rows_of + [jnp.zeros((D,), jnp.float32)] * (8 - len(rows_of)))

    def parts(grad, like):
        return as_parts(grad, sizes, like)

    def in_order(mine, other):
        return jnp.where(
            core == 0,
            jnp.concatenate([mine, other], axis=0),
            jnp.concatenate([other, mine], axis=0),
        )

    def halves(whole):
        first, second = whole[:rows], whole[rows:]
        return jnp.where(core == 0, first, second), jnp.where(core == 0, second, first)

    hidden0 = jnp.where(masked, mask_full[None, :], frames_here.astype(jnp.float32))
    hidden1, inner1, normed1, normed2, *gathered = ffn(
        hidden0, norms_of(0, 1), w_early_in, w_early_out, Traffic(sizes, 1, shards=shard_of[2:4])
    )
    w_qkv, w_mixer = as_weight(gathered[0], qkv_weight), as_weight(gathered[1], mixer_out)
    packed = product(normed2, w_qkv).astype(jnp.bfloat16)
    key_values = in_order(packed[:, D:], from_other(packed[:, D:]))
    mixed_rows, log_total, *gathered = attend(
        packed, key_values, offsets, Traffic(sizes, 2, shards=shard_of[4:6], swapped=[cotangent], swap_at=3)
    )
    w_point_in = as_weight(gathered[0], pointwise_in)
    w_point_out = as_weight(gathered[1], pointwise_out)
    upstream = gathered[2].reshape(rows, D).astype(jnp.float32)
    hidden2 = hidden1 + product(mixed_rows, w_mixer)

    normed3 = layer_norm(hidden2, gains[2], biases[2]).astype(jnp.bfloat16)
    paired = product(normed3, w_point_in).astype(jnp.bfloat16)
    gated = gated_unit(paired.astype(jnp.float32)).astype(jnp.bfloat16)

    def with_edges(array):
        sent = jnp.where(core == 0, array[rows - EDGE :], array[:EDGE])
        edge = from_other(sent)
        nothing = jnp.zeros_like(edge)
        return jnp.concatenate(
            [jnp.where(core == 0, nothing, edge), array, jnp.where(core == 0, edge, nothing)], axis=0
        )

    padded = with_edges(gated)
    taps = jnp.pad(kernel_full, ((0, 1), (0, 0)))
    channel_norms = jnp.pad(jnp.stack([channel_gain, channel_bias]), ((0, 6), (0, 0)))
    depth_values, post, *gathered = convolve(
        padded, taps, channel_norms, Traffic(sizes, 3, shards=shard_of[6:])
    )
    w_late_in, w_late_out = as_weight(gathered[0], late_in), as_weight(gathered[1], late_out)
    hidden3 = hidden2 + product(post, w_point_out)
    hidden4, inner5, normed5, activations = ffn(
        hidden3, norms_of(3, 4), w_late_in, w_late_out, Traffic(sizes, None)
    )

    grad4, gain_grad4, bias_grad4 = norm_back(hidden4, gains[4], biases[4], upstream)
    grad3, late_in_grad, late_out_grad, norm_sums3 = ffn_back(
        hidden3, normed5, grad4, norms_of(3), inner5, w_late_in, w_late_out, Traffic(sizes, None)
    )
    grad_out3 = grad3.astype(jnp.bfloat16)
    pointwise_out_grad = weight_grad(post, grad_out3)
    grad_post = back_product(grad_out3, w_point_out)
    post_unused, post_pull = jax.vjp(depth_post, depth_values, channel_gain, channel_bias)
    grad_depth, channel_gain_grad, channel_bias_grad = post_pull(grad_post)
    grad_depth_low = grad_depth.astype(jnp.bfloat16)
    grad_first, grad_second, taps_grad, *sums_late = convolve_back(
        with_edges(grad_depth_low),
        padded,
        paired,
        taps,
        Traffic(
            sizes, 4, grads=[parts(late_out_grad, late_out), parts(late_in_grad, late_in)]
        ),
    )
    kernel_grad = taps_grad[:KERNEL]
    grad_paired = jnp.concatenate([grad_first, grad_second], axis=1)
    pointwise_in_grad = weight_grad(normed3, grad_paired)
    grad_normed3 = back_product(grad_paired, w_point_in)
    grad_in3, gain_grad2, bias_grad2 = norm_back(hidden2, gains[2], biases[2], grad_normed3)
    grad2 = grad3 + grad_in3

    grad_out2 = grad2.astype(jnp.bfloat16)
    mixer_out_grad = weight_grad(mixed_rows, grad_out2)
    grad_mixed = back_product(grad_out2, w_mixer).astype(jnp.bfloat16)
    grad_queries, grad_keys, grad_values, near, far_sums, *sums_depth = attend_back(
        packed,
        key_values,
        offsets,
        log_total,
        grad_mixed,
        Traffic(
            sizes,
            5,
            grads=[parts(pointwise_out_grad, pointwise_out), parts(pointwise_in_grad, pointwise_in)],
            swapped=[activations.reshape(groups, run, D)],
        ),
    )
    table_grad = table_back(near, far_sums, core * (rows // QB)).reshape(H * NB)
    keys_own, keys_other = halves(grad_keys)
    values_own, values_other = halves(grad_values)
    keys_there, values_there = from_other(keys_other), from_other(values_other)
    grad_packed = jnp.concatenate(
        [
            grad_queries,
            (keys_own.astype(jnp.float32) + keys_there.astype(jnp.float32)).astype(jnp.bfloat16),
            (values_own.astype(jnp.float32) + values_there.astype(jnp.float32)).astype(jnp.bfloat16),
        ],
        axis=-1,
    )
    qkv_grad = weight_grad(normed2, grad_packed)
    grad_normed2 = back_product(grad_packed, w_qkv)
    grad_in2, gain_grad1, bias_grad1 = norm_back(hidden1, gains[1], biases[1], grad_normed2)
    grad1 = grad2 + grad_in2
    grad0, early_in_grad, early_out_grad, norm_sums0, *sums_mixer = ffn_back(
        hidden0,
        normed1,
        grad1,
        norms_of(0),
        inner1,
        w_early_in,
        w_early_out,
        Traffic(sizes, 6, grads=[parts(mixer_out_grad, mixer_out), parts(qkv_grad, qkv_weight)]),
    )
    grad_frames = jnp.where(masked, 0.0, grad0).astype(jnp.bfloat16)
    mask_grad = jnp.sum(jnp.where(masked, grad0, 0.0), axis=0)
    gain_stack = jnp.stack([norm_sums0[0], gain_grad1, gain_grad2, norm_sums3[0], gain_grad4])
    bias_stack = jnp.stack([norm_sums0[1], bias_grad1, bias_grad2, norm_sums3[1], bias_grad4])
    small_grads = repack_small(
        [mask_grad, gain_stack, bias_stack, channel_gain_grad, channel_bias_grad, kernel_grad, table_grad],
        small_shapes,
        devices,
    ).astype(jnp.bfloat16)

    sums_early = move(
        Traffic(
            sizes,
            7,
            grads=[
                parts(early_out_grad, early_out),
                parts(early_in_grad, early_in),
                small_grads.reshape((chips, 2, line) + SMALL),
            ],
            swapped=[grad_frames.reshape(groups, run, D)],
        )
    )
    small_sums = sums_early[2].reshape(-1)[:small_size]
    small_out, at = [], 0
    for shape in small_shapes:
        size = math.prod(shape)
        small_out.append(small_sums[at : at + size].reshape(shape))
        at += size
    return (
        sums_depth[2],
        sums_early[3].astype(jnp.float32),
        small_out[0],
        small_out[1],
        small_out[2],
        small_out[3],
        small_out[4],
        sums_early[1].reshape(early_in.shape),
        sums_early[0].reshape(early_out.shape),
        sums_mixer[1].reshape(qkv_weight.shape),
        sums_mixer[0].reshape(mixer_out.shape),
        sums_depth[1].reshape(pointwise_in.shape),
        sums_depth[0].reshape(pointwise_out.shape),
        small_out[5],
        sums_late[1].reshape(late_in.shape),
        sums_late[0].reshape(late_out.shape),
        small_out[6],
    )


def solution(mesh):
    in_specs = (
        P("batch", "frames", None),
        P("batch", None),
        P(("batch", "frames")),
        P(None, ("batch", "frames")),
        P(None, ("batch", "frames")),
        P(("batch", "frames")),
        P(("batch", "frames")),
        P(("batch", "frames"), None),
        P(("batch", "frames"), None),
        P(("batch", "frames"), None),
        P(("batch", "frames"), None),
        P(("batch", "frames"), None),
        P(("batch", "frames"), None),
        P(None, ("batch", "frames")),
        P(("batch", "frames"), None),
        P(("batch", "frames"), None),
        P(("batch", "frames")),
        P("batch", "frames", None),
    )
    out_specs = (
        P("batch", "frames", None),
        P("batch", "frames", None),
        P(("batch", "frames")),
        P(None, ("batch", "frames")),
        P(None, ("batch", "frames")),
        P(("batch", "frames")),
        P(("batch", "frames")),
        P(("batch", "frames"), None),
        P(("batch", "frames"), None),
        P(("batch", "frames"), None),
        P(("batch", "frames"), None),
        P(("batch", "frames"), None),
        P(("batch", "frames"), None),
        P(None, ("batch", "frames")),
        P(("batch", "frames"), None),
        P(("batch", "frames"), None),
        P(("batch", "frames")),
    )
    return jax.shard_map(shards, mesh=mesh, in_specs=in_specs, out_specs=out_specs, check_vma=False)
```

time: 4140 us -> 912 us (0.22)
  waiting for transfers between devices: 2670 us -> 0.53 us
  Pallas kernels: 0 us -> 715 us
  local copies, waits for them, and re-layouts: 432 us -> 46.9 us
  matrix products: 440 us -> 79.3 us
  blocking collectives: 289 us -> 0 us
  other arithmetic: 269 us -> 57.1 us
    reduce_scatter x9 -> x0, waiting for transfers between devices: 2470 us -> none  [the longest x1 366 us: shards(): lax.psum_scatter(early_out_grad, ('batch', 'frames'), scatter_dimension=0...]
    pallas_call x0 -> x10, Pallas kernels: none -> 715 us  [the longest x2 165 us: move(): pl.pallas_call(functools.partial(traffic_kernel, traffic), out_shape=traf...]
    all_gather x3 -> x0, blocking collectives: 204 us -> none  [the longest x1 71.2 us: fetch_early(): lax.all_gather(depth_kernel, ('batch', 'frames'), axis=1, tiled=True)]
    dot_general x16 -> x4, matrix products: 189 us -> 2.6 us  [the longest x1 0.9 us: table_back(): jnp.einsum('zthl,thlb->zb', near.reshape(H, 3, 2, QB), onehot, precision=...]
    reshape x5 -> x17, local copies, waits for them, and re-layouts: 136 us -> 7.24 us  [the longest x3 2.31 us: pack_small(): flat = jnp.concatenate([value.reshape(-1) for value in values])]
    all_gather x9 -> x0, waiting for transfers between devices: 118 us -> none  [the longest x1 67.4 us: fetch_late(): lax.all_gather(late_out, ('batch', 'frames'), axis=0, tiled=True)]
    add x6 -> x2, other arithmetic: 111 us -> 0.01 us  [the longest x1 0.01 us: table_back(): here + 1]
    unnamed x2 -> x0, blocking collectives: 84.3 us -> none
  transfers between devices with their start and end apart: 25 -> 6, of which waited for: 16 -> 1; matrix products, arithmetic and copies ran while one was open for 17% -> 5% of each run, Pallas kernels for 0% -> 9%
where the time goes in v2:
time: 912 us; the launch traced here: 905 us
  Pallas kernels  715 us (78%)
  matrix products  79.3 us (9%)
  other arithmetic  57.1 us (6%)
  local copies, waits for them, and re-layouts  46.9 us (5%)
    pallas_call x2, Pallas kernels, move(): pl.pallas_call(functools.partial(traffic_kernel, traffic), out_shape=traf...  165 us
    pallas_call x2, Pallas kernels, ffn_back(): pl.pallas_call(functools.partial(ffn_back_kernel, traffic), grid=(FFN_STE...  107 us
    pallas_call x1, Pallas kernels, attend_back(): pl.pallas_call(functools.partial(attend_back_kernel, rows, length, traffi...  99.1 us
    pallas_call x1, Pallas kernels, convolve(): pl.pallas_call(functools.partial(conv_kernel, traffic), grid=(CONV_BLOCKS...  93.5 us
    pallas_call x1, Pallas kernels, convolve_back(): pl.pallas_call(functools.partial(conv_back_kernel, traffic), grid=(half,)...  92.7 us
    pallas_call x2, Pallas kernels, ffn(): pl.pallas_call(functools.partial(ffn_kernel, traffic), grid=(FFN_STEPS,),...  79.5 us
    pallas_call x1, Pallas kernels, attend(): pl.pallas_call(functools.partial(attend_kernel, rows, length, traffic), g...  78.5 us
    dot_general x4, matrix products, weight_grad(): lax.dot_general(operand_a, operand_b, (((0,), (0,)), ((), ())), preferred...  27.4 us
  transfers between devices with their start and end apart: 6, of which 1 were waited for; matrix products, arithmetic and copies ran while one was open for 5% of the time, Pallas kernels for 9%

profile of v2, /device:TPU:0, one launch (start us, length us, event | category | flops | bytes accessed | tf_op | source)
XLA Modules:
  0.0 904.7 jit_solution(6582918561415701149)
XLA Ops:
  3.5 2.8 concatenate.29
  6.9 80.8 %shard_map.305 = (bf16[4,2,4,32,4096]{4,3,2,1,0:T(8,128)(2,1)}, bf16[4,2,4,128,1024]{4,3,2,1,0:T(8,128)(2,1)}, bf16[4,2,4,16,512]{4,3,2,1,0:T(8,128)(2,1)}, bf16[2,320,1024]{2,1,0:T(8,128)(2,1)}) custom-call(bf16[32,4096]{1,0:T(8,128)(2,1)} %refs_0_.4, bf16[128,1024]{1,0:T(8,128)(2,1)} %refs_1_.4, bf16[16,512]{1,0:T(8,128)(2,1)} %reshape.686.refs_2_, ...), custom_call_target="tpu_custom_call" | custom-call | tf_op jit(solution)/shard_map/pallas_call | solution.py:427
  93.3 56.7 %shard_map.306 = (f32[640,1024]{1,0:T(8,128)}, bf16[640,4096]{1,0:T(8,128)(2,1)}, bf16[640,1024]{1,0:T(8,128)(2,1)}, bf16[640,1024]{1,0:T(8,128)(2,1)}, bf16[4,2...) custom-call(f32[640,1024]{1,0:T(8,128)} %convert_select_fusion.hidden_ref, f32[8,1024]{1,0:T(8,128)} %stack.50.norms_ref, ...), custom_call_target="tpu_custom_call" | custom-call | tf_op jit(solution)/shard_map/pallas_call | solution.py:567
  150.0 7.4 convolution_convert_fusion.3.q_ref
  169.8 7.3 maximum_select_fusion.k_ref.v_ref
  177.1 78.5 %shard_map.307 = (bf16[640,1024]{1,0:T(8,128)(2,1)}, f32[40,1,256]{2,1,0:T(1,128)}, bf16[4,2,4,32,4096]{4,3,2,1,0:T(8,128)(2,1)}, bf16[4,2,4,64,1024]{4,3,2,1,0:T(8,128)(2,1)}, bf16[2,320,1024]{2,1,0:T(8,128)(2,1)}) custom-call(f32[8,8,128]{2,1,0:T(8,128)} %reshape.689.rows_ref, bf16[640,3072]{1,0:T(8,128)(2,1)} %copy-done.2, ...), custom_call_target="tpu_custom_call" | custom-call | tf_op jit(solution)/shard_map/pallas_call | solution.py:782
  255.7 3.1 fusion.62
  259.4 7.5 fusion.63
  273.3 93.5 %shard_map.308 = (f32[640,2048]{1,0:T(8,128)}, bf16[640,2048]{1,0:T(8,128)(2,1)}, bf16[4,2,4,32,4096]{4,3,2,1,0:T(8,128)(2,1)}, bf16[4,2,4,128,1024]{4,3,2,1,0:T(8,128)(2,1)}) custom-call(bf16[672,2048]{1,0:T(8,128)(2,1)} %pad_maximum_fusion.1.padded_ref.gated_ref, f32[32,2048]{1,0:T(8,128)} %pad_convert_fusion.taps_ref, f32[8,2048]{1,0:T(8,128)} %fusion.28.norms_ref, ...), custom_call_target="tpu_custom_call" | custom-call | tf_op jit(solution)/shard_map/pallas_call | solution.py:1010
  366.8 2.8 reduce_sum.238
  369.6 3.3 multiply_reduce_fusion.2
  373.7 6.5 convolution_add_fusion.hidden_ref
  380.2 22.9 %shard_map.309 = (f32[640,1024]{1,0:T(8,128)}, bf16[640,4096]{1,0:T(8,128)(2,1)}, bf16[640,1024]{1,0:T(8,128)(2,1)}, bf16[640,1024]{1,0:T(8,128)(2,1)}) custom-call(f32[640,1024]{1,0:T(8,128)} %convolution_add_fusion.hidden_ref, f32[8,1024]{1,0:T(8,128)} %stack.52.norms_ref, bf16[1024,4096]{1,0:T(8,128)(2,1)} %bitcast.109, bf16[4096,1024]{1,0:T(8,128)(2,1)} %bitcast.111), custom_call_target="tpu_custom_call" | custom-call | tf_op jit(solution)/shard_map/pallas_call | solution.py:567
  409.4 2.3 broadcast_add_fusion.grad_ref
  411.7 36.8 %shard_map.310 = (f32[640,1024]{1,0:T(8,128)}, bf16[1024,4096]{1,0:T(8,128)(2,1)}, bf16[4096,1024]{1,0:T(8,128)(2,1)}, f32[8,1024]{1,0:T(8,128)}) custom-call(f32[640,1024]{1,0:T(8,128)} %convolution_add_fusion.hidden_ref, bf16[640,1024]{1,0:T(8,128)(2,1)} %get-tuple-element.81.normed_ref, f32[640,1024]{1,0:T(8,128)} %broadcast_add_fusion.grad_ref, ...), custom_call_target="tpu_custom_call" | custom-call | tf_op jit(solution)/shard_map/pallas_call | solution.py:645
  448.5 8.7 multiply_reduce_fusion
  461.3 5.1 convolution_convert_fusion.4
  468.3 92.7 %shard_map.311 = (bf16[640,2048]{1,0:T(8,128)(2,1)}, bf16[640,2048]{1,0:T(8,128)(2,1)}, f32[32,2048]{1,0:T(8,128)}, f32[128,1024]{1,0:T(8,128)}, f32[32,4096]{1,0:T(8,128)}) custom-call(bf16[672,2048]{1,0:T(8,128)(2,1)} %pad_maximum_fusion.2.change_ref, bf16[672,2048]{1,0:T(8,128)(2,1)} %pad_maximum_fusion.1.padded_ref.gated_ref, ...), custom_call_target="tpu_custom_call" | custom-call | tf_op jit(solution)/shard_map/pallas_call | solution.py:1070
  561.1 2.2 constant_dynamic-update-slice_fusion.1
  565.3 8.7 multiply_reduce_fusion.3
  574.0 9.8 %convolution_convert_fusion = bf16[1024,4096]{1,0:T(8,128)(2,1)} fusion(bf16[640,4096]{1,0:T(8,128)(2,1)S(1)} %constant_dynamic-update-slice_fusion, f32[640,1024]{1,0:T(8,128)S(1)} %copy-done.11, f32[1024]{0:T(1024)S(1)} %add.306, f32[1024]{0:T(1024)S(1)} %mul.264, f32[640]{0:T(1024)S(1)} %fusion.43, f32[640]{0:T(1024)S(1)} %broadcast_multiply_fusion.3), kind=kOutput, calls=%fused_computation.2 | convolution fusion | flops 5376180224 | bytes 16266240 | tf_op jit(solution)/shard_map/dot_general | solution.py:465
  586.2 2.6 convolution_convert_fusion.6.g_ref
  588.9 99.1 %shard_map.312 = (bf16[640,1024]{1,0:T(8,128)(2,1)}, bf16[1280,1024]{1,0:T(8,128)(2,1)}, bf16[1280,1024]{1,0:T(8,128)(2,1)}, f32[8,12,128]{2,1,0:T(8,128)}, f32[...) custom-call(f32[8,8,128]{2,1,0:T(8,128)} %reshape.689.rows_ref, ...), custom_call_target="tpu_custom_call" | custom-call | tf_op jit(solution)/shard_map/pallas_call | solution.py:892
  688.0 3.1 broadcast_select_fusion
  703.9 4.7 convolution_convert_fusion.5
  708.6 2.3 add_convert_fusion.1
  710.9 2.3 add_convert_fusion.2
  713.4 7.9 convolution_convert_fusion.2
  721.3 4.8 multiply_reduce_fusion.4
  728.9 70.6 %shard_map.313 = (f32[640,1024]{1,0:T(8,128)}, bf16[1024,4096]{1,0:T(8,128)(2,1)}, bf16[4096,1024]{1,0:T(8,128)(2,1)}, f32[8,1024]{1,0:T(8,128)}, f32[32,1024]{1,0:T(8,128)}, /*index=5*/f32[32,3072]{1,0:T(8,128)}) custom-call(f32[640,1024]{1,0:T(8,128)} %convert_select_fusion.hidden_ref, bf16[640,1024]{1,0:T(8,128)(2,1)} %get-tuple-element.94.normed_ref, ...), custom_call_target="tpu_custom_call" | custom-call | tf_op jit(solution)/shard_map/pallas_call | solution.py:645
  805.5 83.9 %shard_map.314 = (f32[128,1024]{1,0:T(8,128)}, f32[32,4096]{1,0:T(8,128)}, f32[16,512]{1,0:T(8,128)}, bf16[2,320,1024]{2,1,0:T(8,128)(2,1)}) custom-call(bf16[4,2,4,128,1024]{4,3,2,1,0:T(8,128)(2,1)} %bitcast.114, bf16[4,2,4,32,4096]{4,3,2,1,0:T(8,128)(2,1)} %bitcast.113, bf16[4,2,4,16,512]{4,3,2,1,0:T(8,128)(2,1)} %bitcast.121, bf16[2,320,1024]{2,1,0:T(8,128)(2,1)} %bitcast.119), custom_call_target="tpu_custom_call" | custom-call | tf_op jit(solution)/shard_map/pallas_call | solution.py:427
  894.1 3.2 convert_element_type.338
  (303 shorter events, 79.2 us)
Async XLA Ops:
  0.7 90.5 %copy-start.43 = (s32[2,640]{1,0:T(2,128)S(1)}, s32[2,640]{1,0:T(2,128)}, u32[]{:S(2)}) copy-start(s32[2,640]{1,0:T(2,128)} %param.19) | copy-start | bytes 15364
  0.7 90.5 %collective-permute-start = (s32[2,640]{1,0:T(2,128)}, s32[2,640]{1,0:T(2,128)S(1)}, u32[]{:S(2)}, u32[]{:S(2)}) collective-permute-start(s32[2,640]{1,0:T(2,128)} %param.19), channel_id=1, source_target_pairs={{0,4},{4,0},{8,12},{12,8},{16,20},{20,16},{24,28},{28,24},{1,5},{5... | collective-permute-start | bytes 15368 | tf_op jit(solution)/shard_map/ppermute | solution.py:1169
  87.7 3.8 copy-start.18
  91.5 58.5 %copy-start.41 = (pred[640]{0:T(1024)(128)(4,1)}, pred[640]{0:T(1024)(128)(4,1)S(1)}, u32[]{:S(2)}) copy-start(pred[640]{0:T(1024)(128)(4,1)S(1)} %compare_reduce_fusion) | copy-start | bytes 1924
  160.3 9.3 %copy-start.3 = (f32[640,1024]{1,0:T(8,128)S(1)}, f32[640,1024]{1,0:T(8,128)}, u32[]{:S(2)}) copy-start(f32[640,1024]{1,0:T(8,128)} %get-tuple-element.73) | copy-start | bytes 7864324
  160.3 9.5 %collective-permute-start.1 = (bf16[640,2048]{1,0:T(8,128)(2,1)}, bf16[640,2048]{1,0:T(8,128)(2,1)}, u32[]{:S(2)}, u32[]{:S(2)}) collective-permute-start(bf16[640,2048]{1,0:T(8,128)(2,1)} %slice.228), channel_id=1, source_target_pairs={{0,4},{4,0},{8,12},{12,8},{16,20},{20,16},{24,28},{28,24},{1,5},{5... | collective-permute-start | bytes 7864328 | tf_op jit(solution)/shard_map/ppermute | solution.py:1169
  177.1 78.6 %copy-start.47 = (bf16[4,2,4,32,1024]{4,3,2,1,0:T(8,128)(2,1)S(1)}, bf16[4,2,4,32,1024]{4,3,2,1,0:T(8,128)(2,1)}, u32[]{:S(2)}) copy-start(bf16[4,2,4,32,1024]{4,3,2,1,0:T(8,128)(2,1)} %get-tuple-element.75) | copy-start | bytes 6291460
  258.7 8.3 copy-start.9
  268.4 3.0 collective-permute-start.2
  369.6 4.1 copy-start.45
  409.4 39.1 %slice-start = ((s8[5242880]{0:T(1024)(128)(4,1)}), s8[4194304]{0:T(1024)(128)(4,1)S(1)}, s32[]{:S(2)}) async-start(s8[5242880]{0:T(1024)(128)(4,1)} %bitcast.103), calls=%async_computation | async-start | bytes 8388608
  411.7 36.8 %slice-start.1 = ((s8[5242880]{0:T(1024)(128)(4,1)}), s8[1048576]{0:T(1024)(128)(4,1)S(1)}, s32[]{:S(2)}) async-start(s8[5242880]{0:T(1024)(128)(4,1)} %bitcast.103), calls=%async_computation.1 | async-start | bytes 2097152
  459.2 7.2 collective-permute-start.3
  691.0 17.5 %collective-permute-start.5 = (bf16[640,1024]{1,0:T(8,128)(2,1)}, bf16[640,1024]{1,0:T(8,128)(2,1)}, u32[]{:S(2)}, u32[]{:S(2)}) collective-permute-start(bf16[640,1024]{1,0:T(8,128)(2,1)} %broadcast_select_fusion), channel_id=1, source_target_pairs={{0,4},{4,0},{8,12},{12,8},{16,20},{20,16},{24,28},{28,24},{1,5},{5... | collective-permute-start | bytes 3932168 | tf_op jit(solution)/shard_map/ppermute | solution.py:1169
  691.0 3.9 copy-start.31
  691.0 6.1 copy-start.29
  691.1 8.1 copy-start.28
  692.3 18.7 %collective-permute-start.4 = (bf16[640,1024]{1,0:T(8,128)(2,1)}, bf16[640,1024]{1,0:T(8,128)(2,1)}, u32[]{:S(2)}, u32[]{:S(2)}) collective-permute-start(bf16[640,1024]{1,0:T(8,128)(2,1)} %broadcast_select_fusion.1), channel_id=1, source_target_pairs={{0,4},{4,0},{8,12},{12,8},{16,20},{20,16},{24,28},{28,24},{1,5},{5... | collective-permute-start | bytes 3932168 | tf_op jit(solution)/shard_map/ppermute | solution.py:1169
  693.6 10.3 %copy-start.8 = (f32[640,1024]{1,0:T(8,128)S(1)}, f32[640,1024]{1,0:T(8,128)}, u32[]{:S(2)}) copy-start(f32[640,1024]{1,0:T(8,128)} %copy-done.7) | copy-start | bytes 7864324
  703.9 4.7 copy-start.15
  708.6 12.7 %slice-start.2 = ((s8[6291456]{0:T(1024)(128)(4,1)}), s8[4194304]{0:T(1024)(128)(4,1)S(1)}, s32[]{:S(2)}) async-start(s8[6291456]{0:T(1024)(128)(4,1)} %bitcast.151), calls=%async_computation.2 | async-start | bytes 8388608
  713.3 7.9 copy-start.4
  713.3 7.9 copy-start.39
  713.3 7.9 copy-start.40
  713.3 7.9 slice-start.3
  713.3 7.9 copy-start.51
  728.9 70.6 %copy-start.42 = (pred[640]{0:T(1024)(128)(4,1)S(1)}, pred[640]{0:T(1024)(128)(4,1)}, u32[]{:S(2)}) copy-start(pred[640]{0:T(1024)(128)(4,1)} %copy-done.41) | copy-start | bytes 1924
  889.4 8.0 copy-start.19
  894.1 4.3 copy-start.24
  897.3 4.1 copy-start.22
  898.4 4.5 copy-start.21
  898.4 5.3 copy-start.20
  (30 other events, 71.8 us)

commit v3 on v2

--- a/solution.py
+++ b/solution.py
@@ -118,13 +118,71 @@
     return lambda: pl.when(condition)(action)
 
 
+def shares(columns, split):
+    first = columns * split // 8
+    if first % 256 or (columns - first) % 256:
+        first = columns
+    return (0, first), (first, columns - first)
+
+
+class Timetable:
+    def __init__(self, sizes, split):
+        chips, frames = sizes
+        half = chips // 2
+        self.known = chips == 4 and frames == 4
+        self.both = split < 8
+        self.half, self.frames = half, frames
+
+    def gather(self, distance, step):
+        if not self.known:
+            return distance + step + 0.1 * bool(step)
+        if self.both:
+            return ((0, 0.95, 2.45, 3.7), (1.0, 2.6, 3.75, 4.5), (3.0, 4.5, 4.9, 4.9))[step][distance]
+        return ((0, 0.95, 1.95, 2.95), (1.0, 3.0, 4.5, 5.0), (3.5, 4.6, 5.6, 6.0))[step][distance]
+
+    def gather_ring(self, distance, step):
+        if not self.known:
+            return distance + step
+        return ((0, 1.0, 3.0), (1.0, 2.5, 4.25), (2.5, 4.25, 5.0), (4.0, 5.0, 5.25))[step][distance]
+
+    def pair(self, distance):
+        if not self.known:
+            return distance + self.half + 0.5
+        if self.both:
+            return (3.05, 4.55, 5.05, 5.3)[distance]
+        return (3.55, 4.65, 5.65, 6.05)[distance]
+
+    def merge(self, distance):
+        if not self.known:
+            return 0.01 * (self.frames - distance)
+        return (1.3, 1.0, 0.7, 0.35)[distance]
+
+    def scatter(self, distance, step):
+        if not self.known:
+            return self.frames - 1 - distance + step
+        if self.both:
+            return ((4.29, 3.49, 2.69, 1.35), (5.1, 4.3, 3.5, 2.7))[step - 1][distance]
+        return ((2.6, 2.2, 1.8, 1.4), (6.4, 5.4, 4.4, 3.4))[step - 1][distance]
+
+    def scatter_ring(self, distance, step):
+        if not self.known:
+            return self.half - distance + step + 0.5
+        return ((2.66, 1.33, 0.4), (3.46, 2.67, 1.34), (4.27, 3.47, 2.68), (5.0, 4.28, 3.48))[step][distance]
+
+    def scatter_last(self, distance):
+        if not self.known:
+            return self.half - distance + self.frames - 1 + 0.5
+        return (5.1, 4.29)[distance]
+
+
 class Mover:
-    def __init__(self, spots, sizes, send_sems, recv_sems):
+    def __init__(self, spots, sizes, split, send_sems, recv_sems):
+        self.time = Timetable(sizes, split)
         self.chips, self.frames = sizes
         self.chip, self.core, self.depth, self.chip_at = spots
         self.send_sems, self.recv_sems = send_sems, recv_sems
         self.used = 0
-        self.levels = [[] for _ in range(self.frames + self.chips // 2 + 1)]
+        self.events = []
         self.departures = []
 
     def copy(self, source, target, device, condition):
@@ -141,6 +199,9 @@
         self.departures.append(gated(condition, made.wait_send))
         return made
 
+    def at(self, time, *actions):
+        self.events += [(time, action) for action in actions]
+
     def other_core(self):
         return (self.chip * 2 + 1 - self.core, self.depth)
 
@@ -150,78 +211,122 @@
             return at, None
         return jnp.clip(at, 0, self.frames - 1), jnp.logical_and(at >= 0, at < self.frames)
 
+    def chips_at(self, distance):
+        if distance == 0:
+            return (self.chip,)
+        if distance == self.chips // 2:
+            return (self.chip_at(distance),)
+        return (self.chip_at(distance), self.chip_at(-distance))
+
     def offsets(self, distance):
         return (0,) if distance == 0 else (-distance, distance)
 
 
 class Gather(Mover):
-    def __init__(self, spots, sizes, shard, whole, send_sems, recv_sems, local_sems):
-        super().__init__(spots, sizes, send_sems, recv_sems)
+    def __init__(self, spots, sizes, shard, whole, split, send_sems, recv_sems, local_sems):
+        super().__init__(spots, sizes, split, send_sems, recv_sems)
         self.shard, self.whole = shard, whole
+        self.first, self.last = shares(shard.shape[1], split)
         self.local = pltpu.make_async_copy(
             shard, whole.at[self.chip, self.core, self.depth], local_sems.at[0]
         )
-        self.levels[0].append(self.local.start)
+        self.at(0, self.local.start)
         for distance in range(self.frames):
             self.spread(distance)
-        self.levels[-1] += self.departures
+        if self.last[1]:
+            for distance in range(self.chips // 2 + 1):
+                self.spread_ring(distance)
+        for distance in range(self.frames):
+            self.hand_over(distance)
+        self.ends = self.departures
 
     def spread(self, distance):
         chip, core, depth, half = self.chip, self.core, self.depth, self.chips // 2
         for offset in self.offsets(distance):
             held, valid = self.group(offset)
-            block = self.whole.at[chip, core, held]
-            source = block if distance else self.shard
+            start, columns = self.first
+            block = self.whole.at[chip, core, held, :, pl.ds(start, columns)]
+            source = block if distance else self.shard.at[:, pl.ds(start, columns)]
             for way in (1, -1):
                 if distance + 1 == self.frames or offset * way > 0:
                     continue
                 into, there = self.group(way)
                 condition = there if valid is None else jnp.logical_and(valid, there)
                 made = self.copy(source, block, (chip * 2 + core, into), condition)
-                self.levels[distance].append(gated(condition, made.start))
+                self.at(self.time.gather(distance, 0), gated(condition, made.start))
                 comes = self.group(offset - way)[1]
-                self.levels[distance + 1].insert(0, gated(comes, made.wait_recv))
-            columns = self.shard.shape[1]
+                self.at(self.time.gather(distance + 1, 0), gated(comes, made.wait_recv))
             for step in range(1, half + 1):
-                level = distance + step - 1
                 for side, way in enumerate((1, -1)):
-                    part = slice(None)
+                    part = pl.ds(start, columns)
                     if step == half:
-                        part = pl.ds(side * columns // 2, columns // 2)
+                        part = pl.ds(start + side * columns // 2, columns // 2)
                     origin = self.chip_at(-way * (step - 1))
                     target = self.whole.at[origin, core, held, :, part]
-                    start = self.shard.at[:, part] if distance == 0 and step == 1 else target
-                    made = self.copy(start, target, (self.chip_at(way) * 2 + core, depth), valid)
-                    self.levels[level].append(gated(valid, made.start))
-                    self.levels[level + 1].append(gated(valid, made.wait_recv))
+                    given = self.shard.at[:, part] if distance == 0 and step == 1 else target
+                    made = self.copy(given, target, (self.chip_at(way) * 2 + core, depth), valid)
+                    self.at(self.time.gather(distance, step - 1), gated(valid, made.start))
+                    self.at(self.time.gather(distance, step), gated(valid, made.wait_recv))
+
+    def hand_over(self, distance):
+        for offset in self.offsets(distance):
+            held, valid = self.group(offset)
+            line = self.whole.at[:, self.core, held]
+            pair = self.copy(line, line, self.other_core(), valid)
             if distance == 0:
-                self.levels[half].append(self.local.wait)
-            line = self.whole.at[:, core, held]
-            pair = self.copy(line, line, self.other_core(), valid)
-            self.levels[distance + half].append(gated(valid, pair.start))
-            self.levels[-1].append(gated(valid, pair.wait_recv))
+                self.at(self.time.pair(0), self.local.wait)
+            self.at(self.time.pair(distance), gated(valid, pair.start))
+            self.departures.append(gated(valid, pair.wait_recv))
+
+    def spread_ring(self, distance):
+        core, depth, half = self.core, self.depth, self.chips // 2
+        start, columns = self.last
+        everything = pl.ds(start, columns)
+        if distance < half:
+            step = distance + 1
+            for side, way in enumerate((1, -1)):
+                part = everything
+                if step == half:
+                    part = pl.ds(start + side * columns // 2, columns // 2)
+                target = self.whole.at[self.chip_at(-way * distance), core, depth, :, part]
+                given = target if distance else self.shard.at[:, part]
+                made = self.copy(given, target, (self.chip_at(way) * 2 + core, depth), None)
+                self.at(self.time.gather_ring(distance, 0), made.start)
+                self.at(self.time.gather_ring(distance + 1, 0), made.wait_recv)
+        for place, chip in enumerate(self.chips_at(distance)):
+            for step in range(1, self.frames):
+                for way in (1, -1):
+                    held, there = self.group(-way * (step - 1))
+                    into, beside = self.group(way)
+                    valid = beside if there is None else jnp.logical_and(there, beside)
+                    block = self.whole.at[chip, core, held, :, everything]
+                    given = block if distance or step > 1 else self.shard.at[:, everything]
+                    made = self.copy(given, block, (self.chip * 2 + core, into), valid)
+                    self.at(self.time.gather_ring(distance, step - 1), gated(valid, made.start))
+                    comes = self.group(-way * step)[1]
+                    self.at(self.time.gather_ring(distance, step), gated(comes, made.wait_recv))
 
 
 class Scatter(Mover):
     def __init__(
-        self, spots, sizes, grads, out, total, stage, landings, send_sems, recv_sems, local_sems
+        self, spots, sizes, grads, out, total, stage, landings, split, send_sems, recv_sems, local_sems
     ):
-        super().__init__(spots, sizes, send_sems, recv_sems)
+        super().__init__(spots, sizes, split, send_sems, recv_sems)
         self.grads, self.out, self.total, self.stage = grads, out, total, stage
-        self.landings = list(landings)
+        (self.halves, self.fulls, self.lines), self.landings = landings[:3], list(landings[3:])
         self.local_sems = local_sems
-        self.begins = []
-        self.columns = out.shape[1]
+        self.first, self.last = shares(out.shape[1], split)
         self.merges = 0
         for distance in reversed(range(self.frames)):
             self.collect(distance)
-        self.levels[-1] += [self.finish] + self.departures
+        if self.last[1]:
+            for distance in reversed(range(self.chips // 2 + 1)):
+                self.collect_ring(distance)
+        self.ends = [self.finish] + self.departures
 
     def add(self, where, piece):
         total = self.total
-        total[where] = (total[where].astype(jnp.float32) + piece.astype(jnp.float32)).astype(
-            total.dtype
-        )
+        total[where] = total[where] + piece
 
     def merge(self, held, pair, load, stage):
         load.wait()
@@ -237,81 +342,148 @@
 
     def collect(self, distance):
         core, depth, half = self.core, self.depth, self.chips // 2
-        first = self.frames - 1 - distance
         for offset in self.offsets(distance):
             held, valid = self.group(offset)
             pair = self.copy(
                 self.grads.at[:, 1 - core, held], self.total.at[:, held], self.other_core(), valid
             )
-            stage = self.stage.at[self.merges]
+            stage = self.stage.at[held]
             load = pltpu.make_async_copy(
                 self.grads.at[:, core, held], stage, self.local_sems.at[self.merges]
             )
             self.merges += 1
-            self.begins += [gated(valid, pair.start), gated(valid, load.start)]
-            self.levels[0].append(
-                gated(valid, functools.partial(self.merge, held, pair, load, stage))
+            begin = -0.01 * (distance + 1)
+            self.at(begin, gated(valid, pair.start), gated(valid, load.start))
+            self.at(
+                self.time.merge(distance),
+                gated(valid, functools.partial(self.merge, held, pair, load, stage)),
             )
+            start, columns = self.first
+            everything = pl.ds(start, columns)
             for step in range(1, half + 1):
                 for side, way in enumerate((1, -1)):
-                    part = slice(None)
+                    part = everything
                     if step == 1:
-                        part = pl.ds(side * self.columns // 2, self.columns // 2)
+                        part = pl.ds(start + side * columns // 2, columns // 2)
                     reach = half - step + 1
                     goal = self.chip_at(way * reach)
-                    landed = self.landings.pop(0)
+                    if step == 1:
+                        landed = self.halves.at[held, side]
+                    else:
+                        landed = self.fulls.at[held, 2 * (step - 2) + side]
                     made = self.copy(
                         self.total.at[goal, held, :, part],
                         landed,
                         (self.chip_at(way) * 2 + core, depth),
                         valid,
                     )
-                    self.levels[step - 1 if step == 1 else first + step - 1].append(
-                        gated(valid, made.start)
-                    )
+                    ready = self.time.scatter(distance, step - 1) if step > 1 else self.time.merge(distance)
+                    self.at(ready, gated(valid, made.start))
                     where = (self.chip_at(way * (reach - 1)), held, slice(None), part)
-                    self.levels[first + step].append(
-                        gated(valid, functools.partial(self.settle, made, where, landed))
+                    self.at(
+                        self.time.scatter(distance, step),
+                        gated(valid, functools.partial(self.settle, made, where, landed)),
                     )
             if distance == 0:
                 continue
             way = 1 if offset > 0 else -1
-            landed = self.landings.pop(0)
+            landed = self.lines.at[0 if way > 0 else 1, held]
             made = self.copy(
-                self.total.at[self.chip, held],
+                self.total.at[self.chip, held, :, everything],
                 landed,
                 (self.chip * 2 + core, self.group(way)[0]),
                 valid,
             )
-            self.levels[first + half].append(gated(valid, made.start))
+            self.at(self.time.scatter(distance, half), gated(valid, made.start))
             before = self.group(-way)[1]
             goes, there = self.group(offset - way)
             comes = before if there is None else jnp.logical_and(before, there)
-            where = (self.chip, goes, slice(None), slice(None))
-            self.levels[first + half + 1].append(
-                gated(comes, functools.partial(self.settle, made, where, landed))
+            where = (self.chip, goes, slice(None), everything)
+            arrived = self.lines.at[0 if way > 0 else 1, goes]
+            self.at(
+                self.time.scatter(distance - 1, half) - 0.01,
+                gated(comes, functools.partial(self.settle, made, where, arrived)),
+            )
+
+    def collect_ring(self, distance):
+        core, depth, half = self.core, self.depth, self.chips // 2
+        start, columns = self.last
+        everything = pl.ds(start, columns)
+        for chip in self.chips_at(distance):
+            for step in range(1, self.frames):
+                for way in (1, -1):
+                    reach = way * (self.frames - step)
+                    held, valid = self.group(reach)
+                    landed = self.landings.pop(0)
+                    made = self.copy(
+                        self.total.at[chip, held, :, everything],
+                        landed,
+                        (self.chip * 2 + core, self.group(way)[0]),
+                        valid,
+                    )
+                    self.at(self.time.scatter_ring(distance, step - 1), gated(valid, made.start))
+                    before = self.group(-way)[1]
+                    goes, there = self.group(reach - way)
+                    comes = before if there is None else jnp.logical_and(before, there)
+                    where = (chip, goes, slice(None), everything)
+                    self.at(
+                        self.time.scatter_ring(distance, step),
+                        gated(comes, functools.partial(self.settle, made, where, landed)),
+                    )
+        if distance == 0:
+            return
+        whole = max(
+            self.time.scatter_ring(distance, self.frames - 1),
+            self.time.scatter_last(distance) if distance < half else 0,
+        )
+        for side, way in enumerate((1, -1)):
+            part = everything
+            if distance == half:
+                part = pl.ds(start + side * columns // 2, columns // 2)
+            goal = self.chip_at(way * distance)
+            landed = self.landings.pop(0)
+            made = self.copy(
+                self.total.at[goal, depth, :, part],
+                landed,
+                (self.chip_at(way) * 2 + core, depth),
+                None,
+            )
+            self.at(whole + 0.01, made.start)
+            where = (self.chip_at(way * (distance - 1)), depth, slice(None), part)
+            self.at(
+                self.time.scatter_last(distance - 1),
+                functools.partial(self.settle, made, where, landed),
             )
 
     def finish(self):
         self.out[...] = self.total[self.chip, self.depth].astype(self.out.dtype)
 
 
-def landing_shapes(sizes, rows, columns):
+def landing_shapes(sizes, rows, columns, split):
     chips, frames = sizes
-    shapes = []
-    for distance in reversed(range(frames)):
-        for _ in range(2 if distance else 1):
-            shapes += [(rows, columns // 2)] * 2 + [(rows, columns)] * (2 * (chips // 2 - 1))
+    (_, first), (_, last) = shares(columns, split)
+    half = chips // 2
+    shapes = [
+        (frames, 2, rows, first // 2),
+        (frames, max(2 * (half - 1), 1), rows, first),
+        (2, frames, rows, first),
+    ]
+    if last:
+        for distance in reversed(range(half + 1)):
+            many = 1 if distance in (0, half) else 2
+            shapes += [(rows, last)] * (many * 2 * (frames - 1))
             if distance:
-                shapes.append((rows, columns))
+                shapes += [(rows, last // 2 if distance == half else last)] * 2
     return shapes
 
 
 class Traffic:
-    def __init__(self, sizes, identity, shards=(), grads=(), swapped=(), swap_at=0):
+    def __init__(
+        self, sizes, identity, shards=(), grads=(), swapped=(), swap_at=0, split=8, pace=1.0
+    ):
         self.sizes, self.identity = sizes, identity
         self.shards, self.grads, self.swapped = list(shards), list(grads), list(swapped)
-        self.swap_at = swap_at
+        self.swap_at, self.split, self.pace = swap_at, split, pace
         self.active = bool(self.shards or self.grads or self.swapped)
 
     def operands(self):
@@ -345,10 +517,10 @@
             shard = grad.shape[3:]
             shapes += [
                 pltpu.VMEM((chips, frames) + shard, grad.dtype),
-                pltpu.VMEM((2 * frames - 1, chips) + shard, grad.dtype),
+                pltpu.VMEM((frames, chips) + shard, grad.dtype),
             ]
-            shapes += [pltpu.VMEM(shape, grad.dtype) for shape in landing_shapes(self.sizes, *shard)]
-        copies = (2 * frames - 1) * (3 + chips)
+            shapes += [pltpu.VMEM(shape, grad.dtype) for shape in landing_shapes(self.sizes, *shard, self.split)]
+        copies = (2 * frames - 1) * (3 + chips) + chips * (2 * frames - 1)
         arrays = max(len(self.shards) + len(self.grads), 1)
         swaps = max(len(self.swapped), 1)
         return shapes + [
@@ -368,59 +540,64 @@
         send_sems, recv_sems, local_sems, swap_send, swap_recv, swap_local = scratch[-6:]
         spots = places(chips, frames)
         gathers, scatters = len(self.shards), len(self.grads)
-        parts, begins = [], []
+        parts = []
         for at in range(gathers + scatters):
             sems = (send_sems.at[at], recv_sems.at[at], local_sems.at[at])
             if at < gathers:
-                parts.append(Gather(spots, self.sizes, ins[at], outs[at], *sems))
+                parts.append(Gather(spots, self.sizes, ins[at], outs[at], self.split, *sems))
                 continue
             total, stage = scratch.pop(0), scratch.pop(0)
-            many = len(landing_shapes(self.sizes, *outs[at].shape))
+            many = len(landing_shapes(self.sizes, *outs[at].shape, self.split))
             landings = [scratch.pop(0) for _ in range(many)]
             parts.append(
-                Scatter(spots, self.sizes, ins[at], outs[at], total, stage, landings, *sems)
+                Scatter(
+                    spots, self.sizes, ins[at], outs[at], total, stage, landings, self.split, *sems
+                )
             )
-            begins += parts[-1].begins
-        times = [[], []]
-        if parts:
-            times = [sum(level, []) for level in zip(*[part.levels for part in parts])]
+        events = [event for part in parts for event in part.events]
+        last = max([time for time, _ in events], default=1.0)
+        ends = sum([part.ends for part in parts], [])
         if self.swapped:
-            starts, ends = swap_frames(
-                chips, frames, ins[gathers + scatters :], outs[gathers + scatters :],
-                swap_send, swap_recv, swap_local,
+            starts, waits = swap_frames(
+                chips,
+                frames,
+                ins[gathers + scatters :],
+                outs[gathers + scatters :],
+                swap_send,
+                swap_recv,
+                swap_local,
             )
-            times[min(self.swap_at, len(times) - 1)] += starts
-            times[-1] += ends
-        times[0] = [functools.partial(greet, chips, frames, bool(self.swapped))] + begins + times[0]
-        return times
-
-
-def run_plan(times, step=None, steps=1):
-    if step is None:
-        for actions in times:
-            for action in actions:
+            events += [(self.swap_at, action) for action in starts]
+            ends += waits
+        events.append((-1, functools.partial(greet, chips, frames, bool(self.swapped))))
+        events = sorted(events, key=lambda event: event[0])
+        return [(max(time / last, 0.0) * 0.97, action) for time, action in events] + [
+            (1.0, action) for action in ends
+        ]
+
+
+def run_plan(traffic, ins, outs, scratch, step, steps, late=False):
+    if not traffic.active:
+        return
+    whens = [when for when, _ in traffic.plan(ins, outs, scratch)]
+    due = [min(int(when * traffic.pace * steps), steps) for when in whens]
+
+    def run(place):
+        for at, (_, action) in zip(due, traffic.plan(ins, outs, scratch)):
+            if at == place:
                 action()
+
+    if late:
+        pl.when(step == steps - 1)(functools.partial(run, steps))
         return
-    by_step = {}
-    for at, actions in enumerate(times):
-        by_step.setdefault(at * steps // len(times), []).extend(actions)
-    for at, actions in by_step.items():
-
-        def run(actions=actions):
-            for action in actions:
-                action()
-
-        pl.when(step == at)(run)
-
-
-def finish_plan(times):
-    for action in times[-1]:
-        action()
+    for place in sorted(set(due) - {steps}):
+        pl.when(step == place)(functools.partial(run, place))
 
 
 def traffic_kernel(traffic, *refs):
     count = len(traffic.operands())
-    run_plan(traffic.plan(refs[:count], refs[count : 2 * count], refs[2 * count :]))
+    for _, action in traffic.plan(refs[:count], refs[count : 2 * count], refs[2 * count :]):
+        action()
 
 
 def move(traffic):
@@ -529,7 +706,7 @@
     outs, refs = refs[4 : 4 + moved], refs[4 + moved :]
     total, refs = refs[0], refs[1:]
     step, steps = pl.program_id(0), pl.num_programs(0)
-    run_plan(traffic.plan(ins, outs, refs), step, FFN_STEPS)
+    run_plan(traffic, ins, outs, refs, step, FFN_STEPS)
     each = chunks(hidden_ref.shape[0])
 
     @pl.when(step == 0)
@@ -552,6 +729,8 @@
             next_ref[here, :] = norm_chunk(hidden, norms_ref, 1).astype(jnp.bfloat16)
 
         each(body)
+
+    run_plan(traffic, ins, outs, refs, step, FFN_STEPS, late=True)
 
 
 FFN_STEPS = 8
@@ -602,7 +781,7 @@
     outs, refs = refs[4 : 4 + moved], refs[4 + moved :]
     (half_grad, turned, total), refs = refs[:3], refs[3:]
     step, steps = pl.program_id(0), pl.num_programs(0)
-    run_plan(traffic.plan(ins, outs, refs), step, FFN_STEPS)
+    run_plan(traffic, ins, outs, refs, step, FFN_STEPS)
     each = chunks(hidden_ref.shape[0])
 
     @pl.when(step == 0)
@@ -637,6 +816,8 @@
             out_ref[here, :] = grad_ref[here, :] + rstd * back
 
         each(body)
+
+    run_plan(traffic, ins, outs, refs, step, FFN_STEPS, late=True)
 
 
 def ffn_back(hidden, normed, grad, norms, inner, weight_in, weight_out, traffic):
@@ -731,24 +912,34 @@
     return pl.multiple_of(length - QB - first, QB), first
 
 
-def attend_kernel(rows, length, traffic, rows_ref, q_ref, k_ref, v_ref, *refs):
+def in_order(whole, own_ref, far_ref):
+    rows = own_ref.shape[0]
+    core = lax.rem(lax.axis_index("batch"), 2)
+    whole[pl.ds(pl.multiple_of(core * rows, QB), rows), :] = own_ref[...]
+    whole[pl.ds(pl.multiple_of((1 - core) * rows, QB), rows), :] = far_ref[...]
+
+
+def attend_kernel(
+    rows, length, traffic, rows_ref, q_ref, k_own_ref, v_own_ref, k_far_ref, v_far_ref, *refs
+):
     moved = len(traffic.operands())
     ins, refs = refs[:moved], refs[moved:]
     (out_ref, log_ref), refs = refs[:2], refs[2:]
     outs, refs = refs[:moved], refs[moved:]
-    (strip, score, prob, vt), refs = refs[:4], refs[4:]
+    (strip, score, prob, vt, k_all, v_all), refs = refs[:6], refs[6:]
     blocks = rows // QB
-    run_plan(
-        traffic.plan(ins, outs, refs), pl.program_id(0) * blocks + pl.program_id(1), PAIRS * blocks
-    )
+    step = pl.program_id(0) * blocks + pl.program_id(1)
+    run_plan(traffic, ins, outs, refs, step, PAIRS * blocks)
 
     @pl.when(pl.program_id(1) == 0)
     def _():
         fill_strip(strip, rows_ref, length)
-        vt[...] = v_ref[...].T
+        in_order(k_all, k_own_ref, k_far_ref)
+        in_order(v_all, v_own_ref, v_far_ref)
+        vt[...] = v_all[...].T
 
     start, _ = strip_start(rows, length)
-    score[...] = dot_nt(k_ref[...], stacked(q_ref[...] * 0.125))
+    score[...] = dot_nt(k_all[...], stacked(q_ref[...] * 0.125))
 
     def highest(at, most):
         here = pl.ds(pl.multiple_of(at * QB, QB), QB)
@@ -774,10 +965,12 @@
     mixed = dot_nn(vt[...], prob[...]) / total
     out_ref[...] = own_halves(mixed).astype(out_ref.dtype)
     log_ref[0] = most + jnp.log(total)
-
-
-def attend(queries, key_values, offsets, traffic):
-    rows, length = queries.shape[0], key_values.shape[0]
+    run_plan(traffic, ins, outs, refs, step, PAIRS * blocks, late=True)
+
+
+def attend(packed, far, offsets, traffic):
+    rows = packed.shape[0]
+    length = 2 * rows
     blocks = rows // QB
     return pl.pallas_call(
         functools.partial(attend_kernel, rows, length, traffic),
@@ -790,8 +983,10 @@
         in_specs=[
             pl.BlockSpec((1, 8, QB), lambda p, b: (p, 0, 0)),
             pl.BlockSpec((QB, 2 * DH), lambda p, b: (b, p)),
-            pl.BlockSpec((length, 2 * DH), lambda p, b: (0, p)),
-            pl.BlockSpec((length, 2 * DH), lambda p, b: (0, PAIRS + p)),
+            pl.BlockSpec((rows, 2 * DH), lambda p, b: (0, PAIRS + p)),
+            pl.BlockSpec((rows, 2 * DH), lambda p, b: (0, 2 * PAIRS + p)),
+            pl.BlockSpec((rows, 2 * DH), lambda p, b: (0, p)),
+            pl.BlockSpec((rows, 2 * DH), lambda p, b: (0, PAIRS + p)),
         ]
         + traffic.in_specs(),
         out_specs=[
@@ -804,27 +999,45 @@
             pltpu.VMEM((length, 2 * QB), jnp.float32),
             pltpu.VMEM((length, 2 * QB), jnp.bfloat16),
             pltpu.VMEM((2 * DH, length), jnp.bfloat16),
+            pltpu.VMEM((length, 2 * DH), jnp.bfloat16),
+            pltpu.VMEM((length, 2 * DH), jnp.bfloat16),
         ]
         + traffic.scratch(),
         compiler_params=traffic_params(traffic),
-    )(offsets, queries, key_values, key_values, *traffic.operands())
+    )(offsets, packed, packed, packed, far, far, *traffic.operands())
 
 
 def attend_back_kernel(
-    rows, length, traffic, rows_ref, q_ref, k_ref, v_ref, g_ref, log_ref, *refs
+    rows,
+    length,
+    traffic,
+    rows_ref,
+    q_ref,
+    k_own_ref,
+    v_own_ref,
+    k_far_ref,
+    v_far_ref,
+    g_ref,
+    log_ref,
+    *refs,
 ):
     moved = len(traffic.operands())
     ins, refs = refs[:moved], refs[moved:]
-    (dq_ref, dk_ref, dv_ref, near_ref, sums_ref), refs = refs[:5], refs[5:]
+    (dq_ref, dk_own_ref, dv_own_ref, dk_far_ref, dv_far_ref), refs = refs[:5], refs[5:]
+    (near_ref, sums_ref), refs = refs[:2], refs[2:]
     outs, refs = refs[:moved], refs[moved:]
     (strip, score, slope, prob, change, kt, dk_sum, dv_sum, near), refs = refs[:9], refs[9:]
+    (k_all, v_all), refs = refs[:2], refs[2:]
     block, blocks = pl.program_id(1), rows // QB
-    run_plan(traffic.plan(ins, outs, refs), pl.program_id(0) * blocks + block, PAIRS * blocks)
+    step = pl.program_id(0) * blocks + block
+    run_plan(traffic, ins, outs, refs, step, PAIRS * blocks)
 
     @pl.when(block == 0)
     def _():
         fill_strip(strip, rows_ref, length)
-        kt[...] = k_ref[...].T
+        in_order(k_all, k_own_ref, k_far_ref)
+        in_order(v_all, v_own_ref, v_far_ref)
+        kt[...] = k_all[...].T
         dk_sum[...] = jnp.zeros_like(dk_sum)
         dv_sum[...] = jnp.zeros_like(dv_sum)
         near[...] = jnp.zeros_like(near)
@@ -834,8 +1047,8 @@
     start, first = strip_start(rows, length)
     q_both = stacked(q_ref[...] * 0.125)
     g_both = stacked(g_ref[...])
-    score[...] = dot_nt(k_ref[...], q_both)
-    slope[...] = dot_nt(v_ref[...], g_both)
+    score[...] = dot_nt(k_all[...], q_both)
+    slope[...] = dot_nt(v_all[...], g_both)
     log_total = log_ref[0]
 
     def weigh(at, total):
@@ -866,8 +1079,13 @@
 
     @pl.when(block == pl.num_programs(1) - 1)
     def _():
-        dk_ref[...] = dk_sum[...].astype(dk_ref.dtype)
-        dv_ref[...] = dv_sum[...].astype(dv_ref.dtype)
+        core = lax.rem(lax.axis_index("batch"), 2)
+        own = pl.ds(pl.multiple_of(core * rows, QB), rows)
+        far = pl.ds(pl.multiple_of((1 - core) * rows, QB), rows)
+        dk_own_ref[...] = dk_sum[own, :].astype(jnp.bfloat16)
+        dv_own_ref[...] = dv_sum[own, :].astype(jnp.bfloat16)
+        dk_far_ref[...] = dk_sum[far, :].astype(jnp.bfloat16)
+        dv_far_ref[...] = dv_sum[far, :].astype(jnp.bfloat16)
         rows_of = lax.broadcasted_iota(jnp.int32, (QB, QB), 0)
         lanes_of = lax.broadcasted_iota(jnp.int32, (QB, QB), 1)
         for head in range(2):
@@ -884,9 +1102,12 @@
                     at = head * 6 + tile * 2 + half
                     near_ref[0, at : at + 1, :] = jnp.sum(piece, axis=0, keepdims=True)
 
-
-def attend_back(queries, key_values, offsets, log_total, grads, traffic):
-    rows, length = queries.shape[0], key_values.shape[0]
+    run_plan(traffic, ins, outs, refs, step, PAIRS * blocks, late=True)
+
+
+def attend_back(packed, far, offsets, log_total, grads, traffic):
+    rows = packed.shape[0]
+    length = 2 * rows
     blocks = rows // QB
     big = (length, 2 * QB)
     return pl.pallas_call(
@@ -894,8 +1115,10 @@
         grid=(PAIRS, blocks),
         out_shape=[
             jax.ShapeDtypeStruct((rows, D), jnp.bfloat16),
-            jax.ShapeDtypeStruct((length, D), jnp.bfloat16),
-            jax.ShapeDtypeStruct((length, D), jnp.bfloat16),
+            jax.ShapeDtypeStruct((rows, D), jnp.bfloat16),
+            jax.ShapeDtypeStruct((rows, D), jnp.bfloat16),
+            jax.ShapeDtypeStruct((rows, D), jnp.bfloat16),
+            jax.ShapeDtypeStruct((rows, D), jnp.bfloat16),
             jax.ShapeDtypeStruct((PAIRS, 12, QB), jnp.float32),
             jax.ShapeDtypeStruct((PAIRS * blocks, length // QB, 2 * QB), jnp.float32),
         ]
@@ -903,16 +1126,20 @@
         in_specs=[
             pl.BlockSpec((1, 8, QB), lambda p, b: (p, 0, 0)),
             pl.BlockSpec((QB, 2 * DH), lambda p, b: (b, p)),
-            pl.BlockSpec((length, 2 * DH), lambda p, b: (0, p)),
-            pl.BlockSpec((length, 2 * DH), lambda p, b: (0, PAIRS + p)),
+            pl.BlockSpec((rows, 2 * DH), lambda p, b: (0, PAIRS + p)),
+            pl.BlockSpec((rows, 2 * DH), lambda p, b: (0, 2 * PAIRS + p)),
+            pl.BlockSpec((rows, 2 * DH), lambda p, b: (0, p)),
+            pl.BlockSpec((rows, 2 * DH), lambda p, b: (0, PAIRS + p)),
             pl.BlockSpec((QB, 2 * DH), lambda p, b: (b, p)),
             pl.BlockSpec((1, 1, 2 * QB), lambda p, b: (p * blocks + b, 0, 0)),
         ]
         + traffic.in_specs(),
         out_specs=[
             pl.BlockSpec((QB, 2 * DH), lambda p, b: (b, p)),
-            pl.BlockSpec((length, 2 * DH), lambda p, b: (0, p)),
-            pl.BlockSpec((length, 2 * DH), lambda p, b: (0, p)),
+            pl.BlockSpec((rows, 2 * DH), lambda p, b: (0, p)),
+            pl.BlockSpec((rows, 2 * DH), lambda p, b: (0, p)),
+            pl.BlockSpec((rows, 2 * DH), lambda p, b: (0, p)),
+            pl.BlockSpec((rows, 2 * DH), lambda p, b: (0, p)),
             pl.BlockSpec((1, 12, QB), lambda p, b: (p, 0, 0)),
             pl.BlockSpec((1, length // QB, 2 * QB), lambda p, b: (p * blocks + b, 0, 0)),
         ]
@@ -927,10 +1154,12 @@
             pltpu.VMEM((length, 2 * DH), jnp.float32),
             pltpu.VMEM((length, 2 * DH), jnp.float32),
             pltpu.VMEM((BAND, 2 * QB), jnp.float32),
+            pltpu.VMEM((length, 2 * DH), jnp.bfloat16),
+            pltpu.VMEM((length, 2 * DH), jnp.bfloat16),
         ]
         + traffic.scratch(),
         compiler_params=traffic_params(traffic),
-    )(offsets, queries, key_values, key_values, grads, log_total, *traffic.operands())
+    )(offsets, packed, packed, packed, far, far, grads, log_total, *traffic.operands())
 
 
 def table_back(near, sums, first_block):
@@ -979,10 +1208,10 @@
 def conv_kernel(traffic, padded_ref, taps_ref, norms_ref, *refs):
     moved = len(traffic.operands())
     ins, refs = refs[:moved], refs[moved:]
-    (depth_ref, post_ref), refs = refs[:2], refs[2:]
+    (depth_ref, post_ref, mean_ref, rstd_ref), refs = refs[:4], refs[4:]
     outs, refs = refs[:moved], refs[moved:]
     step = pl.program_id(0)
-    run_plan(traffic.plan(ins, outs, refs), step, CONV_BLOCKS)
+    run_plan(traffic, ins, outs, refs, step, CONV_BLOCKS)
     first = pl.multiple_of(step * BLOCK, BLOCK)
 
     @pl.loop(0, C // LANES)
@@ -997,9 +1226,13 @@
     @pl.loop(0, BLOCK // 16)
     def _(at):
         here = pl.ds(pl.multiple_of(at * 16, 16), 16)
-        scaled, _ = norm_parts(depth_ref[here, :])
+        scaled, rstd = norm_parts(depth_ref[here, :])
+        mean_ref[here, :] = jnp.mean(depth_ref[here, :], axis=-1, keepdims=True)
+        rstd_ref[here, :] = rstd
         normed = scaled * norms_ref[0:1, :] + norms_ref[1:2, :]
         post_ref[here, :] = (normed * sigmoid(normed)).astype(jnp.bfloat16)
+
+    run_plan(traffic, ins, outs, refs, step, CONV_BLOCKS, late=True)
 
 
 CONV_BLOCKS = 5
@@ -1013,6 +1246,8 @@
         out_shape=[
             jax.ShapeDtypeStruct((rows, C), jnp.float32),
             jax.ShapeDtypeStruct((rows, C), jnp.bfloat16),
+            jax.ShapeDtypeStruct((rows, 1), jnp.float32),
+            jax.ShapeDtypeStruct((rows, 1), jnp.float32),
         ]
         + traffic.out_shapes(),
         in_specs=[resident(padded.shape), resident(taps.shape), resident(norms.shape)]
@@ -1020,6 +1255,8 @@
         out_specs=[
             pl.BlockSpec((BLOCK, C), lambda step: (step, 0)),
             pl.BlockSpec((BLOCK, C), lambda step: (step, 0)),
+            pl.BlockSpec((BLOCK, 1), lambda step: (step, 0)),
+            pl.BlockSpec((BLOCK, 1), lambda step: (step, 0)),
         ]
         + traffic.out_specs(),
         scratch_shapes=traffic.scratch(),
@@ -1033,7 +1270,8 @@
     (g_first_ref, g_second_ref, g_taps_ref), refs = refs[:3], refs[3:]
     outs, refs = refs[:moved], refs[moved:]
     sums, refs = refs[0], refs[1:]
-    run_plan(traffic.plan(ins, outs, refs), pl.program_id(0), C // LANES)
+    step = pl.program_id(0)
+    run_plan(traffic, ins, outs, refs, step, C // LANES)
     sums[...] = jnp.zeros_like(sums)
 
     @pl.loop(0, CONV_BLOCKS)
@@ -1060,6 +1298,8 @@
 
     for tap in range(KERNEL):
         g_taps_ref[tap : tap + 1, :] = jnp.sum(sums[8 * tap : 8 * tap + 8, :], axis=0, keepdims=True)
+
+    run_plan(traffic, ins, outs, refs, step, C // LANES, late=True)
 
 
 def convolve_back(change, gated, paired, taps, traffic):
@@ -1179,7 +1419,7 @@
             0,
             shards=shard_of[:2] + [pack_small(small, small_shapes)],
             swapped=[frames_in],
-            swap_at=2,
+            swap_at=3.0,
         )
     )
     w_early_in, w_early_out = as_weight(gathered[0], early_in), as_weight(gathered[1], early_out)
@@ -1207,30 +1447,23 @@
     def parts(grad, like):
         return as_parts(grad, sizes, like)
 
-    def in_order(mine, other):
-        return jnp.where(
-            core == 0,
-            jnp.concatenate([mine, other], axis=0),
-            jnp.concatenate([other, mine], axis=0),
-        )
-
-    def halves(whole):
-        first, second = whole[:rows], whole[rows:]
-        return jnp.where(core == 0, first, second), jnp.where(core == 0, second, first)
-
     hidden0 = jnp.where(masked, mask_full[None, :], frames_here.astype(jnp.float32))
     hidden1, inner1, normed1, normed2, *gathered = ffn(
-        hidden0, norms_of(0, 1), w_early_in, w_early_out, Traffic(sizes, 1, shards=shard_of[2:4])
+        hidden0,
+        norms_of(0, 1),
+        w_early_in,
+        w_early_out,
+        Traffic(sizes, 1, shards=shard_of[2:4], swapped=[cotangent], swap_at=3.0, pace=2.0),
     )
     w_qkv, w_mixer = as_weight(gathered[0], qkv_weight), as_weight(gathered[1], mixer_out)
+    upstream = gathered[2].reshape(rows, D).astype(jnp.float32)
     packed = product(normed2, w_qkv).astype(jnp.bfloat16)
-    key_values = in_order(packed[:, D:], from_other(packed[:, D:]))
+    far = from_other(packed[:, D:])
     mixed_rows, log_total, *gathered = attend(
-        packed, key_values, offsets, Traffic(sizes, 2, shards=shard_of[4:6], swapped=[cotangent], swap_at=3)
+        packed, far, offsets, Traffic(sizes, 2, shards=shard_of[4:6], split=6, pace=1.15)
     )
     w_point_in = as_weight(gathered[0], pointwise_in)
     w_point_out = as_weight(gathered[1], pointwise_out)
-    upstream = gathered[2].reshape(rows, D).astype(jnp.float32)
     hidden2 = hidden1 + product(mixed_rows, w_mixer)
 
     normed3 = layer_norm(hidden2, gains[2], biases[2]).astype(jnp.bfloat16)
@@ -1248,8 +1481,8 @@
     padded = with_edges(gated)
     taps = jnp.pad(kernel_full, ((0, 1), (0, 0)))
     channel_norms = jnp.pad(jnp.stack([channel_gain, channel_bias]), ((0, 6), (0, 0)))
-    depth_values, post, *gathered = convolve(
-        padded, taps, channel_norms, Traffic(sizes, 3, shards=shard_of[6:])
+    depth_values, post, depth_mean, depth_rstd, *gathered = convolve(
+        padded, taps, channel_norms, Traffic(sizes, 3, shards=shard_of[6:], split=6, pace=2.4)
     )
     w_late_in, w_late_out = as_weight(gathered[0], late_in), as_weight(gathered[1], late_out)
     hidden3 = hidden2 + product(post, w_point_out)
@@ -1264,8 +1497,18 @@
     grad_out3 = grad3.astype(jnp.bfloat16)
     pointwise_out_grad = weight_grad(post, grad_out3)
     grad_post = back_product(grad_out3, w_point_out)
-    post_unused, post_pull = jax.vjp(depth_post, depth_values, channel_gain, channel_bias)
-    grad_depth, channel_gain_grad, channel_bias_grad = post_pull(grad_post)
+    scaled = (depth_values - depth_mean) * depth_rstd
+    shifted = scaled * channel_gain + channel_bias
+    gate = jax.nn.sigmoid(shifted)
+    grad_shifted = grad_post * gate * (1.0 + shifted * (1.0 - gate))
+    channel_gain_grad = jnp.sum(grad_shifted * scaled, axis=0)
+    channel_bias_grad = jnp.sum(grad_shifted, axis=0)
+    weighted = grad_shifted * channel_gain
+    grad_depth = depth_rstd * (
+        weighted
+        - jnp.mean(weighted, axis=-1, keepdims=True)
+        - scaled * jnp.mean(weighted * scaled, axis=-1, keepdims=True)
+    )
     grad_depth_low = grad_depth.astype(jnp.bfloat16)
     grad_first, grad_second, taps_grad, *sums_late = convolve_back(
         with_edges(grad_depth_low),
@@ -1273,7 +1516,10 @@
         paired,
         taps,
         Traffic(
-            sizes, 4, grads=[parts(late_out_grad, late_out), parts(late_in_grad, late_in)]
+            sizes,
+            4,
+            grads=[parts(late_out_grad, late_out), parts(late_in_grad, late_in)],
+            split=6,
         ),
     )
     kernel_grad = taps_grad[:KERNEL]
@@ -1286,9 +1532,9 @@
     grad_out2 = grad2.astype(jnp.bfloat16)
     mixer_out_grad = weight_grad(mixed_rows, grad_out2)
     grad_mixed = back_product(grad_out2, w_mixer).astype(jnp.bfloat16)
-    grad_queries, grad_keys, grad_values, near, far_sums, *sums_depth = attend_back(
+    grad_queries, keys_own, values_own, keys_far, values_far, near, far_sums, *sums_depth = attend_back(
         packed,
-        key_values,
+        far,
         offsets,
         log_total,
         grad_mixed,
@@ -1296,13 +1542,11 @@
             sizes,
             5,
             grads=[parts(pointwise_out_grad, pointwise_out), parts(pointwise_in_grad, pointwise_in)],
-            swapped=[activations.reshape(groups, run, D)],
+            split=6,
         ),
     )
     table_grad = table_back(near, far_sums, core * (rows // QB)).reshape(H * NB)
-    keys_own, keys_other = halves(grad_keys)
-    values_own, values_other = halves(grad_values)
-    keys_there, values_there = from_other(keys_other), from_other(values_other)
+    keys_there, values_there = from_other(keys_far), from_other(values_far)
     grad_packed = jnp.concatenate(
         [
             grad_queries,
@@ -1323,7 +1567,13 @@
         inner1,
         w_early_in,
         w_early_out,
-        Traffic(sizes, 6, grads=[parts(mixer_out_grad, mixer_out), parts(qkv_grad, qkv_weight)]),
+        Traffic(
+            sizes,
+            6,
+            grads=[parts(mixer_out_grad, mixer_out), parts(qkv_grad, qkv_weight)],
+            swapped=[activations.reshape(groups, run, D)],
+            pace=1.3,
+        ),
     )
     grad_frames = jnp.where(masked, 0.0, grad0).astype(jnp.bfloat16)
     mask_grad = jnp.sum(jnp.where(masked, grad0, 0.0), axis=0)
@@ -1354,7 +1604,7 @@
         small_out.append(small_sums[at : at + size].reshape(shape))
         at += size
     return (
-        sums_depth[2],
+        sums_mixer[2],
         sums_early[3].astype(jnp.float32),
         small_out[0],
         small_out[1],

time: 912 us -> 846 us (0.928)
  Pallas kernels: 715 us -> 661 us
  other arithmetic: 57.1 us -> 43.9 us
    pallas_call x1, Pallas kernels: 93.5 us -> 74.5 us  [convolve(): pl.pallas_call(functools.partial(conv_kernel, traffic), grid=(CONV_BLOCKS...]
    select_n x3 -> x0, other arithmetic: 11.5 us -> none  [the longest x1 7.26 us: in_order(): jnp.where(core == 0, jnp.concatenate([mine, other], axis=0), jnp.concaten...]
    pallas_call x1, Pallas kernels: 92.7 us -> 82 us  [convolve_back(): pl.pallas_call(functools.partial(conv_back_kernel, traffic), grid=(half,)...]
    pallas_call x1, Pallas kernels: 99.1 us -> 89.4 us  [attend_back(): pl.pallas_call(functools.partial(attend_back_kernel, rows, length, traffi...]
    pallas_call x2, Pallas kernels: 107 us -> 98.2 us  [ffn_back(): pl.pallas_call(functools.partial(ffn_back_kernel, traffic), grid=(FFN_STE...]
    unnamed x135 -> x125, local copies, waits for them, and re-layouts: 21.3 us -> 20.5 us
  transfers between devices with their start and end apart: 6 -> 6, of which waited for: 1 -> 1; matrix products, arithmetic and copies ran while one was open for 5% -> 5% of each run, Pallas kernels for 9% -> 10%
where the time goes in v3:
time: 846 us; the launch traced here: 841 us
  Pallas kernels  661 us (78%)
  matrix products  81.8 us (10%)
  local copies, waits for them, and re-layouts  46.2 us (5%)
  other arithmetic  43.9 us (5%)
    pallas_call x2, Pallas kernels, move(): pl.pallas_call(functools.partial(traffic_kernel, traffic), out_shape=traf...  165 us
    pallas_call x2, Pallas kernels, ffn_back(): pl.pallas_call(functools.partial(ffn_back_kernel, traffic), grid=(FFN_STE...  98.2 us
    pallas_call x1, Pallas kernels, attend_back(): pl.pallas_call(functools.partial(attend_back_kernel, rows, length, traffi...  89.4 us
    pallas_call x1, Pallas kernels, convolve_back(): pl.pallas_call(functools.partial(conv_back_kernel, traffic), grid=(half,)...  82 us
    pallas_call x2, Pallas kernels, ffn(): pl.pallas_call(functools.partial(ffn_kernel, traffic), grid=(FFN_STEPS,),...  76.4 us
    pallas_call x1, Pallas kernels, attend(): pl.pallas_call(functools.partial(attend_kernel, rows, length, traffic), g...  75.6 us
    pallas_call x1, Pallas kernels, convolve(): pl.pallas_call(functools.partial(conv_kernel, traffic), grid=(CONV_BLOCKS...  74.5 us
    dot_general x4, matrix products, weight_grad(): lax.dot_general(operand_a, operand_b, (((0,), (0,)), ((), ())), preferred...  27.9 us
  transfers between devices with their start and end apart: 6, of which 1 were waited for; matrix products, arithmetic and copies ran while one was open for 5% of the time, Pallas kernels for 10%

profile of v3, /device:TPU:0, one launch (start us, length us, event | category | flops | bytes accessed | tf_op | source)
XLA Modules:
  0.0 841.0 jit_solution(12585127777821495711)
XLA Ops:
  3.5 2.8 concatenate.23
  6.9 83.8 %shard_map.305 = (bf16[4,2,4,32,4096]{4,3,2,1,0:T(8,128)(2,1)}, bf16[4,2,4,128,1024]{4,3,2,1,0:T(8,128)(2,1)}, bf16[4,2,4,16,512]{4,3,2,1,0:T(8,128)(2,1)}, bf16[2,320,1024]{2,1,0:T(8,128)(2,1)}) custom-call(bf16[32,4096]{1,0:T(8,128)(2,1)} %refs_0_.4, bf16[128,1024]{1,0:T(8,128)(2,1)} %refs_1_.4, bf16[16,512]{1,0:T(8,128)(2,1)} %reshape.662.refs_2_, ...), custom_call_target="tpu_custom_call" | custom-call | tf_op jit(solution)/shard_map/pallas_call | solution.py:604
  96.1 53.3 %shard_map.306 = (f32[640,1024]{1,0:T(8,128)}, bf16[640,4096]{1,0:T(8,128)(2,1)}, bf16[640,1024]{1,0:T(8,128)(2,1)}, bf16[640,1024]{1,0:T(8,128)(2,1)}, bf16[4,2...) custom-call(f32[640,1024]{1,0:T(8,128)} %convert_select_fusion.hidden_ref, ...), custom_call_target="tpu_custom_call" | custom-call | tf_op jit(solution)/shard_map/pallas_call | solution.py:746
  149.5 7.4 convolution_convert_fusion.3.q_ref.k_own_ref.v_own_ref
  159.6 3.3 collective-permute-start.1
  175.5 75.6 %shard_map.307 = (bf16[640,1024]{1,0:T(8,128)(2,1)}, f32[40,1,256]{2,1,0:T(1,128)}, bf16[4,2,4,32,4096]{4,3,2,1,0:T(8,128)(2,1)}, bf16[4,2,4,64,1024]{4,3,2,1,0:T(8,128)(2,1)}) custom-call(f32[8,8,128]{2,1,0:T(8,128)} %reshape.667.rows_ref, bf16[640,3072]{1,0:T(8,128)(2,1)} %copy-done, bf16[640,3072]{1,0:T(8,128)(2,1)} %copy-done, ...), custom_call_target="tpu_custom_call" | custom-call | tf_op jit(solution)/shard_map/pallas_call | solution.py:975
  251.1 3.7 fusion.55
  255.4 7.6 fusion.56
  267.7 74.5 %shard_map.308 = (f32[640,2048]{1,0:T(8,128)}, bf16[640,2048]{1,0:T(8,128)(2,1)}, f32[640,1]{1,0:T(8,128)}, f32[640,1]{1,0:T(8,128)}, bf16[4,2,4,32,4096]{4,3,2,...) custom-call(bf16[672,2048]{1,0:T(8,128)(2,1)} %pad_maximum_fusion.1.padded_ref.gated_ref, ...), custom_call_target="tpu_custom_call" | custom-call | tf_op jit(solution)/shard_map/pallas_call | solution.py:1243
  344.6 7.4 convolution_add_fusion.hidden_ref
  351.9 23.1 %shard_map.309 = (f32[640,1024]{1,0:T(8,128)}, bf16[640,4096]{1,0:T(8,128)(2,1)}, bf16[640,1024]{1,0:T(8,128)(2,1)}, bf16[640,1024]{1,0:T(8,128)(2,1)}) custom-call(f32[640,1024]{1,0:T(8,128)} %convolution_add_fusion.hidden_ref, f32[8,1024]{1,0:T(8,128)} %stack.52.norms_ref, bf16[1024,4096]{1,0:T(8,128)(2,1)} %bitcast.107, bf16[4096,1024]{1,0:T(8,128)(2,1)} %bitcast.109), custom_call_target="tpu_custom_call" | custom-call | tf_op jit(solution)/shard_map/pallas_call | solution.py:746
  375.0 2.1 reduce_sum.212
  377.5 2.1 multiply_reduce_fusion.8
  381.0 2.3 broadcast_add_fusion.grad_ref
  383.3 37.0 %shard_map.310 = (f32[640,1024]{1,0:T(8,128)}, bf16[1024,4096]{1,0:T(8,128)(2,1)}, bf16[4096,1024]{1,0:T(8,128)(2,1)}, f32[8,1024]{1,0:T(8,128)}) custom-call(f32[640,1024]{1,0:T(8,128)} %convolution_add_fusion.hidden_ref, bf16[640,1024]{1,0:T(8,128)(2,1)} %get-tuple-element.86.normed_ref, f32[640,1024]{1,0:T(8,128)} %broadcast_add_fusion.grad_ref, ...), custom_call_target="tpu_custom_call" | custom-call | tf_op jit(solution)/shard_map/pallas_call | solution.py:826
  420.3 9.1 %multiply_reduce_fusion = (bf16[2048]{0:T(1024)(128)(2,1)S(1)}, f32[640]{0:T(1024)S(1)}, f32[640]{0:T(1024)S(1)}, bf16[2048]{0:T(1024)(128)(2,1)S(1)}, f32[640,2048]{1,0:T(8,128)S(1)}) fusion(f32[640,2048]{1,0:T(8,128)} %get-tuple-element.92, f32[640]{0:T(1024)S(1)} %reduce.4, f32[640]{0:T(1024)S(1)} %reduce.3, f32[2048]{0:T(1024)S(1)} %reshape.699, ...), kind=kOutput, calls=%fused_computation.8 | convolution fusion | flops 2709908480 | bytes 17336320 | tf_op jit(solution)/shard_map/dot_general | solution.py:648
  432.0 5.1 convolution_convert_fusion.4
  439.0 82.0 %shard_map.311 = (bf16[640,2048]{1,0:T(8,128)(2,1)}, bf16[640,2048]{1,0:T(8,128)(2,1)}, f32[32,2048]{1,0:T(8,128)}, f32[128,1024]{1,0:T(8,128)}, f32[32,4096]{1,0:T(8,128)}) custom-call(bf16[672,2048]{1,0:T(8,128)(2,1)} %pad_maximum_fusion.2.change_ref, bf16[672,2048]{1,0:T(8,128)(2,1)} %pad_maximum_fusion.1.padded_ref.gated_ref, ...), custom_call_target="tpu_custom_call" | custom-call | tf_op jit(solution)/shard_map/pallas_call | solution.py:1310
  521.0 2.2 constant_dynamic-update-slice_fusion.1
  525.3 8.7 %multiply_reduce_fusion.3 = (bf16[1024]{0:T(1024)(128)(2,1)S(1)}, f32[640]{0:T(1024)S(1)}, bf16[1024]{0:T(1024)(128)(2,1)S(1)}, f32[640,1024]{1,0:T(8,128)S(1)}) fusion(f32[640,1024]{1,0:T(8,128)S(1)} %copy-done.9, f32[640]{0:T(1024)S(1)} %fusion.38, f32[640]{0:T(1024)S(1)} %broadcast_multiply_fusion.4, f32[1024]{0:T(1024)S(1)} %mul.248, ...), kind=kOutput, calls=%fused_computation.31 | convolution fusion | flops 5373949440 | bytes 18890240 | tf_op jit(solution)/shard_map/dot_general | solution.py:648
  534.0 9.7 %convolution_convert_fusion = bf16[1024,4096]{1,0:T(8,128)(2,1)} fusion(bf16[640,4096]{1,0:T(8,128)(2,1)S(1)} %constant_dynamic-update-slice_fusion, f32[640,1024]{1,0:T(8,128)S(1)} %copy-done.9, f32[1024]{0:T(1024)S(1)} %add.298, f32[1024]{0:T(1024)S(1)} %mul.248, f32[640]{0:T(1024)S(1)} %fusion.38, f32[640]{0:T(1024)S(1)} %broadcast_multiply_fusion.4), kind=kOutput, calls=%fused_computation | convolution fusion | flops 5376180224 | bytes 16266240 | tf_op jit(solution)/shard_map/dot_general | solution.py:642
  546.2 2.6 convolution_convert_fusion.6.g_ref
  548.8 89.4 %shard_map.312 = (bf16[640,1024]{1,0:T(8,128)(2,1)}, bf16[640,1024]{1,0:T(8,128)(2,1)}, bf16[640,1024]{1,0:T(8,128)(2,1)}, bf16[640,1024]{1,0:T(8,128)(2,1)}, bf...) custom-call(f32[8,8,128]{2,1,0:T(8,128)} %reshape.667.rows_ref, ...), custom_call_target="tpu_custom_call" | custom-call | tf_op jit(solution)/shard_map/pallas_call | solution.py:1113
  651.7 5.5 convolution_convert_fusion.5
  657.2 2.0 add_convert_fusion.1
  659.3 2.0 add_convert_fusion
  661.3 7.6 convolution_convert_fusion.2
  668.9 4.8 multiply_reduce_fusion.4
  677.3 61.2 %shard_map.313 = (f32[640,1024]{1,0:T(8,128)}, bf16[1024,4096]{1,0:T(8,128)(2,1)}, bf16[4096,1024]{1,0:T(8,128)(2,1)}, f32[8,1024]{1,0:T(8,128)}, f32[32,1024]{1...) custom-call(f32[640,1024]{1,0:T(8,128)} %convert_select_fusion.hidden_ref, ...), custom_call_target="tpu_custom_call" | custom-call | tf_op jit(solution)/shard_map/pallas_call | solution.py:826
  738.5 2.2 select_reduce_fusion
  744.5 81.1 %shard_map.314 = (f32[128,1024]{1,0:T(8,128)}, f32[32,4096]{1,0:T(8,128)}, f32[16,512]{1,0:T(8,128)}, bf16[2,320,1024]{2,1,0:T(8,128)(2,1)}) custom-call(bf16[4,2,4,128,1024]{4,3,2,1,0:T(8,128)(2,1)} %bitcast.112, bf16[4,2,4,32,4096]{4,3,2,1,0:T(8,128)(2,1)} %bitcast.111, bf16[4,2,4,16,512]{4,3,2,1,0:T(8,128)(2,1)} %bitcast.121, bf16[2,320,1024]{2,1,0:T(8,128)(2,1)} %bitcast.117), custom_call_target="tpu_custom_call" | custom-call | tf_op jit(solution)/shard_map/pallas_call | solution.py:604
  830.4 3.2 convert_element_type.338
  (286 shorter events, 74.8 us)
Async XLA Ops:
  0.7 93.3 %copy-start.40 = (s32[2,640]{1,0:T(2,128)S(1)}, s32[2,640]{1,0:T(2,128)}, u32[]{:S(2)}) copy-start(s32[2,640]{1,0:T(2,128)} %param.19) | copy-start | bytes 15364
  0.7 93.3 %collective-permute-start = (s32[2,640]{1,0:T(2,128)}, s32[2,640]{1,0:T(2,128)S(1)}, u32[]{:S(2)}, u32[]{:S(2)}) collective-permute-start(s32[2,640]{1,0:T(2,128)} %param.19), channel_id=1, source_target_pairs={{0,4},{4,0},{8,12},{12,8},{16,20},{20,16},{24,28},{28,24},{1,5},{5... | collective-permute-start | bytes 15368 | tf_op jit(solution)/shard_map/ppermute | solution.py:1409
  90.7 3.6 copy-start.13
  94.3 55.2 %copy-start.38 = (pred[640]{0:T(1024)(128)(4,1)}, pred[640]{0:T(1024)(128)(4,1)S(1)}, u32[]{:S(2)}) copy-start(pred[640]{0:T(1024)(128)(4,1)S(1)} %compare_reduce_fusion) | copy-start | bytes 1924
  159.6 14.4 %collective-permute-start.1 = (bf16[640,2048]{1,0:T(8,128)(2,1)}, bf16[640,2048]{1,0:T(8,128)(2,1)S(1)}, u32[]{:S(2)}, u32[]{:S(2)}) collective-permute-start(bf16[640,2048]{1,0:T(8,128)(2,1)} %slice.211), channel_id=1, source_target_pairs={{0,4},{4,0},{8,12},{12,8},{16,20},{20,16},{24,28},{28,24},{1,5},{5... | collective-permute-start | bytes 7864328 | tf_op jit(solution)/shard_map/ppermute | solution.py:1409
  174.0 77.1 %copy-start.3 = (f32[640,1024]{1,0:T(8,128)S(1)}, f32[640,1024]{1,0:T(8,128)}, u32[]{:S(2)}) copy-start(f32[640,1024]{1,0:T(8,128)} %get-tuple-element.76) | copy-start | bytes 7864324
  251.0 4.4 copy-start.41
  254.8 89.8 %copy-start.8 = (f32[640,1024]{1,0:T(8,128)}, f32[640,1024]{1,0:T(8,128)S(1)}, u32[]{:S(2)}) copy-start(f32[640,1024]{1,0:T(8,128)S(1)} %get-tuple-element.176) | copy-start | bytes 7864324
  264.5 1.3 collective-permute-start.2
  383.3 37.0 %copy-start.42 = (bf16[4,2,4,64,1024]{4,3,2,1,0:T(8,128)(2,1)S(1)}, bf16[4,2,4,64,1024]{4,3,2,1,0:T(8,128)(2,1)}, u32[]{:S(2)}) copy-start(bf16[4,2,4,64,1024]{4,3,2,1,0:T(8,128)(2,1)} %get-tuple-element.83) | copy-start | bytes 12582916
  420.3 9.1 %slice-start = ((s8[5242880]{0:T(1024)(128)(4,1)}), s8[4194304]{0:T(1024)(128)(4,1)S(1)}, s32[]{:S(2)}) async-start(s8[5242880]{0:T(1024)(128)(4,1)} %bitcast.118), calls=%async_computation | async-start | bytes 8388608
  420.3 9.1 %slice-start.1 = ((s8[5242880]{0:T(1024)(128)(4,1)}), s8[1048576]{0:T(1024)(128)(4,1)S(1)}, s32[]{:S(2)}) async-start(s8[5242880]{0:T(1024)(128)(4,1)} %bitcast.118), calls=%async_computation.1 | async-start | bytes 2097152
  431.3 5.8 collective-permute-start.3
  548.8 89.6 %copy-start.4 = (f32[640,1024]{1,0:T(8,128)S(1)}, f32[640,1024]{1,0:T(8,128)}, u32[]{:S(2)}) copy-start(f32[640,1024]{1,0:T(8,128)} %get-tuple-element.76) | copy-start | bytes 7864324
  638.2 4.6 copy-start.28
  638.2 6.7 copy-start.26
  638.3 8.7 %copy-start.25 = (f32[8,12,128]{2,1,0:T(8,128)S(1)}, f32[8,12,128]{2,1,0:T(8,128)}, u32[]{:S(2)}) copy-start(f32[8,12,128]{2,1,0:T(8,128)} %get-tuple-element.113) | copy-start | bytes 147460
  638.3 19.0 %collective-permute-start.4 = (bf16[640,1024]{1,0:T(8,128)(2,1)}, bf16[640,1024]{1,0:T(8,128)(2,1)}, u32[]{:S(2)}, u32[]{:S(2)}) collective-permute-start(bf16[640,1024]{1,0:T(8,128)(2,1)} %get-tuple-element.101), channel_id=1, source_target_pairs={{0,4},{4,0},{8,12},{12,8},{16,20},{20,16},{24,28},{28,24},{1,5},{5... | collective-permute-start | bytes 3932168 | tf_op jit(solution)/shard_map/ppermute | solution.py:1409
  638.7 20.5 %collective-permute-start.5 = (bf16[640,1024]{1,0:T(8,128)(2,1)}, bf16[640,1024]{1,0:T(8,128)(2,1)}, u32[]{:S(2)}, u32[]{:S(2)}) collective-permute-start(bf16[640,1024]{1,0:T(8,128)(2,1)} %get-tuple-element.103), channel_id=1, source_target_pairs={{0,4},{4,0},{8,12},{12,8},{16,20},{20,16},{24,28},{28,24},{1,5},{5... | collective-permute-start | bytes 3932168 | tf_op jit(solution)/shard_map/ppermute | solution.py:1409
  651.7 5.5 copy-start.16
  651.7 9.5 %copy-start.46 = (bf16[640,1024]{1,0:T(8,128)(2,1)S(1)}, bf16[640,1024]{1,0:T(8,128)(2,1)}, u32[]{:S(2)}) copy-start(bf16[640,1024]{1,0:T(8,128)(2,1)} %get-tuple-element.99) | copy-start | bytes 3932164
  657.2 11.7 %slice-start.2 = ((s8[6291456]{0:T(1024)(128)(4,1)}), s8[4194304]{0:T(1024)(128)(4,1)S(1)}, s32[]{:S(2)}) async-start(s8[6291456]{0:T(1024)(128)(4,1)} %bitcast.151), calls=%async_computation.2 | async-start | bytes 8388608
  661.2 7.7 copy-start.36
  661.3 7.7 copy-start.37
  661.3 7.7 slice-start.3
  677.3 61.2 %copy-start.39 = (pred[640]{0:T(1024)(128)(4,1)S(1)}, pred[640]{0:T(1024)(128)(4,1)}, u32[]{:S(2)}) copy-start(pred[640]{0:T(1024)(128)(4,1)} %copy-done.38) | copy-start | bytes 1924
  825.6 8.0 copy-start.14
  830.4 4.3 copy-start.21
  833.6 4.1 copy-start.19
  834.6 3.8 copy-start.23
  834.6 4.5 copy-start.18
  834.6 5.3 copy-start.17
  (25 other events, 54.3 us)

commit v4 on v3

--- a/solution.py
+++ b/solution.py
@@ -685,9 +685,13 @@
     return centred * rstd, rstd
 
 
-def norm_chunk(values, norms_ref, which):
+def gain_row(rows_ref, which):
+    return rows_ref[1 + which : 2 + which, :]
+
+
+def norm_chunk(values, rows_ref, which):
     scaled, _ = norm_parts(values)
-    return scaled * norms_ref[2 * which : 2 * which + 1, :] + norms_ref[2 * which + 1 : 2 * which + 2, :]
+    return scaled * gain_row(rows_ref, which) + rows_ref[6 + which : 7 + which, :]
 
 
 def chunks(rows):
@@ -699,7 +703,7 @@
     return each
 
 
-def ffn_kernel(traffic, hidden_ref, norms_ref, w_in_ref, w_out_ref, *refs):
+def ffn_kernel(traffic, which, hidden_ref, norms_ref, w_in_ref, w_out_ref, *refs):
     moved = len(traffic.operands())
     ins, refs = refs[:moved], refs[moved:]
     out_ref, inner_ref, normed_ref, next_ref = refs[:4]
@@ -712,7 +716,7 @@
     @pl.when(step == 0)
     def _():
         def body(here):
-            normed_ref[here, :] = norm_chunk(hidden_ref[here, :], norms_ref, 0).astype(jnp.bfloat16)
+            normed_ref[here, :] = norm_chunk(hidden_ref[here, :], norms_ref, which).astype(jnp.bfloat16)
             total[here, :] = jnp.zeros((CHUNK, total.shape[1]), jnp.float32)
 
         each(body)
@@ -726,7 +730,7 @@
         def body(here):
             hidden = hidden_ref[here, :] + 0.5 * total[here, :]
             out_ref[here, :] = hidden
-            next_ref[here, :] = norm_chunk(hidden, norms_ref, 1).astype(jnp.bfloat16)
+            next_ref[here, :] = norm_chunk(hidden, norms_ref, which + 1).astype(jnp.bfloat16)
 
         each(body)
 
@@ -740,11 +744,11 @@
     return pl.BlockSpec(shape, lambda step: (0,) * len(shape))
 
 
-def ffn(hidden, norms, weight_in, weight_out, traffic):
+def ffn(hidden, norms, which, weight_in, weight_out, traffic):
     rows, width = hidden.shape
     tile = weight_in.shape[1] // FFN_STEPS
     return pl.pallas_call(
-        functools.partial(ffn_kernel, traffic),
+        functools.partial(ffn_kernel, traffic, which),
         grid=(FFN_STEPS,),
         out_shape=[
             jax.ShapeDtypeStruct((rows, width), jnp.float32),
@@ -773,7 +777,7 @@
 
 
 def ffn_back_kernel(
-    traffic, hidden_ref, normed_ref, grad_ref, norms_ref, inner_ref, w_in_ref, w_out_ref, *refs
+    traffic, which, hidden_ref, normed_ref, grad_ref, norms_ref, inner_ref, w_in_ref, w_out_ref, *refs
 ):
     moved = len(traffic.operands())
     ins, refs = refs[:moved], refs[moved:]
@@ -810,7 +814,7 @@
             upstream = total[here, :]
             sums_ref[0:1, :] += jnp.sum(upstream * scaled, axis=0, keepdims=True)
             sums_ref[1:2, :] += jnp.sum(upstream, axis=0, keepdims=True)
-            weighted = upstream * norms_ref[0:1, :]
+            weighted = upstream * gain_row(norms_ref, which)
             back = weighted - jnp.mean(weighted, axis=-1, keepdims=True)
             back = back - scaled * jnp.mean(weighted * scaled, axis=-1, keepdims=True)
             out_ref[here, :] = grad_ref[here, :] + rstd * back
@@ -820,11 +824,11 @@
     run_plan(traffic, ins, outs, refs, step, FFN_STEPS, late=True)
 
 
-def ffn_back(hidden, normed, grad, norms, inner, weight_in, weight_out, traffic):
+def ffn_back(hidden, normed, grad, norms, which, inner, weight_in, weight_out, traffic):
     rows, width = hidden.shape
     tile = weight_in.shape[1] // FFN_STEPS
     return pl.pallas_call(
-        functools.partial(ffn_back_kernel, traffic),
+        functools.partial(ffn_back_kernel, traffic, which),
         grid=(FFN_STEPS,),
         out_shape=[
             jax.ShapeDtypeStruct((rows, width), jnp.float32),
@@ -924,7 +928,7 @@
 ):
     moved = len(traffic.operands())
     ins, refs = refs[:moved], refs[moved:]
-    (out_ref, log_ref), refs = refs[:2], refs[2:]
+    (out_ref, exact_ref, log_ref), refs = refs[:3], refs[3:]
     outs, refs = refs[:moved], refs[moved:]
     (strip, score, prob, vt, k_all, v_all), refs = refs[:6], refs[6:]
     blocks = rows // QB
@@ -963,7 +967,8 @@
     )
     total = jnp.sum(total, axis=0, keepdims=True)
     mixed = dot_nn(vt[...], prob[...]) / total
-    out_ref[...] = own_halves(mixed).astype(out_ref.dtype)
+    exact_ref[...] = own_halves(mixed)
+    out_ref[...] = exact_ref[...].astype(out_ref.dtype)
     log_ref[0] = most + jnp.log(total)
     run_plan(traffic, ins, outs, refs, step, PAIRS * blocks, late=True)
 
@@ -977,6 +982,7 @@
         grid=(PAIRS, blocks),
         out_shape=[
             jax.ShapeDtypeStruct((rows, D), jnp.bfloat16),
+            jax.ShapeDtypeStruct((rows, D), jnp.float32),
             jax.ShapeDtypeStruct((PAIRS * blocks, 1, 2 * QB), jnp.float32),
         ]
         + traffic.out_shapes(),
@@ -990,6 +996,7 @@
         ]
         + traffic.in_specs(),
         out_specs=[
+            pl.BlockSpec((QB, 2 * DH), lambda p, b: (b, p)),
             pl.BlockSpec((QB, 2 * DH), lambda p, b: (b, p)),
             pl.BlockSpec((1, 1, 2 * QB), lambda p, b: (p * blocks + b, 0, 0)),
         ]
@@ -1018,6 +1025,7 @@
     k_far_ref,
     v_far_ref,
     g_ref,
+    mixed_ref,
     log_ref,
     *refs,
 ):
@@ -1051,23 +1059,20 @@
     slope[...] = dot_nt(v_all[...], g_both)
     log_total = log_ref[0]
 
-    def weigh(at, total):
-        here = pl.ds(pl.multiple_of(at * QB, QB), QB)
-        values = jnp.exp(
-            score[here, :] + strip[pl.ds(pl.multiple_of(start + at * QB, QB), QB), :] - log_total
-        )
-        score[here, :] = values
-        prob[here, :] = values.astype(jnp.bfloat16)
-        return total + jnp.sum((values * slope[here, :]).reshape(QB // 8, 8, 2 * QB), axis=0)
-
-    centre = lax.fori_loop(
-        0, length // QB, weigh, jnp.zeros((8, 2 * QB), jnp.float32), unroll=True
-    )
-    centre = jnp.sum(centre, axis=0, keepdims=True)
-
+    inner = (g_ref[...].astype(jnp.float32) * mixed_ref[...]).T
+    centre = jnp.concatenate(
+        [
+            jnp.sum(inner[:DH, :], axis=0, keepdims=True),
+            jnp.sum(inner[DH:, :], axis=0, keepdims=True),
+        ],
+        axis=1,
+    )
     for at in range(length // QB):
         here = pl.ds(at * QB, QB)
-        values = score[here, :] * (slope[here, :] - centre)
+        bias = strip[pl.ds(pl.multiple_of(start + at * QB, QB), QB), :]
+        weights = jnp.exp(score[here, :] + bias - log_total)
+        prob[here, :] = weights.astype(jnp.bfloat16)
+        values = weights * (slope[here, :] - centre)
         change[pl.ds(at * QB + QB, QB), :] = values.astype(jnp.bfloat16)
         sums_ref[0, at : at + 1, :] = jnp.sum(values, axis=0, keepdims=True)
 
@@ -1105,7 +1110,7 @@
     run_plan(traffic, ins, outs, refs, step, PAIRS * blocks, late=True)
 
 
-def attend_back(packed, far, offsets, log_total, grads, traffic):
+def attend_back(packed, far, offsets, mixed, log_total, grads, traffic):
     rows = packed.shape[0]
     length = 2 * rows
     blocks = rows // QB
@@ -1131,6 +1136,7 @@
             pl.BlockSpec((rows, 2 * DH), lambda p, b: (0, p)),
             pl.BlockSpec((rows, 2 * DH), lambda p, b: (0, PAIRS + p)),
             pl.BlockSpec((QB, 2 * DH), lambda p, b: (b, p)),
+            pl.BlockSpec((QB, 2 * DH), lambda p, b: (b, p)),
             pl.BlockSpec((1, 1, 2 * QB), lambda p, b: (p * blocks + b, 0, 0)),
         ]
         + traffic.in_specs(),
@@ -1159,7 +1165,7 @@
         ]
         + traffic.scratch(),
         compiler_params=traffic_params(traffic),
-    )(offsets, packed, packed, packed, far, far, grads, log_total, *traffic.operands())
+    )(offsets, packed, packed, packed, far, far, grads, mixed, log_total, *traffic.operands())
 
 
 def table_back(near, sums, first_block):
@@ -1205,7 +1211,7 @@
                 yield offset, turned[8 * high : 8 * high + BLOCK, :]
 
 
-def conv_kernel(traffic, padded_ref, taps_ref, norms_ref, *refs):
+def conv_kernel(traffic, padded_ref, channels_ref, *refs):
     moved = len(traffic.operands())
     ins, refs = refs[:moved], refs[moved:]
     (depth_ref, post_ref, mean_ref, rstd_ref), refs = refs[:4], refs[4:]
@@ -1220,7 +1226,7 @@
         window = padded_ref[pl.ds(first, BLOCK + 2 * EDGE), lanes].astype(jnp.float32)
         total = jnp.zeros((BLOCK, LANES), jnp.float32)
         for offset, rows in shifted_rows(window):
-            total = total + rows * taps_ref[offset - 1 : offset, lanes]
+            total = total + rows * channels_ref[offset + 1 : offset + 2, lanes]
         depth_ref[:, lanes] = total
 
     @pl.loop(0, BLOCK // 16)
@@ -1229,7 +1235,7 @@
         scaled, rstd = norm_parts(depth_ref[here, :])
         mean_ref[here, :] = jnp.mean(depth_ref[here, :], axis=-1, keepdims=True)
         rstd_ref[here, :] = rstd
-        normed = scaled * norms_ref[0:1, :] + norms_ref[1:2, :]
+        normed = scaled * channels_ref[0:1, :] + channels_ref[1:2, :]
         post_ref[here, :] = (normed * sigmoid(normed)).astype(jnp.bfloat16)
 
     run_plan(traffic, ins, outs, refs, step, CONV_BLOCKS, late=True)
@@ -1238,7 +1244,7 @@
 CONV_BLOCKS = 5
 
 
-def convolve(padded, taps, norms, traffic):
+def convolve(padded, channels, traffic):
     rows = padded.shape[0] - 2 * EDGE
     return pl.pallas_call(
         functools.partial(conv_kernel, traffic),
@@ -1250,7 +1256,7 @@
             jax.ShapeDtypeStruct((rows, 1), jnp.float32),
         ]
         + traffic.out_shapes(),
-        in_specs=[resident(padded.shape), resident(taps.shape), resident(norms.shape)]
+        in_specs=[resident(padded.shape), resident(channels.shape)]
         + traffic.in_specs(),
         out_specs=[
             pl.BlockSpec((BLOCK, C), lambda step: (step, 0)),
@@ -1261,10 +1267,10 @@
         + traffic.out_specs(),
         scratch_shapes=traffic.scratch(),
         compiler_params=traffic_params(traffic),
-    )(padded, taps, norms, *traffic.operands())
-
-
-def conv_back_kernel(traffic, change_ref, gated_ref, first_ref, second_ref, taps_ref, *refs):
+    )(padded, channels, *traffic.operands())
+
+
+def conv_back_kernel(traffic, change_ref, gated_ref, first_ref, second_ref, channels_ref, *refs):
     moved = len(traffic.operands())
     ins, refs = refs[:moved], refs[moved:]
     (g_first_ref, g_second_ref, g_taps_ref), refs = refs[:3], refs[3:]
@@ -1282,7 +1288,7 @@
         window = change_ref[around, :].astype(jnp.float32)
         total = jnp.zeros((BLOCK, LANES), jnp.float32)
         for offset, rows in shifted_rows(window):
-            total = total + rows * taps_ref[KERNEL - offset : KERNEL - offset + 1, :]
+            total = total + rows * channels_ref[KERNEL - offset + 2 : KERNEL - offset + 3, :]
         gate = sigmoid(second_ref[here, :].astype(jnp.float32))
         through = total * gate
         g_first_ref[here, :] = through.astype(jnp.bfloat16)
@@ -1302,7 +1308,7 @@
     run_plan(traffic, ins, outs, refs, step, C // LANES, late=True)
 
 
-def convolve_back(change, gated, paired, taps, traffic):
+def convolve_back(change, gated, paired, channels, traffic):
     rows = change.shape[0] - 2 * EDGE
     half = C // LANES
     column = pl.BlockSpec((rows, LANES), lambda step: (0, step))
@@ -1313,7 +1319,7 @@
         out_shape=[
             jax.ShapeDtypeStruct((rows, C), jnp.bfloat16),
             jax.ShapeDtypeStruct((rows, C), jnp.bfloat16),
-            jax.ShapeDtypeStruct((KERNEL + 1, C), jnp.float32),
+            jax.ShapeDtypeStruct((KERNEL, C), jnp.float32),
         ]
         + traffic.out_shapes(),
         in_specs=[
@@ -1321,14 +1327,14 @@
             edged,
             column,
             pl.BlockSpec((rows, LANES), lambda step: (0, half + step)),
-            pl.BlockSpec((KERNEL + 1, LANES), lambda step: (0, step)),
+            pl.BlockSpec((KERNEL + 2, LANES), lambda step: (0, step)),
         ]
         + traffic.in_specs(),
-        out_specs=[column, column, pl.BlockSpec((KERNEL + 1, LANES), lambda step: (0, step))]
+        out_specs=[column, column, pl.BlockSpec((KERNEL, LANES), lambda step: (0, step))]
         + traffic.out_specs(),
         scratch_shapes=[pltpu.VMEM((8 * KERNEL, LANES), jnp.float32)] + traffic.scratch(),
         compiler_params=traffic_params(traffic),
-    )(change, gated, paired, paired, taps, *traffic.operands())
+    )(change, gated, paired, paired, channels, *traffic.operands())
 
 
 def as_shard(array):
@@ -1352,25 +1358,16 @@
     return jnp.pad(flat, (0, SMALL[0] * SMALL[1] - flat.shape[0])).reshape(SMALL)
 
 
-def unpack_small(packed, shapes):
+def unpack_small(packed, at, many):
+    count, size = many
     devices = packed.shape[0]
-    at, out = 0, []
-    for shape in shapes:
-        size = math.prod(shape)
-        piece = packed[:, at : at + size].reshape((devices,) + shape)
-        at += size
-        piece = jnp.moveaxis(piece, 0, -2)
-        out.append(piece.reshape(shape[:-1] + (devices * shape[-1],)))
-    return out
-
-
-def repack_small(values, shapes, devices):
-    pieces = []
-    for value, shape in zip(values, shapes):
-        piece = value.reshape(shape[:-1] + (devices, shape[-1]))
-        pieces.append(jnp.moveaxis(piece, -2, 0).reshape(devices, -1))
-    flat = jnp.concatenate(pieces, axis=1)
-    return jnp.pad(flat, ((0, 0), (0, SMALL[0] * SMALL[1] - flat.shape[1])))
+    piece = packed[:, at : at + count * size].reshape(devices, count, size).astype(jnp.float32)
+    return jnp.moveaxis(piece, 0, 1).reshape(count, devices * size)
+
+
+def repack_small(rows, devices):
+    count = rows.shape[0]
+    return jnp.moveaxis(rows.reshape(count, devices, -1), 1, 0).reshape(devices, -1)
 
 
 def shards(
@@ -1424,10 +1421,15 @@
     )
     w_early_in, w_early_out = as_weight(gathered[0], early_in), as_weight(gathered[1], early_out)
     small_whole = gathered[2].reshape(devices, SMALL[0] * SMALL[1])
-    mask_full, gains, biases, channel_gain, channel_bias, kernel_full, table = [
-        value.astype(jnp.float32) for value in unpack_small(small_whole, small_shapes)
-    ]
-    table = table.reshape(H, NB)
+    model_rows = (1 + 2 * norm_gains.shape[0], mask_vector.shape[0])
+    channel_rows = (2 + KERNEL, depth_gain.shape[0])
+    channels_at = math.prod(model_rows)
+    table_at = channels_at + math.prod(channel_rows)
+    vectors = unpack_small(small_whole, 0, model_rows)
+    channels = unpack_small(small_whole, channels_at, channel_rows)
+    table = unpack_small(small_whole, table_at, (1, position_bias.shape[0])).reshape(H, NB)
+    mask_full, gains, biases = vectors[0], vectors[1:6], vectors[6:11]
+    channel_gain, channel_bias = channels[0], channels[1]
     frames_here = gathered[3].reshape(rows, D)
 
     both = jnp.where(core == 0, 0, 1)
@@ -1440,17 +1442,14 @@
 
     offsets = offset_rows(table)
 
-    def norms_of(*which):
-        rows_of = [row for at in which for row in (gains[at], biases[at])]
-        return jnp.stack(rows_of + [jnp.zeros((D,), jnp.float32)] * (8 - len(rows_of)))
-
     def parts(grad, like):
         return as_parts(grad, sizes, like)
 
     hidden0 = jnp.where(masked, mask_full[None, :], frames_here.astype(jnp.float32))
     hidden1, inner1, normed1, normed2, *gathered = ffn(
         hidden0,
-        norms_of(0, 1),
+        vectors,
+        0,
         w_early_in,
         w_early_out,
         Traffic(sizes, 1, shards=shard_of[2:4], swapped=[cotangent], swap_at=3.0, pace=2.0),
@@ -1459,8 +1458,8 @@
     upstream = gathered[2].reshape(rows, D).astype(jnp.float32)
     packed = product(normed2, w_qkv).astype(jnp.bfloat16)
     far = from_other(packed[:, D:])
-    mixed_rows, log_total, *gathered = attend(
-        packed, far, offsets, Traffic(sizes, 2, shards=shard_of[4:6], split=6, pace=1.15)
+    mixed_rows, mixed_exact, log_total, *gathered = attend(
+        packed, far, offsets, Traffic(sizes, 2, shards=shard_of[4:6], pace=1.15)
     )
     w_point_in = as_weight(gathered[0], pointwise_in)
     w_point_out = as_weight(gathered[1], pointwise_out)
@@ -1479,20 +1478,18 @@
         )
 
     padded = with_edges(gated)
-    taps = jnp.pad(kernel_full, ((0, 1), (0, 0)))
-    channel_norms = jnp.pad(jnp.stack([channel_gain, channel_bias]), ((0, 6), (0, 0)))
     depth_values, post, depth_mean, depth_rstd, *gathered = convolve(
-        padded, taps, channel_norms, Traffic(sizes, 3, shards=shard_of[6:], split=6, pace=2.4)
+        padded, channels, Traffic(sizes, 3, shards=shard_of[6:], split=6, pace=2.4)
     )
     w_late_in, w_late_out = as_weight(gathered[0], late_in), as_weight(gathered[1], late_out)
     hidden3 = hidden2 + product(post, w_point_out)
     hidden4, inner5, normed5, activations = ffn(
-        hidden3, norms_of(3, 4), w_late_in, w_late_out, Traffic(sizes, None)
+        hidden3, vectors, 3, w_late_in, w_late_out, Traffic(sizes, None)
     )
 
     grad4, gain_grad4, bias_grad4 = norm_back(hidden4, gains[4], biases[4], upstream)
     grad3, late_in_grad, late_out_grad, norm_sums3 = ffn_back(
-        hidden3, normed5, grad4, norms_of(3), inner5, w_late_in, w_late_out, Traffic(sizes, None)
+        hidden3, normed5, grad4, vectors, 3, inner5, w_late_in, w_late_out, Traffic(sizes, None)
     )
     grad_out3 = grad3.astype(jnp.bfloat16)
     pointwise_out_grad = weight_grad(post, grad_out3)
@@ -1514,7 +1511,7 @@
         with_edges(grad_depth_low),
         padded,
         paired,
-        taps,
+        channels,
         Traffic(
             sizes,
             4,
@@ -1522,7 +1519,6 @@
             split=6,
         ),
     )
-    kernel_grad = taps_grad[:KERNEL]
     grad_paired = jnp.concatenate([grad_first, grad_second], axis=1)
     pointwise_in_grad = weight_grad(normed3, grad_paired)
     grad_normed3 = back_product(grad_paired, w_point_in)
@@ -1536,13 +1532,13 @@
         packed,
         far,
         offsets,
+        mixed_exact,
         log_total,
         grad_mixed,
         Traffic(
             sizes,
             5,
             grads=[parts(pointwise_out_grad, pointwise_out), parts(pointwise_in_grad, pointwise_in)],
-            split=6,
         ),
     )
     table_grad = table_back(near, far_sums, core * (rows // QB)).reshape(H * NB)
@@ -1563,7 +1559,8 @@
         hidden0,
         normed1,
         grad1,
-        norms_of(0),
+        vectors,
+        0,
         inner1,
         w_early_in,
         w_early_out,
@@ -1577,13 +1574,37 @@
     )
     grad_frames = jnp.where(masked, 0.0, grad0).astype(jnp.bfloat16)
     mask_grad = jnp.sum(jnp.where(masked, grad0, 0.0), axis=0)
-    gain_stack = jnp.stack([norm_sums0[0], gain_grad1, gain_grad2, norm_sums3[0], gain_grad4])
-    bias_stack = jnp.stack([norm_sums0[1], bias_grad1, bias_grad2, norm_sums3[1], bias_grad4])
-    small_grads = repack_small(
-        [mask_grad, gain_stack, bias_stack, channel_gain_grad, channel_bias_grad, kernel_grad, table_grad],
-        small_shapes,
-        devices,
-    ).astype(jnp.bfloat16)
+    vector_grads = jnp.concatenate(
+        [
+            row.reshape(1, D)
+            for row in (
+                mask_grad,
+                norm_sums0[0],
+                gain_grad1,
+                gain_grad2,
+                norm_sums3[0],
+                gain_grad4,
+                norm_sums0[1],
+                bias_grad1,
+                bias_grad2,
+                norm_sums3[1],
+                bias_grad4,
+            )
+        ]
+    )
+    channel_grads = jnp.concatenate(
+        [channel_gain_grad.reshape(1, C), channel_bias_grad.reshape(1, C), taps_grad]
+    )
+    small_grads = jnp.concatenate(
+        [
+            repack_small(vector_grads, devices),
+            repack_small(channel_grads, devices),
+            table_grad.reshape(devices, -1),
+        ],
+        axis=1,
+    )
+    small_grads = jnp.pad(small_grads, ((0, 0), (0, SMALL[0] * SMALL[1] - small_size)))
+    small_grads = small_grads.astype(jnp.bfloat16)
 
     sums_early = move(
         Traffic(

time: 846 us -> 836 us (0.988)
  Pallas kernels: 661 us -> 648 us
    pallas_call x1, Pallas kernels: 89.4 us -> 77.9 us  [attend_back(): pl.pallas_call(functools.partial(attend_back_kernel, rows, length, traffi...]
    unnamed x125 -> x127, local copies, waits for them, and re-layouts: 20.5 us -> 20.9 us
  transfers between devices with their start and end apart: 6 -> 6, of which waited for: 1 -> 0; matrix products, arithmetic and copies ran while one was open for 5% -> 5% of each run, Pallas kernels for 10% -> 10%
where the time goes in v4:
time: 836 us; the launch traced here: 831 us
  Pallas kernels  648 us (78%)
  matrix products  84.5 us (10%)
  local copies, waits for them, and re-layouts  48.8 us (6%)
  other arithmetic  42.5 us (5%)
    pallas_call x2, Pallas kernels, move(): pl.pallas_call(functools.partial(traffic_kernel, traffic), out_shape=traf...  167 us
    pallas_call x2, Pallas kernels, ffn_back(): pl.pallas_call(functools.partial(ffn_back_kernel, traffic, which), grid=(...  94.3 us
    pallas_call x1, Pallas kernels, convolve_back(): pl.pallas_call(functools.partial(conv_back_kernel, traffic), grid=(half,)...  82 us
    pallas_call x1, Pallas kernels, attend_back(): pl.pallas_call(functools.partial(attend_back_kernel, rows, length, traffi...  77.9 us
    pallas_call x1, Pallas kernels, convolve(): pl.pallas_call(functools.partial(conv_kernel, traffic), grid=(CONV_BLOCKS...  76.9 us
    pallas_call x2, Pallas kernels, ffn(): pl.pallas_call(functools.partial(ffn_kernel, traffic, which), grid=(FFN_S...  76.3 us
    pallas_call x1, Pallas kernels, attend(): pl.pallas_call(functools.partial(attend_kernel, rows, length, traffic), g...  73.7 us
    dot_general x4, matrix products, product(): return jnp.dot(operand_a, operand_b, preferred_element_type=jnp.float32)  28.3 us
  transfers between devices with their start and end apart: 6, of which 0 were waited for; matrix products, arithmetic and copies ran while one was open for 5% of the time, Pallas kernels for 10%

profile of v4, /device:TPU:0, one launch (start us, length us, event | category | flops | bytes accessed | tf_op | source)
XLA Modules:
  0.0 830.7 jit_solution(10016452520224487492)
XLA Ops:
  3.6 2.8 concatenate.57
  7.0 83.8 %shard_map.305 = (bf16[4,2,4,32,4096]{4,3,2,1,0:T(8,128)(2,1)}, bf16[4,2,4,128,1024]{4,3,2,1,0:T(8,128)(2,1)}, bf16[4,2,4,16,512]{4,3,2,1,0:T(8,128)(2,1)}, bf16[2,320,1024]{2,1,0:T(8,128)(2,1)}) custom-call(bf16[32,4096]{1,0:T(8,128)(2,1)} %refs_0_.4, bf16[128,1024]{1,0:T(8,128)(2,1)} %refs_1_.4, bf16[16,512]{1,0:T(8,128)(2,1)} %reshape.617.refs_2_, ...), custom_call_target="tpu_custom_call" | custom-call | tf_op jit(solution)/shard_map/pallas_call | solution.py:604
  95.9 53.2 %shard_map.306 = (f32[640,1024]{1,0:T(8,128)}, bf16[640,4096]{1,0:T(8,128)(2,1)}, bf16[640,1024]{1,0:T(8,128)(2,1)}, bf16[640,1024]{1,0:T(8,128)(2,1)}, bf16[4,2...) custom-call(f32[640,1024]{1,0:T(8,128)} %convert_select_fusion.hidden_ref, ...), custom_call_target="tpu_custom_call" | custom-call | tf_op jit(solution)/shard_map/pallas_call | solution.py:750
  149.1 7.4 convolution_convert_fusion.3.q_ref.k_own_ref.v_own_ref
  159.2 3.2 collective-permute-start.1
  175.2 73.7 %shard_map.307 = (bf16[640,1024]{1,0:T(8,128)(2,1)}, f32[640,1024]{1,0:T(8,128)}, f32[40,1,256]{2,1,0:T(1,128)}, bf16[4,2,4,32,4096]{4,3,2,1,0:T(8,128)(2,1)}, bf16[4,2,4,64,1024]{4,3,2,1,0:T(8,128)(2,1)}) custom-call(f32[8,8,128]{2,1,0:T(8,128)} %reshape.622.rows_ref, bf16[640,3072]{1,0:T(8,128)(2,1)} %copy-done, bf16[640,3072]{1,0:T(8,128)(2,1)} %copy-done, ...), custom_call_target="tpu_custom_call" | custom-call | tf_op jit(solution)/shard_map/pallas_call | solution.py:980
  248.9 3.6 fusion.48
  253.2 9.9 %fusion.49 = (f32[640,4096]{1,0:T(8,128)S(1)}, bf16[640,4096]{1,0:T(8,128)(2,1)}) fusion(bf16[1024,4096]{1,0:T(8,128)(2,1)} %bitcast.132, f32[640,1024]{1,0:T(8,128)S(1)} %get-tuple-element.167, f32[1024]{0:T(1024)S(1)} %copy-done.41, f32[1024]{0:T(1024)S(1)} %copy-done.37, f32[640]{0:T(1024)S(1)} %fusion.34, f32[640]{0:T(1024)S(1)} %broadcast_multiply_fusion.4), kind=kOutput, calls=%fused_computation.164 | convolution fusion | flops 5377228800 | bytes 26752000 | tf_op jit(solution)/shard_map/dot_general | solution.py:638
  267.8 3.6 pad_maximum_fusion.1.padded_ref.gated_ref
  271.4 76.9 %shard_map.308 = (f32[640,2048]{1,0:T(8,128)}, bf16[640,2048]{1,0:T(8,128)(2,1)}, f32[640,1]{1,0:T(8,128)}, f32[640,1]{1,0:T(8,128)}, bf16[4,2,4,32,4096]{4,3,2,...) custom-call(bf16[672,2048]{1,0:T(8,128)(2,1)} %pad_maximum_fusion.1.padded_ref.gated_ref, ...), custom_call_target="tpu_custom_call" | custom-call | tf_op jit(solution)/shard_map/pallas_call | solution.py:1249
  350.6 7.3 convolution_add_fusion.hidden_ref
  358.0 23.2 %shard_map.309 = (f32[640,1024]{1,0:T(8,128)}, bf16[640,4096]{1,0:T(8,128)(2,1)}, bf16[640,1024]{1,0:T(8,128)(2,1)}, bf16[640,1024]{1,0:T(8,128)(2,1)}) custom-call(f32[640,1024]{1,0:T(8,128)} %convolution_add_fusion.hidden_ref, f32[11,1024]{1,0:T(8,128)} %reshape.619.norms_ref, bf16[1024,4096]{1,0:T(8,128)(2,1)} %bitcast.92, bf16[4096,1024]{1,0:T(8,128)(2,1)} %bitcast.94), custom_call_target="tpu_custom_call" | custom-call | tf_op jit(solution)/shard_map/pallas_call | solution.py:750
  381.1 2.1 reduce_sum.212
  383.7 2.1 multiply_reduce_fusion.8
  387.2 2.2 broadcast_add_fusion.grad_ref
  389.4 37.0 %shard_map.310 = (f32[640,1024]{1,0:T(8,128)}, bf16[1024,4096]{1,0:T(8,128)(2,1)}, bf16[4096,1024]{1,0:T(8,128)(2,1)}, f32[8,1024]{1,0:T(8,128)}) custom-call(f32[640,1024]{1,0:T(8,128)} %convolution_add_fusion.hidden_ref, bf16[640,1024]{1,0:T(8,128)(2,1)} %get-tuple-element.87.normed_ref, f32[640,1024]{1,0:T(8,128)} %broadcast_add_fusion.grad_ref, ...), custom_call_target="tpu_custom_call" | custom-call | tf_op jit(solution)/shard_map/pallas_call | solution.py:830
  426.4 9.1 %multiply_reduce_fusion = (bf16[2048]{0:T(1024)(128)(2,1)S(1)}, f32[640]{0:T(1024)S(1)}, f32[640]{0:T(1024)S(1)}, bf16[2048]{0:T(1024)(128)(2,1)S(1)}, f32[640,2048]{1,0:T(8,128)S(1)}) fusion(f32[640,2048]{1,0:T(8,128)} %get-tuple-element.93, f32[640]{0:T(1024)S(1)} %reduce.8, f32[640]{0:T(1024)S(1)} %reduce.7, f32[2048]{0:T(1024)S(1)} %mul.267, ...), kind=kOutput, calls=%fused_computation.8 | convolution fusion | flops 2709908480 | bytes 17336320 | tf_op jit(solution)/shard_map/dot_general | solution.py:648
  438.0 5.1 convolution_convert_fusion.4
  445.0 82.0 %shard_map.311 = (bf16[640,2048]{1,0:T(8,128)(2,1)}, bf16[640,2048]{1,0:T(8,128)(2,1)}, f32[31,2048]{1,0:T(8,128)}, f32[128,1024]{1,0:T(8,128)}, f32[32,4096]{1,0:T(8,128)}) custom-call(bf16[672,2048]{1,0:T(8,128)(2,1)} %pad_maximum_fusion.2.change_ref, bf16[672,2048]{1,0:T(8,128)(2,1)} %pad_maximum_fusion.1.padded_ref.gated_ref, ...), custom_call_target="tpu_custom_call" | custom-call | tf_op jit(solution)/shard_map/pallas_call | solution.py:1316
  527.1 2.2 constant_dynamic-update-slice_fusion.1
  531.4 8.7 %multiply_reduce_fusion.3 = (bf16[1024]{0:T(1024)(128)(2,1)S(1)}, f32[640]{0:T(1024)S(1)}, bf16[1024]{0:T(1024)(128)(2,1)S(1)}, f32[640,1024]{1,0:T(8,128)S(1)}) fusion(f32[640,1024]{1,0:T(8,128)S(1)} %copy-done.10, f32[640]{0:T(1024)S(1)} %fusion.34, f32[640]{0:T(1024)S(1)} %broadcast_multiply_fusion.4, f32[1024]{0:T(1024)S(1)} %copy-done.37, ...), kind=kOutput, calls=%fused_computation.31 | convolution fusion | flops 5373949440 | bytes 18890240 | tf_op jit(solution)/shard_map/dot_general | solution.py:648
  540.0 9.8 %convolution_convert_fusion = bf16[1024,4096]{1,0:T(8,128)(2,1)} fusion(bf16[640,4096]{1,0:T(8,128)(2,1)S(1)} %constant_dynamic-update-slice_fusion, f32[640,1024]{1,0:T(8,128)S(1)} %copy-done.10, f32[1024]{0:T(1024)S(1)} %copy-done.41, f32[1024]{0:T(1024)S(1)} %copy-done.37, f32[640]{0:T(1024)S(1)} %fusion.34, f32[640]{0:T(1024)S(1)} %broadcast_multiply_fusion.4), kind=kOutput, calls=%fused_computation | convolution fusion | flops 5376180224 | bytes 16266240 | tf_op jit(solution)/shard_map/dot_general | solution.py:642
  552.2 2.6 convolution_convert_fusion.6.g_ref
  554.9 77.9 %shard_map.312 = (bf16[640,1024]{1,0:T(8,128)(2,1)}, bf16[640,1024]{1,0:T(8,128)(2,1)}, bf16[640,1024]{1,0:T(8,128)(2,1)}, bf16[640,1024]{1,0:T(8,128)(2,1)}, bf...) custom-call(f32[8,8,128]{2,1,0:T(8,128)} %reshape.622.rows_ref, ...), custom_call_target="tpu_custom_call" | custom-call | tf_op jit(solution)/shard_map/pallas_call | solution.py:1118
  644.0 4.7 convolution_convert_fusion.5
  648.7 2.0 add_convert_fusion.1
  652.7 7.7 convolution_convert_fusion.2
  660.4 6.1 multiply_reduce_fusion.4
  669.4 57.4 %shard_map.313 = (f32[640,1024]{1,0:T(8,128)}, bf16[1024,4096]{1,0:T(8,128)(2,1)}, bf16[4096,1024]{1,0:T(8,128)(2,1)}, f32[8,1024]{1,0:T(8,128)}, f32[32,1024]{1...) custom-call(f32[640,1024]{1,0:T(8,128)} %convert_select_fusion.hidden_ref, ...), custom_call_target="tpu_custom_call" | custom-call | tf_op jit(solution)/shard_map/pallas_call | solution.py:830
  726.8 2.2 select_reduce_fusion
  732.6 82.7 %shard_map.314 = (f32[128,1024]{1,0:T(8,128)}, f32[32,4096]{1,0:T(8,128)}, f32[16,512]{1,0:T(8,128)}, bf16[2,320,1024]{2,1,0:T(8,128)(2,1)}) custom-call(bf16[4,2,4,128,1024]{4,3,2,1,0:T(8,128)(2,1)} %bitcast.102, bf16[4,2,4,32,4096]{4,3,2,1,0:T(8,128)(2,1)} %bitcast.101, bf16[4,2,4,16,512]{4,3,2,1,0:T(8,128)(2,1)} %bitcast.113, bf16[2,320,1024]{2,1,0:T(8,128)(2,1)} %bitcast.106), custom_call_target="tpu_custom_call" | custom-call | tf_op jit(solution)/shard_map/pallas_call | solution.py:604
  820.1 3.2 convert_element_type.253
  (257 shorter events, 73.5 us)
Async XLA Ops:
  0.7 93.1 %copy-start.42 = (s32[2,640]{1,0:T(2,128)S(1)}, s32[2,640]{1,0:T(2,128)}, u32[]{:S(2)}) copy-start(s32[2,640]{1,0:T(2,128)} %param.19) | copy-start | bytes 15364
  0.7 93.1 %collective-permute-start = (s32[2,640]{1,0:T(2,128)}, s32[2,640]{1,0:T(2,128)S(1)}, u32[]{:S(2)}, u32[]{:S(2)}) collective-permute-start(s32[2,640]{1,0:T(2,128)} %param.19), channel_id=1, source_target_pairs={{0,4},{4,0},{8,12},{12,8},{16,20},{20,16},{24,28},{28,24},{1,5},{5... | collective-permute-start | bytes 15368 | tf_op jit(solution)/shard_map/ppermute | solution.py:1406
  90.8 3.2 copy-start.14
  94.1 55.0 %copy-start.39 = (pred[640]{0:T(1024)(128)(4,1)}, pred[640]{0:T(1024)(128)(4,1)S(1)}, u32[]{:S(2)}) copy-start(pred[640]{0:T(1024)(128)(4,1)S(1)} %compare_reduce_fusion) | copy-start | bytes 1924
  159.2 14.5 %collective-permute-start.1 = (bf16[640,2048]{1,0:T(8,128)(2,1)}, bf16[640,2048]{1,0:T(8,128)(2,1)S(1)}, u32[]{:S(2)}, u32[]{:S(2)}) collective-permute-start(bf16[640,2048]{1,0:T(8,128)(2,1)} %slice.148), channel_id=1, source_target_pairs={{0,4},{4,0},{8,12},{12,8},{16,20},{20,16},{24,28},{28,24},{1,5},{5... | collective-permute-start | bytes 7864328 | tf_op jit(solution)/shard_map/ppermute | solution.py:1406
  173.7 75.2 %copy-start.3 = (f32[640,1024]{1,0:T(8,128)S(1)}, f32[640,1024]{1,0:T(8,128)}, u32[]{:S(2)}) copy-start(f32[640,1024]{1,0:T(8,128)} %get-tuple-element.77) | copy-start | bytes 7864324
  252.5 10.7 %copy-start.8 = (f32[640,1024]{1,0:T(8,128)}, f32[640,1024]{1,0:T(8,128)S(1)}, u32[]{:S(2)}) copy-start(f32[640,1024]{1,0:T(8,128)S(1)} %get-tuple-element.167) | copy-start | bytes 7864324
  264.6 3.2 collective-permute-start.2
  271.4 79.2 %copy-start.9 = (f32[640,1024]{1,0:T(8,128)S(1)}, f32[640,1024]{1,0:T(8,128)}, u32[]{:S(2)}) copy-start(f32[640,1024]{1,0:T(8,128)} %copy-done.8) | copy-start | bytes 7864324
  389.4 37.0 %copy-start.43 = (bf16[4,2,4,64,1024]{4,3,2,1,0:T(8,128)(2,1)S(1)}, bf16[4,2,4,64,1024]{4,3,2,1,0:T(8,128)(2,1)}, u32[]{:S(2)}) copy-start(bf16[4,2,4,64,1024]{4,3,2,1,0:T(8,128)(2,1)} %get-tuple-element.84) | copy-start | bytes 12582916
  426.4 9.1 %slice-start = ((s8[5242880]{0:T(1024)(128)(4,1)}), s8[4194304]{0:T(1024)(128)(4,1)S(1)}, s32[]{:S(2)}) async-start(s8[5242880]{0:T(1024)(128)(4,1)} %bitcast.107), calls=%async_computation | async-start | bytes 8388608
  426.4 9.1 %slice-start.1 = ((s8[5242880]{0:T(1024)(128)(4,1)}), s8[1048576]{0:T(1024)(128)(4,1)S(1)}, s32[]{:S(2)}) async-start(s8[5242880]{0:T(1024)(128)(4,1)} %bitcast.107), calls=%async_computation.1 | async-start | bytes 2097152
  437.4 5.7 collective-permute-start.3
  554.8 79.3 %copy-start.28 = (f32[8,1024]{1,0:T(8,128)S(1)}, f32[8,1024]{1,0:T(8,128)}, u32[]{:S(2)}) copy-start(f32[8,1024]{1,0:T(8,128)} %get-tuple-element.113) | copy-start | bytes 98308
  554.8 80.9 %copy-start.24 = (f32[31,2048]{1,0:T(8,128)S(1)}, f32[31,2048]{1,0:T(8,128)}, u32[]{:S(2)}) copy-start(f32[31,2048]{1,0:T(8,128)} %get-tuple-element.114) | copy-start | bytes 761860
  632.8 15.9 %collective-permute-start.4 = (bf16[640,1024]{1,0:T(8,128)(2,1)}, bf16[640,1024]{1,0:T(8,128)(2,1)}, u32[]{:S(2)}, u32[]{:S(2)}) collective-permute-start(bf16[640,1024]{1,0:T(8,128)(2,1)} %get-tuple-element.103), channel_id=1, source_target_pairs={{0,4},{4,0},{8,12},{12,8},{16,20},{20,16},{24,28},{28,24},{1,5},{5... | collective-permute-start | bytes 3932168 | tf_op jit(solution)/shard_map/ppermute | solution.py:1406
  636.1 14.6 %collective-permute-start.5 = (bf16[640,1024]{1,0:T(8,128)(2,1)}, bf16[640,1024]{1,0:T(8,128)(2,1)}, u32[]{:S(2)}, u32[]{:S(2)}) collective-permute-start(bf16[640,1024]{1,0:T(8,128)(2,1)} %get-tuple-element.105), channel_id=1, source_target_pairs={{0,4},{4,0},{8,12},{12,8},{16,20},{20,16},{24,28},{28,24},{1,5},{5... | collective-permute-start | bytes 3932168 | tf_op jit(solution)/shard_map/ppermute | solution.py:1406
  644.0 4.7 copy-start.17
  644.0 8.7 %copy-start.47 = (bf16[640,1024]{1,0:T(8,128)(2,1)S(1)}, bf16[640,1024]{1,0:T(8,128)(2,1)}, u32[]{:S(2)}) copy-start(bf16[640,1024]{1,0:T(8,128)(2,1)} %get-tuple-element.101) | copy-start | bytes 3932164
  648.7 11.7 %slice-start.2 = ((s8[6291456]{0:T(1024)(128)(4,1)}), s8[4194304]{0:T(1024)(128)(4,1)S(1)}, s32[]{:S(2)}) async-start(s8[6291456]{0:T(1024)(128)(4,1)} %bitcast.135), calls=%async_computation.2 | async-start | bytes 8388608
  652.7 7.7 copy-start.4
  652.7 7.7 copy-start.36
  652.7 7.7 copy-start.38
  652.7 7.7 slice-start.3
  669.4 57.4 %copy-start.40 = (pred[640]{0:T(1024)(128)(4,1)S(1)}, pred[640]{0:T(1024)(128)(4,1)}, u32[]{:S(2)}) copy-start(pred[640]{0:T(1024)(128)(4,1)} %copy-done.39) | copy-start | bytes 1924
  815.3 8.0 copy-start.15
  820.1 4.3 copy-start.22
  823.3 3.4 copy-start.26
  823.3 4.1 copy-start.20
  824.4 3.8 copy-start.25
  824.4 4.5 copy-start.19
  824.4 5.3 copy-start.18
  (26 other events, 51.5 us)

commit v5 on v4

--- a/solution.py
+++ b/solution.py
@@ -776,27 +776,48 @@
     )(hidden, norms, weight_in, weight_out, *traffic.operands())
 
 
+def norm_back_chunk(upstream, hidden, norms_ref, which, sums_ref, at):
+    scaled, rstd = norm_parts(hidden)
+    sums_ref[at : at + 1, :] += jnp.sum(upstream * scaled, axis=0, keepdims=True)
+    sums_ref[at + 1 : at + 2, :] += jnp.sum(upstream, axis=0, keepdims=True)
+    weighted = upstream * gain_row(norms_ref, which)
+    back = weighted - jnp.mean(weighted, axis=-1, keepdims=True)
+    return rstd * (back - scaled * jnp.mean(weighted * scaled, axis=-1, keepdims=True))
+
+
 def ffn_back_kernel(
-    traffic, which, hidden_ref, normed_ref, grad_ref, norms_ref, inner_ref, w_in_ref, w_out_ref, *refs
+    traffic, which, last, hidden_ref, normed_ref, grad_ref, norms_ref, inner_ref, w_in_ref, w_out_ref, *refs
 ):
+    if last:
+        after_ref, refs = refs[0], refs[1:]
     moved = len(traffic.operands())
     ins, refs = refs[:moved], refs[moved:]
     out_ref, g_in_ref, g_out_ref, sums_ref = refs[:4]
     outs, refs = refs[4 : 4 + moved], refs[4 + moved :]
     (half_grad, turned, total), refs = refs[:3], refs[3:]
+    if last:
+        arriving, refs = refs[0], refs[1:]
+    else:
+        arriving = grad_ref
     step, steps = pl.program_id(0), pl.num_programs(0)
     run_plan(traffic, ins, outs, refs, step, FFN_STEPS)
     each = chunks(hidden_ref.shape[0])
 
     @pl.when(step == 0)
     def _():
+        sums_ref[...] = jnp.zeros_like(sums_ref)
+
         def body(here):
-            half_grad[here, :] = (0.5 * grad_ref[here, :]).astype(jnp.bfloat16)
+            if last:
+                upstream = grad_ref[here, :].astype(jnp.float32)
+                arriving[here, :] = norm_back_chunk(
+                    upstream, after_ref[here, :], norms_ref, which + 1, sums_ref, 2
+                )
+            half_grad[here, :] = (0.5 * arriving[here, :]).astype(jnp.bfloat16)
             total[here, :] = jnp.zeros((CHUNK, total.shape[1]), jnp.float32)
 
         each(body)
         turned[...] = normed_ref[...].T
-        sums_ref[...] = jnp.zeros_like(sums_ref)
 
     inner = inner_ref[...].astype(jnp.float32)
     gate = sigmoid(inner)
@@ -810,25 +831,21 @@
     @pl.when(step == steps - 1)
     def _():
         def body(here):
-            scaled, rstd = norm_parts(hidden_ref[here, :])
-            upstream = total[here, :]
-            sums_ref[0:1, :] += jnp.sum(upstream * scaled, axis=0, keepdims=True)
-            sums_ref[1:2, :] += jnp.sum(upstream, axis=0, keepdims=True)
-            weighted = upstream * gain_row(norms_ref, which)
-            back = weighted - jnp.mean(weighted, axis=-1, keepdims=True)
-            back = back - scaled * jnp.mean(weighted * scaled, axis=-1, keepdims=True)
-            out_ref[here, :] = grad_ref[here, :] + rstd * back
+            out_ref[here, :] = arriving[here, :] + norm_back_chunk(
+                total[here, :], hidden_ref[here, :], norms_ref, which, sums_ref, 0
+            )
 
         each(body)
 
     run_plan(traffic, ins, outs, refs, step, FFN_STEPS, late=True)
 
 
-def ffn_back(hidden, normed, grad, norms, which, inner, weight_in, weight_out, traffic):
+def ffn_back(hidden, normed, grad, norms, which, inner, weight_in, weight_out, traffic, after=None):
     rows, width = hidden.shape
+    last = after is not None
     tile = weight_in.shape[1] // FFN_STEPS
     return pl.pallas_call(
-        functools.partial(ffn_back_kernel, traffic, which),
+        functools.partial(ffn_back_kernel, traffic, which, last),
         grid=(FFN_STEPS,),
         out_shape=[
             jax.ShapeDtypeStruct((rows, width), jnp.float32),
@@ -846,6 +863,7 @@
             pl.BlockSpec((width, tile), lambda step: (0, step)),
             pl.BlockSpec((tile, width), lambda step: (step, 0)),
         ]
+        + [resident((rows, width))] * last
         + traffic.in_specs(),
         out_specs=[
             resident((rows, width)),
@@ -859,9 +877,20 @@
             pltpu.VMEM((width, rows), jnp.bfloat16),
             pltpu.VMEM((rows, width), jnp.float32),
         ]
+        + [pltpu.VMEM((rows, width), jnp.float32)] * last
         + traffic.scratch(),
         compiler_params=traffic_params(traffic),
-    )(hidden, normed, grad, norms, inner, weight_in, weight_out, *traffic.operands())
+    )(
+        hidden,
+        normed,
+        grad,
+        norms,
+        inner,
+        weight_in,
+        weight_out,
+        *([after] if last else []),
+        *traffic.operands(),
+    )
 
 
 QB = 128
@@ -1455,7 +1484,7 @@
         Traffic(sizes, 1, shards=shard_of[2:4], swapped=[cotangent], swap_at=3.0, pace=2.0),
     )
     w_qkv, w_mixer = as_weight(gathered[0], qkv_weight), as_weight(gathered[1], mixer_out)
-    upstream = gathered[2].reshape(rows, D).astype(jnp.float32)
+    upstream = gathered[2].reshape(rows, D)
     packed = product(normed2, w_qkv).astype(jnp.bfloat16)
     far = from_other(packed[:, D:])
     mixed_rows, mixed_exact, log_total, *gathered = attend(
@@ -1487,9 +1516,17 @@
         hidden3, vectors, 3, w_late_in, w_late_out, Traffic(sizes, None)
     )
 
-    grad4, gain_grad4, bias_grad4 = norm_back(hidden4, gains[4], biases[4], upstream)
     grad3, late_in_grad, late_out_grad, norm_sums3 = ffn_back(
-        hidden3, normed5, grad4, vectors, 3, inner5, w_late_in, w_late_out, Traffic(sizes, None)
+        hidden3,
+        normed5,
+        upstream,
+        vectors,
+        3,
+        inner5,
+        w_late_in,
+        w_late_out,
+        Traffic(sizes, None),
+        after=hidden4,
     )
     grad_out3 = grad3.astype(jnp.bfloat16)
     pointwise_out_grad = weight_grad(post, grad_out3)
@@ -1539,6 +1576,7 @@
             sizes,
             5,
             grads=[parts(pointwise_out_grad, pointwise_out), parts(pointwise_in_grad, pointwise_in)],
+            swapped=[activations.reshape(groups, run, D)],
         ),
     )
     table_grad = table_back(near, far_sums, core * (rows // QB)).reshape(H * NB)
@@ -1568,8 +1606,8 @@
             sizes,
             6,
             grads=[parts(mixer_out_grad, mixer_out), parts(qkv_grad, qkv_weight)],
-            swapped=[activations.reshape(groups, run, D)],
-            pace=1.3,
+            split=6,
+            pace=1.2,
         ),
     )
     grad_frames = jnp.where(masked, 0.0, grad0).astype(jnp.bfloat16)
@@ -1583,12 +1621,12 @@
                 gain_grad1,
                 gain_grad2,
                 norm_sums3[0],
-                gain_grad4,
+                norm_sums3[2],
                 norm_sums0[1],
                 bias_grad1,
                 bias_grad2,
                 norm_sums3[1],
-                bias_grad4,
+                norm_sums3[3],
             )
         ]
     )
@@ -1625,7 +1663,7 @@
         small_out.append(small_sums[at : at + size].reshape(shape))
         at += size
     return (
-        sums_mixer[2],
+        sums_depth[2],
         sums_early[3].astype(jnp.float32),
         small_out[0],
         small_out[1],

time: 836 us -> 821 us (0.982)
  other arithmetic: 42.5 us -> 32.7 us
    unnamed x127 -> x111, local copies, waits for them, and re-layouts: 20.9 us -> 17.7 us
  transfers between devices with their start and end apart: 6 -> 6, of which waited for: 0 -> 1; matrix products, arithmetic and copies ran while one was open for 5% -> 5% of each run, Pallas kernels for 10% -> 10%
where the time goes in v5:
time: 821 us; the launch traced here: 816 us
  Pallas kernels  649 us (79%)
  matrix products  82.3 us (10%)
  local copies, waits for them, and re-layouts  44.9 us (5%)
  other arithmetic  32.7 us (4%)
    pallas_call x2, Pallas kernels, move(): pl.pallas_call(functools.partial(traffic_kernel, traffic), out_shape=traf...  165 us
    pallas_call x2, Pallas kernels, ffn_back(): pl.pallas_call(functools.partial(ffn_back_kernel, traffic, which, last),...  95.6 us
    pallas_call x1, Pallas kernels, convolve_back(): pl.pallas_call(functools.partial(conv_back_kernel, traffic), grid=(half,)...  82.2 us
    pallas_call x1, Pallas kernels, attend_back(): pl.pallas_call(functools.partial(attend_back_kernel, rows, length, traffi...  78.5 us
    pallas_call x1, Pallas kernels, convolve(): pl.pallas_call(functools.partial(conv_kernel, traffic), grid=(CONV_BLOCKS...  76.7 us
    pallas_call x2, Pallas kernels, ffn(): pl.pallas_call(functools.partial(ffn_kernel, traffic, which), grid=(FFN_S...  76.5 us
    pallas_call x1, Pallas kernels, attend(): pl.pallas_call(functools.partial(attend_kernel, rows, length, traffic), g...  73.6 us
    dot_general x4, matrix products, weight_grad(): lax.dot_general(operand_a, operand_b, (((0,), (0,)), ((), ())), preferred...  27.2 us
  transfers between devices with their start and end apart: 6, of which 1 were waited for; matrix products, arithmetic and copies ran while one was open for 5% of the time, Pallas kernels for 10%

profile of v5, /device:TPU:0, one launch (start us, length us, event | category | flops | bytes accessed | tf_op | source)
XLA Modules:
  0.0 816.1 jit_solution(5785123432143466781)
XLA Ops:
  3.6 2.8 concatenate.57
  7.0 83.8 %shard_map.305 = (bf16[4,2,4,32,4096]{4,3,2,1,0:T(8,128)(2,1)}, bf16[4,2,4,128,1024]{4,3,2,1,0:T(8,128)(2,1)}, bf16[4,2,4,16,512]{4,3,2,1,0:T(8,128)(2,1)}, bf16[2,320,1024]{2,1,0:T(8,128)(2,1)}) custom-call(bf16[32,4096]{1,0:T(8,128)(2,1)} %refs_0_.4, bf16[128,1024]{1,0:T(8,128)(2,1)} %refs_1_.4, bf16[16,512]{1,0:T(8,128)(2,1)} %reshape.581.refs_2_, ...), custom_call_target="tpu_custom_call" | custom-call | tf_op jit(solution)/shard_map/pallas_call | solution.py:604
  95.8 53.6 %shard_map.306 = (f32[640,1024]{1,0:T(8,128)}, bf16[640,4096]{1,0:T(8,128)(2,1)}, bf16[640,1024]{1,0:T(8,128)(2,1)}, bf16[640,1024]{1,0:T(8,128)(2,1)}, bf16[4,2...) custom-call(f32[640,1024]{1,0:T(8,128)} %convert_select_fusion.hidden_ref, ...), custom_call_target="tpu_custom_call" | custom-call | tf_op jit(solution)/shard_map/pallas_call | solution.py:750
  149.4 7.4 convolution_convert_fusion.3.q_ref.k_own_ref.v_own_ref
  159.6 3.2 collective-permute-start.1
  166.7 2.0 reshape.590.channels_ref
  171.4 1.9 reduce_sum.168
  174.9 73.6 %shard_map.307 = (bf16[640,1024]{1,0:T(8,128)(2,1)}, f32[640,1024]{1,0:T(8,128)}, f32[40,1,256]{2,1,0:T(1,128)}, bf16[4,2,4,32,4096]{4,3,2,1,0:T(8,128)(2,1)}, bf16[4,2,4,64,1024]{4,3,2,1,0:T(8,128)(2,1)}) custom-call(f32[8,8,128]{2,1,0:T(8,128)} %reshape.583.rows_ref, bf16[640,3072]{1,0:T(8,128)(2,1)} %copy-done, bf16[640,3072]{1,0:T(8,128)(2,1)} %copy-done, ...), custom_call_target="tpu_custom_call" | custom-call | tf_op jit(solution)/shard_map/pallas_call | solution.py:1009
  248.5 3.7 fusion.42
  253.1 7.6 fusion.43
  265.4 76.7 %shard_map.308 = (f32[640,2048]{1,0:T(8,128)}, bf16[640,2048]{1,0:T(8,128)(2,1)}, f32[640,1]{1,0:T(8,128)}, f32[640,1]{1,0:T(8,128)}, bf16[4,2,4,32,4096]{4,3,2,...) custom-call(bf16[672,2048]{1,0:T(8,128)(2,1)} %pad_maximum_fusion.1.padded_ref.gated_ref, ...), custom_call_target="tpu_custom_call" | custom-call | tf_op jit(solution)/shard_map/pallas_call | solution.py:1278
  344.4 7.3 convolution_add_fusion.hidden_ref
  351.7 22.9 %shard_map.309 = (f32[640,1024]{1,0:T(8,128)}, bf16[640,4096]{1,0:T(8,128)(2,1)}, bf16[640,1024]{1,0:T(8,128)(2,1)}, bf16[640,1024]{1,0:T(8,128)(2,1)}) custom-call(f32[640,1024]{1,0:T(8,128)} %convolution_add_fusion.hidden_ref, f32[11,1024]{1,0:T(8,128)} %reshape.584.norms_ref, bf16[1024,4096]{1,0:T(8,128)(2,1)} %bitcast.84, bf16[4096,1024]{1,0:T(8,128)(2,1)} %bitcast.86), custom_call_target="tpu_custom_call" | custom-call | tf_op jit(solution)/shard_map/pallas_call | solution.py:750
  374.6 39.9 %shard_map.310 = (f32[640,1024]{1,0:T(8,128)}, bf16[1024,4096]{1,0:T(8,128)(2,1)}, bf16[4096,1024]{1,0:T(8,128)(2,1)}, f32[8,1024]{1,0:T(8,128)}) custom-call(f32[640,1024]{1,0:T(8,128)} %convolution_add_fusion.hidden_ref, bf16[640,1024]{1,0:T(8,128)(2,1)} %get-tuple-element.86.normed_ref, bf16[640,1024]{1,0:T(8,128)(2,1)} %bitcast.109, ...), custom_call_target="tpu_custom_call" | custom-call | tf_op jit(solution)/shard_map/pallas_call | solution.py:847
  414.6 9.1 %multiply_reduce_fusion = (bf16[2048]{0:T(1024)(128)(2,1)S(1)}, f32[640]{0:T(1024)S(1)}, f32[640]{0:T(1024)S(1)}, bf16[2048]{0:T(1024)(128)(2,1)S(1)}, f32[640,2048]{1,0:T(8,128)S(1)}) fusion(f32[640,2048]{1,0:T(8,128)} %get-tuple-element.92, f32[640]{0:T(1024)S(1)} %reduce.5, f32[640]{0:T(1024)S(1)} %reduce.4, f32[2048]{0:T(1024)S(1)} %mul.208, ...), kind=kOutput, calls=%fused_computation.8 | convolution fusion | flops 2709908480 | bytes 17336320 | tf_op jit(solution)/shard_map/dot_general | solution.py:648
  426.2 5.2 convolution_convert_fusion.4
  433.3 82.2 %shard_map.311 = (bf16[640,2048]{1,0:T(8,128)(2,1)}, bf16[640,2048]{1,0:T(8,128)(2,1)}, f32[31,2048]{1,0:T(8,128)}, f32[128,1024]{1,0:T(8,128)}, f32[32,4096]{1,0:T(8,128)}) custom-call(bf16[672,2048]{1,0:T(8,128)(2,1)} %pad_maximum_fusion.2.change_ref, bf16[672,2048]{1,0:T(8,128)(2,1)} %pad_maximum_fusion.1.padded_ref.gated_ref, ...), custom_call_target="tpu_custom_call" | custom-call | tf_op jit(solution)/shard_map/pallas_call | solution.py:1345
  515.6 2.2 constant_dynamic-update-slice_fusion.1
  518.4 8.7 %multiply_reduce_fusion.3 = (bf16[1024]{0:T(1024)(128)(2,1)S(1)}, f32[640]{0:T(1024)S(1)}, bf16[1024]{0:T(1024)(128)(2,1)S(1)}, f32[640,1024]{1,0:T(8,128)S(1)}) fusion(f32[640,1024]{1,0:T(8,128)S(1)} %get-tuple-element.162, f32[640]{0:T(1024)S(1)} %fusion.30, f32[640]{0:T(1024)S(1)} %broadcast_multiply_fusion.3, f32[1024]{0:T(1024)S(1)} %copy-done.29, ...), kind=kOutput, calls=%fused_computation.24 | convolution fusion | flops 5373949440 | bytes 18890240 | tf_op jit(solution)/shard_map/dot_general | solution.py:648
  527.1 9.5 %convolution_convert_fusion = bf16[1024,4096]{1,0:T(8,128)(2,1)} fusion(bf16[640,4096]{1,0:T(8,128)(2,1)S(1)} %constant_dynamic-update-slice_fusion, f32[640,1024]{1,0:T(8,128)S(1)} %get-tuple-element.162, f32[1024]{0:T(1024)S(1)} %copy-done.33, f32[1024]{0:T(1024)S(1)} %copy-done.29, f32[640]{0:T(1024)S(1)} %fusion.30, f32[640]{0:T(1024)S(1)} %broadcast_multiply_fusion.3), kind=kOutput, calls=%fused_computation | convolution fusion | flops 5376180224 | bytes 16266240 | tf_op jit(solution)/shard_map/dot_general | solution.py:642
  539.0 2.6 convolution_convert_fusion.6.g_ref
  541.6 78.5 %shard_map.312 = (bf16[640,1024]{1,0:T(8,128)(2,1)}, bf16[640,1024]{1,0:T(8,128)(2,1)}, bf16[640,1024]{1,0:T(8,128)(2,1)}, bf16[640,1024]{1,0:T(8,128)(2,1)}, bf...) custom-call(f32[8,8,128]{2,1,0:T(8,128)} %reshape.583.rows_ref, ...), custom_call_target="tpu_custom_call" | custom-call | tf_op jit(solution)/shard_map/pallas_call | solution.py:1147
  632.0 4.7 convolution_convert_fusion.5
  636.7 2.0 add_convert_fusion.1
  638.7 2.0 add_convert_fusion
  640.8 7.9 convolution_convert_fusion.2
  648.7 6.1 multiply_reduce_fusion.4
  655.7 1.9 add_add_fusion.2.grad_ref
  657.6 55.7 %shard_map.313 = (f32[640,1024]{1,0:T(8,128)}, bf16[1024,4096]{1,0:T(8,128)(2,1)}, bf16[4096,1024]{1,0:T(8,128)(2,1)}, f32[8,1024]{1,0:T(8,128)}, f32[32,1024]{1,0:T(8,128)}, /*index=5*/f32[32,3072]{1,0:T(8,128)}) custom-call(f32[640,1024]{1,0:T(8,128)} %convert_select_fusion.hidden_ref, bf16[640,1024]{1,0:T(8,128)(2,1)} %get-tuple-element.102.normed_ref, ...), custom_call_target="tpu_custom_call" | custom-call | tf_op jit(solution)/shard_map/pallas_call | solution.py:847
  713.3 2.2 select_reduce_fusion
  719.1 81.6 %shard_map.314 = (f32[128,1024]{1,0:T(8,128)}, f32[32,4096]{1,0:T(8,128)}, f32[16,512]{1,0:T(8,128)}, bf16[2,320,1024]{2,1,0:T(8,128)(2,1)}) custom-call(bf16[4,2,4,128,1024]{4,3,2,1,0:T(8,128)(2,1)} %bitcast.94, bf16[4,2,4,32,4096]{4,3,2,1,0:T(8,128)(2,1)} %bitcast.93, bf16[4,2,4,16,512]{4,3,2,1,0:T(8,128)(2,1)} %bitcast.105, bf16[2,320,1024]{2,1,0:T(8,128)(2,1)} %bitcast.98), custom_call_target="tpu_custom_call" | custom-call | tf_op jit(solution)/shard_map/pallas_call | solution.py:604
  805.5 3.2 convert_element_type.241
  (232 shorter events, 62.6 us)
Async XLA Ops:
  0.7 93.0 %copy-start.34 = (s32[2,640]{1,0:T(2,128)S(1)}, s32[2,640]{1,0:T(2,128)}, u32[]{:S(2)}) copy-start(s32[2,640]{1,0:T(2,128)} %param.19) | copy-start | bytes 15364
  0.7 93.0 %collective-permute-start = (s32[2,640]{1,0:T(2,128)}, s32[2,640]{1,0:T(2,128)S(1)}, u32[]{:S(2)}, u32[]{:S(2)}) collective-permute-start(s32[2,640]{1,0:T(2,128)} %param.19), channel_id=1, source_target_pairs={{0,4},{4,0},{8,12},{12,8},{16,20},{20,16},{24,28},{28,24},{1,5},{5... | collective-permute-start | bytes 15368 | tf_op jit(solution)/shard_map/ppermute | solution.py:1435
  90.8 3.2 copy-start.7
  94.0 55.4 %copy-start.31 = (pred[640]{0:T(1024)(128)(4,1)}, pred[640]{0:T(1024)(128)(4,1)S(1)}, u32[]{:S(2)}) copy-start(pred[640]{0:T(1024)(128)(4,1)S(1)} %compare_reduce_fusion) | copy-start | bytes 1924
  156.9 2.7 copy-start
  159.6 13.8 %collective-permute-start.1 = (bf16[640,2048]{1,0:T(8,128)(2,1)}, bf16[640,2048]{1,0:T(8,128)(2,1)S(1)}, u32[]{:S(2)}, u32[]{:S(2)}) collective-permute-start(bf16[640,2048]{1,0:T(8,128)(2,1)} %slice.152), channel_id=1, source_target_pairs={{0,4},{4,0},{8,12},{12,8},{16,20},{20,16},{24,28},{28,24},{1,5},{5... | collective-permute-start | bytes 7864328 | tf_op jit(solution)/shard_map/ppermute | solution.py:1435
  173.4 75.1 %copy-start.2 = (f32[640,1024]{1,0:T(8,128)S(1)}, f32[640,1024]{1,0:T(8,128)}, u32[]{:S(2)}) copy-start(f32[640,1024]{1,0:T(8,128)} %get-tuple-element.78) | copy-start | bytes 7864324
  248.5 4.4 copy-start.35
  262.1 1.3 collective-permute-start.2
  414.5 9.1 %slice-start = ((s8[5242880]{0:T(1024)(128)(4,1)}), s8[4194304]{0:T(1024)(128)(4,1)S(1)}, s32[]{:S(2)}) async-start(s8[5242880]{0:T(1024)(128)(4,1)} %bitcast.99), calls=%async_computation | async-start | bytes 8388608
  414.6 9.1 %slice-start.1 = ((s8[5242880]{0:T(1024)(128)(4,1)}), s8[1048576]{0:T(1024)(128)(4,1)S(1)}, s32[]{:S(2)}) async-start(s8[5242880]{0:T(1024)(128)(4,1)} %bitcast.99), calls=%async_computation.1 | async-start | bytes 2097152
  425.6 5.8 collective-permute-start.3
  541.6 79.2 %copy-start.20 = (f32[8,1024]{1,0:T(8,128)S(1)}, f32[8,1024]{1,0:T(8,128)}, u32[]{:S(2)}) copy-start(f32[8,1024]{1,0:T(8,128)} %get-tuple-element.113) | copy-start | bytes 98308
  541.6 82.1 %copy-start.17 = (f32[31,2048]{1,0:T(8,128)S(1)}, f32[31,2048]{1,0:T(8,128)}, u32[]{:S(2)}) copy-start(f32[31,2048]{1,0:T(8,128)} %get-tuple-element.114) | copy-start | bytes 761860
  620.1 16.6 %collective-permute-start.4 = (bf16[640,1024]{1,0:T(8,128)(2,1)}, bf16[640,1024]{1,0:T(8,128)(2,1)}, u32[]{:S(2)}, u32[]{:S(2)}) collective-permute-start(bf16[640,1024]{1,0:T(8,128)(2,1)} %get-tuple-element.105), channel_id=1, source_target_pairs={{0,4},{4,0},{8,12},{12,8},{16,20},{20,16},{24,28},{28,24},{1,5},{5... | collective-permute-start | bytes 3932168 | tf_op jit(solution)/shard_map/ppermute | solution.py:1435
  624.1 14.6 %collective-permute-start.5 = (bf16[640,1024]{1,0:T(8,128)(2,1)}, bf16[640,1024]{1,0:T(8,128)(2,1)}, u32[]{:S(2)}, u32[]{:S(2)}) collective-permute-start(bf16[640,1024]{1,0:T(8,128)(2,1)} %get-tuple-element.107), channel_id=1, source_target_pairs={{0,4},{4,0},{8,12},{12,8},{16,20},{20,16},{24,28},{28,24},{1,5},{5... | collective-permute-start | bytes 3932168 | tf_op jit(solution)/shard_map/ppermute | solution.py:1435
  632.0 4.7 copy-start.10
  632.0 8.7 %copy-start.39 = (bf16[640,1024]{1,0:T(8,128)(2,1)S(1)}, bf16[640,1024]{1,0:T(8,128)(2,1)}, u32[]{:S(2)}) copy-start(bf16[640,1024]{1,0:T(8,128)(2,1)} %get-tuple-element.103) | copy-start | bytes 3932164
  636.7 11.9 %slice-start.2 = ((s8[6291456]{0:T(1024)(128)(4,1)}), s8[4194304]{0:T(1024)(128)(4,1)S(1)}, s32[]{:S(2)}) async-start(s8[6291456]{0:T(1024)(128)(4,1)} %bitcast.128), calls=%async_computation.2 | async-start | bytes 8388608
  640.7 7.9 copy-start.3
  640.7 7.9 copy-start.28
  640.7 7.9 copy-start.30
  640.8 7.9 slice-start.3
  657.6 55.7 %copy-start.32 = (pred[640]{0:T(1024)(128)(4,1)S(1)}, pred[640]{0:T(1024)(128)(4,1)}, u32[]{:S(2)}) copy-start(pred[640]{0:T(1024)(128)(4,1)} %copy-done.31) | copy-start | bytes 1924
  800.7 8.0 copy-start.8
  805.5 4.3 copy-start.15
  808.7 2.7 copy-start.16
  808.7 3.4 copy-start.19
  808.7 4.1 copy-start.13
  809.8 3.8 copy-start.18
  809.8 4.5 copy-start.12
  809.8 5.3 copy-start.11
  (18 other events, 33.3 us)
